TPU v7x, 32 devices: a whole 2x2x4 slice. The times are simulated.
32 devices in a mesh: groups: 2 (over x), seq: 16 (over z, y, core).
Axes of the slice: x: 2, y: 2, z: 4, core: 2. Of those that a mesh axis runs over, the one named last changes fastest.
Arguments:
- prefill_kv: bfloat16 [4096, 576], P(('groups', 'seq')), parts along dimension 0, may hold values from -6 to 6
- lengths: int32 [128], P('groups'), parts along dimension 0, may hold values from 1 to 63, as said below
- assignment: int32 [128], P('groups'), parts along dimension 0, may hold values from 0 to 63, as said below
- queries: bfloat16 [4, 128, 64, 576], P(None, ('groups', 'seq')), parts along dimension 1, may hold values from -60 to 60
- new_kv: bfloat16 [4, 128, 576], P(None, ('groups', 'seq')), parts along dimension 1, may hold values from -6 to 6
- expert_hidden: bfloat16 [128, 4, 8, 1024], P(('groups', 'seq')), parts along dimension 0, may hold values from -6 to 6
- routes: int32 [128, 4, 8], P(('groups', 'seq')), parts along dimension 0, may hold values from 0 to 15, all different within a row; in each aligned block of 16 rows (0 to 15, 16 to 31, ..., all dimensions but the last counted through in order) at most 16 rows name the same one
- route_weights: float32 [128, 4, 8], P(('groups', 'seq')), parts along dimension 0, may hold values from 0.05 to 0.5
- expert_down: bfloat16 [16, 1024, 3584], P('seq'), may hold values from -0.1875 to 0.1875
Outputs:
- context: bfloat16 [4, 128, 64, 512], P(None, ('groups', 'seq')), parts along dimension 1
- moe_out: bfloat16 [128, 4, 3584], P(('groups', 'seq')), parts along dimension 0
There are 2 independent parts, one for each index of `groups`. A program takes and returns all parts, laid end to end along the dimension named above; an argument that names none is the same for every part. Nothing has to cross between parts.
Inputs may be any that keep to these rules, and one draw needn't show every extreme that they name: `lengths`: each length is 1 to 63; they sum to 2048; 63 is reached. `assignment`: A permutation of the requests. The rows that one device holds of prefill_kv include at most 16 rows of the requests of any one decoding device, and some device reaches 16. Within the routes of one device's rows no expert is named more than 16 times, and some expert reaches it.
All inputs are finite; a program needn't handle non-finite values.
Results may differ from a plain program's by a relative error of at most 0.0051.
Values may be sent and summed in bfloat16 or wider, within the bound.
No kernel may reach another device: no remote copies, remote signals or barrier semaphores. Data moves between devices by JAX's collectives and lax.ppermute only.
A program may use at most 64 MiB of HBM per device.

v0:
```python
import jax
import jax.numpy as jnp
from jax import lax
from jax.sharding import PartitionSpec as P

ROPE = 64
HALF = 2


score_scale = 192.0 ** (-0.5)
masked_score = -1e30


def slot_sources(slot_ids, slot_total):
    source_rows = jnp.arange(slot_ids.shape[0], dtype=jnp.int32)
    matched = slot_ids[None, :] == jnp.arange(slot_total, dtype=jnp.int32)[:, None]
    return jnp.max(jnp.where(matched, source_rows[None, :], -1), axis=1)


def fill_slots(values, sources, filler):
    taken = jnp.take(values, jnp.maximum(sources, 0), axis=0)
    valid = (sources >= 0).reshape((-1,) + (1,) * (values.ndim - 1))
    return jnp.where(valid, taken, jnp.asarray(filler, values.dtype))


def hand_over(prefill_kv, lengths, assignment, per_owner):
    device_count = lax.axis_size("seq")
    own_index = lax.axis_index("seq")
    ctx_here, kv_width = prefill_kv.shape
    position = jnp.arange(ctx_here, dtype=jnp.int32) * device_count + own_index
    request_ends = jnp.cumsum(lengths)
    request = jnp.sum((position[:, None] >= request_ends[None, :]).astype(jnp.int32), axis=1)
    total_rows = assignment.shape[0]
    row_numbers = jnp.arange(total_rows, dtype=jnp.int32)
    serving = jnp.sum(
        jnp.where(assignment[None, :] == row_numbers[:, None], row_numbers[None, :], 0), axis=1
    )
    decode_row = jnp.sum(
        jnp.where(request[:, None] == row_numbers[None, :], serving[None, :], 0), axis=1
    )
    owner_index = decode_row // per_owner
    local_request = decode_row % per_owner
    onehot = (owner_index[:, None] == jnp.arange(device_count, dtype=jnp.int32)[None, :]).astype(
        jnp.int32
    )
    slot_rank = jnp.sum((jnp.cumsum(onehot, axis=0) - onehot) * onehot, axis=1)
    slot_count = 2 * HALF * per_owner
    sources = slot_sources(owner_index * slot_count + slot_rank, device_count * slot_count)
    outbox = fill_slots(prefill_kv, sources, 0).reshape(device_count, slot_count, kv_width)
    labels = fill_slots(local_request, sources, -1).reshape(device_count, slot_count)
    kv_cache, cache_tags = (
        lax.all_to_all(outbox, "seq", split_axis=0, concat_axis=0, tiled=True),
        lax.all_to_all(labels, "seq", split_axis=0, concat_axis=0, tiled=True),
    )
    return (kv_cache.reshape(device_count * slot_count, kv_width), cache_tags.reshape(-1))


def fresh_part(queries, new_kv):
    step_count = queries.shape[0]
    fresh_scores = (
        jnp.einsum("sqhk,uqk->sqhu", queries, new_kv, preferred_element_type=jnp.float32)
        * score_scale
    )
    causal = jnp.arange(step_count)[:, None] >= jnp.arange(step_count)[None, :]
    return jnp.where(causal[:, None, None, :], fresh_scores, masked_score)


def attend_dense(queries, new_kv, kv_cache, cache_tags):
    step_count, per_owner, head_count, kv_width = queries.shape
    latent = kv_width - ROPE
    query_rows = queries.reshape(step_count * per_owner * head_count, kv_width)
    scores = (
        jnp.einsum("rk,ck->rc", query_rows, kv_cache, preferred_element_type=jnp.float32)
        * score_scale
    )
    row_request = jnp.broadcast_to(
        jnp.arange(per_owner, dtype=jnp.int32)[None, :, None], (step_count, per_owner, head_count)
    ).reshape(-1)
    allowed = cache_tags[None, :] == row_request[:, None]
    scores = jnp.where(allowed, scores, masked_score).reshape(step_count, per_owner, head_count, -1)
    fresh_scores = fresh_part(queries, new_kv)
    top_score = jnp.maximum(jnp.max(scores, axis=-1), jnp.max(fresh_scores, axis=-1))
    weights = jnp.exp(scores - top_score[..., None])
    fresh_weights = jnp.exp(fresh_scores - top_score[..., None])
    denominator = jnp.sum(weights, axis=-1) + jnp.sum(fresh_weights, axis=-1)
    summed = jnp.einsum(
        "sqhc,cl->sqhl",
        weights.astype(jnp.bfloat16),
        kv_cache[:, :latent],
        preferred_element_type=jnp.float32,
    )
    summed = summed + jnp.einsum(
        "sqhu,uql->sqhl",
        fresh_weights.astype(jnp.bfloat16),
        new_kv[..., :latent],
        preferred_element_type=jnp.float32,
    )
    return (summed / denominator[..., None]).astype(jnp.bfloat16)


def expert_layer(expert_hidden, routes, route_weights, expert_down):
    device_count = lax.axis_size("seq")
    rows_here, step_count, top_count, hidden_width = expert_hidden.shape
    per_dev = expert_down.shape[0]
    experts = per_dev * device_count
    capacity = max(2, 2 * step_count * rows_here * top_count // experts)
    flat_routes = routes.reshape(-1)
    route_count = flat_routes.shape[0]
    onehot = (flat_routes[:, None] == jnp.arange(experts, dtype=jnp.int32)[None, :]).astype(
        jnp.int32
    )
    slot_index = jnp.sum((jnp.cumsum(onehot, axis=0) - onehot) * onehot, axis=1)
    flat_hidden = expert_hidden.reshape(route_count, hidden_width)
    slot_ids = flat_routes * capacity + slot_index
    sources = slot_sources(slot_ids, experts * capacity)
    outbox = fill_slots(flat_hidden, sources, 0).reshape(
        device_count, per_dev, capacity, hidden_width
    )
    expert_out = jnp.einsum(
        "dekh,ehm->dekm",
        lax.all_to_all(outbox, "seq", split_axis=0, concat_axis=0, tiled=True),
        expert_down,
        preferred_element_type=jnp.float32,
    ).astype(jnp.bfloat16)
    returned = lax.all_to_all(expert_out, "seq", split_axis=0, concat_axis=0, tiled=True)
    returned = returned.reshape(experts * capacity, returned.shape[-1])
    picked = jnp.take(returned, slot_ids, axis=0).astype(jnp.float32)
    weighted = picked * route_weights.reshape(route_count, 1)
    moe_out = jnp.sum(weighted.reshape(rows_here, step_count, top_count, -1), axis=2)
    return moe_out.astype(jnp.bfloat16)


def per_device(
    prefill_kv,
    lengths,
    assignment,
    queries,
    new_kv,
    expert_hidden,
    routes,
    route_weights,
    expert_down,
):
    kv_cache, cache_tags = hand_over(prefill_kv, lengths, assignment, queries.shape[1])
    context = attend_dense(queries, new_kv, kv_cache, cache_tags)
    moe_out = expert_layer(expert_hidden, routes, route_weights, expert_down)
    return (context, moe_out)


def solution(mesh):
    placed = (
        P(("groups", "seq"), None),
        P("groups"),
        P("groups"),
        P(None, ("groups", "seq"), None, None),
        P(None, ("groups", "seq"), None),
        P(("groups", "seq"), None, None, None),
        P(("groups", "seq"), None, None),
        P(("groups", "seq"), None, None),
        P("seq", None, None),
    )
    return jax.shard_map(
        per_device,
        mesh=mesh,
        in_specs=placed,
        out_specs=(P(None, ("groups", "seq"), None, None), P(("groups", "seq"), None, None)),
        check_vma=False,
    )
```

profile of v0, /device:TPU:15, one launch (start us, length us, event | category | flops | bytes accessed | tf_op | source)
XLA Modules:
  0.0 102.3 jit_solution(16971301888945883725)
XLA Ops:
  0.6 0.0 copy-start
  0.6 0.0 copy-start.1
  0.7 0.9 copy.54
  1.5 0.1 reduce-window.8
  1.6 0.1 reduce.2
  1.7 0.8 select_reduce_fusion.5
  2.5 0.1 convert_reduce_fusion
  2.6 0.1 select_reduce_fusion.4
  2.7 0.1 fusion.27
  2.8 0.2 reduce_window_sum.24
  3.0 0.2 select_reduce_fusion.3
  3.2 0.1 select_reduce_fusion.1
  3.3 1.9 %gather_fusion = s32[256]{0:T(256)S(1)} fusion(s32[128]{0:T(128)S(1)} %get-tuple-element.9, s32[1024]{0:T(1024)S(1)} %pad_clamp_fusion.2), kind=kCustom, calls=%fused_computation | custom fusion | bytes 3072 | tf_op jit(solution)/shard_map/jit(_take)/gather | solution.py:21
  5.2 0.7 select_n.138
  5.9 6.6 %all-to-all-start = ((s32[16,1,16]{2,1,0:T(1,128)}), s32[16,1,16]{2,1,0:T(1,128)S(1)}, u32[]{:S(2)}, u32[]{:S(2)}) async-start(s32[16,1,16]{2,1,0:T(1,128)} %select_n.138), calls=%async_computation | async-start | bytes 16384 | tf_op jit(solution)/shard_map/all_to_all | solution.py:53
  12.5 0.8 reshape.338
  13.2 0.1 fusion.26
  13.3 0.2 reduce_window_sum.25
  13.5 0.2 select_reduce_fusion.2
  13.7 0.1 select_reduce_fusion
  13.9 0.1 ge.100
  13.9 0.1 le.59
  14.0 0.0 copy-done.1
  14.0 1.2 %gather_fusion.2 = bf16[256,1024]{1,0:T(8,128)(2,1)S(1)} fusion(bf16[128,1024]{1,0:T(8,128)(2,1)S(1)} %bitcast.63, s32[1024]{0:T(1024)S(1)} %pad_clamp_fusion.1), kind=kCustom, calls=%fused_computation.2 | custom fusion | bytes 1049600 | tf_op jit(solution)/shard_map/jit(_take)/gather | solution.py:21
  15.2 0.0 copy-start.2
  15.2 0.9 select_select_fusion
  16.2 0.0 all-to-all-done
  16.2 6.1 %all-to-all-start.2 = ((bf16[16,1,16,1024]{3,2,1,0:T(8,128)(2,1)}), bf16[16,1,16,1024]{3,2,1,0:T(8,128)(2,1)S(1)}, u32[]{:S(2)}, u32[]{:S(2)}) async-start(bf16[16,1,16,1024]{3,2,1,0:T(8,128)(2,1)} %select_select_fusion), calls=%async_computation.2 | async-start | bytes 1048576 | tf_op jit(solution)/shard_map/all_to_all | solution.py:121
  22.3 0.1 ge.94
  22.4 0.1 le.55
  22.5 0.0 copy-done.2
  22.5 0.2 copy.55
  22.6 1.2 %gather_fusion.1 = bf16[256,576]{1,0:T(8,128)(2,1)S(1)} fusion(bf16[128,576]{1,0:T(8,128)(2,1)S(1)} %copy.55, s32[1024]{0:T(1024)S(1)} %pad_clamp_fusion.2), kind=kCustom, calls=%fused_computation.1 | custom fusion | bytes 590848 | tf_op jit(solution)/shard_map/jit(_take)/gather | solution.py:21
  23.8 0.9 select_select_fusion.1
  24.7 11.2 %all-to-all-done.2 = bf16[16,1,16,1024]{3,2,1,0:T(8,128)(2,1)S(1)} async-done(((bf16[16,1,16,1024]{3,2,1,0:T(8,128)(2,1)}), bf16[16,1,16,1024]{3,2,1,0:T(8,128)(2,1)S(1)}, u32[]{:S(2)}, u32[]{:S(2)}) %all-to-all-start.2) | async-done | bytes 524320 | tf_op jit(solution)/shard_map/all_to_all | solution.py:121
  35.9 4.9 %all-to-all-start.1 = ((bf16[16,16,576]{2,1,0:T(8,128)(2,1)}), bf16[16,16,576]{2,1,0:T(8,128)(2,1)S(1)}, u32[]{:S(2)}, u32[]{:S(2)}) async-start(bf16[16,16,576]{2,1,0:T(8,128)(2,1)} %select_select_fusion.1), calls=%async_computation.1 | async-start | bytes 655360 | tf_op jit(solution)/shard_map/all_to_all | solution.py:52
  40.8 6.4 %fusion.5 = bf16[16,1,16,3584]{3,2,1,0:T(8,128)(2,1)} fusion(bf16[1,1024,3584]{2,1,0:T(8,128)(2,1)} %param.17, bf16[16,1,16,1024]{3,2,1,0:T(8,128)(2,1)S(1)} %all-to-all-done.2), kind=kOutput, calls=%fused_computation.7 | convolution fusion | flops 1879965696 | bytes 9699328 | tf_op jit(solution)/shard_map/dekh,ehm->dekm/dot_general | solution.py:119
  47.2 3.0 %all-to-all-done.1 = bf16[16,16,576]{2,1,0:T(8,128)(2,1)S(1)} async-done(((bf16[16,16,576]{2,1,0:T(8,128)(2,1)}), bf16[16,16,576]{2,1,0:T(8,128)(2,1)S(1)}, u32[]{:S(2)}, u32[]{:S(2)}) %all-to-all-start.1) | async-done | bytes 294944 | tf_op jit(solution)/shard_map/all_to_all | solution.py:52
  50.2 5.4 %all-to-all-start.3 = ((bf16[16,1,16,3584]{3,2,1,0:T(8,128)(2,1)}), bf16[16,1,16,3584]{3,2,1,0:T(8,128)(2,1)S(1)}, u32[]{:S(2)}, u32[]{:S(2)}) async-start(bf16[16,1,16,3584]{3,2,1,0:T(8,128)(2,1)} %fusion.5), calls=%async_computation.3 | async-start | bytes 3670016 | tf_op jit(solution)/shard_map/all_to_all | solution.py:125
  55.6 0.1 reduce_sum.86
  55.7 0.7 eq.111
  56.3 0.0 copy-done.5
  56.3 0.6 slice.7
  57.0 0.0 copy-done
  57.0 1.5 %fusion.33 = (f32[4,4,64]{2,0,1:T(4,128)S(1)}, f32[4,4,64,4]{2,3,0,1:T(4,128)S(1)}) fusion(bf16[4,4,64,576]{3,2,1,0:T(8,128)(2,1)S(1)} %copy-done, bf16[4,4,576,1]{2,1,0,3:T(4,128)(2,1)} %bitcast.70, pred[4,4]{1,0:T(4,128)(4,1)S(1)} %iota_compare_fusion.6), kind=kOutput, calls=%fused_computation.76 | convolution fusion | flops 4729856 | bytes 1218576 | tf_op jit(solution)/shard_map/sqhk,uqk->sqhu/dot_general | solution.py:61
  58.4 0.1 reduce_max.44
  58.5 0.0 copy-done.3
  58.5 0.6 mul.81
  59.1 0.7 fusion.32
  59.8 0.6 pad_clamp_fusion
  60.4 0.5 broadcast.349
  60.9 0.7 reduce.6
  61.6 0.1 eq.109
  61.7 2.3 %fusion.34 = (f32[1024]{0:T(1024)S(1)}, f32[1024,256]{0,1:T(8,128)}) fusion(bf16[256,576]{1,0:T(8,128)(2,1)S(1)} %bitcast.68, bf16[1024,576]{1,0:T(8,128)(2,1)S(1)} %bitcast.62, s32[1024]{0:T(1024)} %eq.111, s32[256]{0:T(256)S(1)} %eq.109), kind=kOutput, calls=%fused_computation.77 | convolution fusion | flops 303037440 | bytes 2532352 | tf_op jit(solution)/shard_map/rk,ck->rc/dot_general | solution.py:73
  64.0 0.1 reduce_max.42
  64.0 2.5 %copy.56 = f32[1024,256]{1,0:T(8,128)} copy(f32[1024,256]{0,1:T(8,128)} %get-tuple-element.14) | data formatting | bytes 2097152 | tf_op jit(solution)/shard_map/jit(_where)/select_n | solution.py:80
  66.6 1.4 %exponential_reduce_fusion = f32[1024]{0:T(1024)S(1)} fusion(f32[1024,256]{0,1:T(8,128)} %get-tuple-element.14, f32[1024]{0:T(1024)S(1)} %max.57), kind=kLoop, calls=%fused_computation.20 | loop fusion | flops 523264 | bytes 1056768 | tf_op jit(solution)/shard_map/reduce_sum | solution.py:85
  68.0 0.1 reduce_sum.83
  68.1 1.7 %fusion.23 = f32[4,4,64,512]{3,2,1,0:T(8,128)S(1)} fusion(f32[4,4,64,256]{3,2,1,0:T(8,128)} %bitcast.65, f32[4,4,64]{2,1,0:T(4,128)S(1)} %copy.60, bf16[256,576]{1,0:T(8,128)(2,1)S(1)} %bitcast.69), kind=kOutput, calls=%fused_computation.22 | convolution fusion | flops 268959744 | bytes 3416064 | tf_op jit(solution)/shard_map/sqhc,cl->sqhl/dot_general | solution.py:86
  69.9 1.5 %fusion.9 = bf16[4,4,64,512]{3,2,1,0:T(8,128)(2,1)} fusion(f32[4,4,64,512]{3,2,1,0:T(8,128)S(1)} %fusion.23, f32[4,4,64]{2,1,0:T(4,128)S(1)} %copy.65, bf16[4,4,512]{2,1,0:T(4,128)(2,1)S(1)} %copy-done.4, bf16[4,4,64,4]{2,3,0,1:T(4,128)(2,1)S(1)} %get-tuple-element.5), kind=kOutput, calls=%fused_computation.10 | convolution fusion | flops 5767168 | bytes 3174400 | tf_op jit(solution)/shard_map/sqhu,uql->sqhl/dot_general | solution.py:92
  71.3 26.0 %all-to-all-done.3 = bf16[16,1,16,3584]{3,2,1,0:T(8,128)(2,1)S(1)} async-done(((bf16[16,1,16,3584]{3,2,1,0:T(8,128)(2,1)}), bf16[16,1,16,3584]{3,2,1,0:T(8,128)(2,1)S(1)}, u32[]{:S(2)}, u32[]{:S(2)}) %all-to-all-start.3) | async-done | bytes 1835040 | tf_op jit(solution)/shard_map/all_to_all | solution.py:125
  97.4 2.3 %gather_fusion.3 = bf16[128,3584]{1,0:T(8,128)(2,1)} fusion(bf16[256,3584]{1,0:T(8,128)(2,1)S(1)} %bitcast.64, s32[1024]{0:T(1024)} %pad_clamp_fusion), kind=kCustom, calls=%fused_computation.3 | custom fusion | bytes 1835520 | tf_op jit(solution)/shard_map/jit(_take)/gather | solution.py:127
  99.7 0.0 copy-done.6
  99.7 2.6 %multiply_reduce_fusion = bf16[4,4,3584]{2,1,0:T(4,128)(2,1)} fusion(f32[4,4,8]{2,1,0:T(4,128)S(1)} %copy-done.6, pred[4,4,8]{2,1,0:T(4,128)(4,1)S(1)} %compare_and_fusion, bf16[128,3584]{1,0:T(8,128)(2,1)} %gather_fusion.3), kind=kLoop, calls=%fused_computation.11 | loop fusion | flops 1777664 | bytes 1032832 | tf_op jit(solution)/shard_map/reduce_sum | solution.py:129
  (26 shorter events, 0.2 us)
Async XLA Ops:
  0.6 56.3 %copy-start = (bf16[4,4,64,576]{3,2,1,0:T(8,128)(2,1)S(1)}, bf16[4,4,64,576]{3,2,1,0:T(8,128)(2,1)}, u32[]{:S(2)}) copy-start(bf16[4,4,64,576]{3,2,1,0:T(8,128)(2,1)} %param.12) | copy-start | bytes 3538948
  0.6 13.4 %copy-start.1 = (bf16[4,4,8,1024]{3,2,1,0:T(8,128)(2,1)S(1)}, bf16[4,4,8,1024]{3,2,1,0:T(8,128)(2,1)}, u32[]{:S(2)}) copy-start(bf16[4,4,8,1024]{3,2,1,0:T(8,128)(2,1)} %param.14) | copy-start | bytes 786436
  5.9 10.3 %all-to-all-start = ((s32[16,1,16]{2,1,0:T(1,128)}), s32[16,1,16]{2,1,0:T(1,128)S(1)}, u32[]{:S(2)}, u32[]{:S(2)}) async-start(s32[16,1,16]{2,1,0:T(1,128)} %select_n.138), calls=%async_computation | async-start | bytes 16384 | tf_op jit(solution)/shard_map/all_to_all | solution.py:53
  15.2 7.2 %copy-start.2 = (bf16[128,576]{0,1:T(8,128)(2,1)S(1)}, bf16[128,576]{0,1:T(8,128)(2,1)}, u32[]{:S(2)}) copy-start(bf16[128,576]{0,1:T(8,128)(2,1)} %param.9) | copy-start | bytes 442372
  16.2 19.7 %all-to-all-start.2 = ((bf16[16,1,16,1024]{3,2,1,0:T(8,128)(2,1)}), bf16[16,1,16,1024]{3,2,1,0:T(8,128)(2,1)S(1)}, u32[]{:S(2)}, u32[]{:S(2)}) async-start(bf16[16,1,16,1024]{3,2,1,0:T(8,128)(2,1)} %select_select_fusion), calls=%async_computation.2 | async-start | bytes 1048576 | tf_op jit(solution)/shard_map/all_to_all | solution.py:121
  35.9 14.3 %all-to-all-start.1 = ((bf16[16,16,576]{2,1,0:T(8,128)(2,1)}), bf16[16,16,576]{2,1,0:T(8,128)(2,1)S(1)}, u32[]{:S(2)}, u32[]{:S(2)}) async-start(bf16[16,16,576]{2,1,0:T(8,128)(2,1)} %select_select_fusion.1), calls=%async_computation.1 | async-start | bytes 655360 | tf_op jit(solution)/shard_map/all_to_all | solution.py:52
  47.2 9.1 %copy-start.5 = (bf16[4,4,576]{2,1,0:T(4,128)(2,1)S(1)}, bf16[4,4,576]{2,1,0:T(4,128)(2,1)}, u32[]{:S(2)}) copy-start(bf16[4,4,576]{2,1,0:T(4,128)(2,1)} %param.13) | copy-start | bytes 55300
  47.2 11.3 %copy-start.3 = (s32[4,4,8]{2,1,0:T(4,128)S(1)}, s32[4,4,8]{2,1,0:T(4,128)}, u32[]{:S(2)}) copy-start(s32[4,4,8]{2,1,0:T(4,128)} %param.15) | copy-start | bytes 1540
  50.2 47.2 %all-to-all-start.3 = ((bf16[16,1,16,3584]{3,2,1,0:T(8,128)(2,1)}), bf16[16,1,16,3584]{3,2,1,0:T(8,128)(2,1)S(1)}, u32[]{:S(2)}, u32[]{:S(2)}) async-start(bf16[16,1,16,3584]{3,2,1,0:T(8,128)(2,1)} %fusion.5), calls=%async_computation.3 | async-start | bytes 3670016 | tf_op jit(solution)/shard_map/all_to_all | solution.py:125
  68.0 1.9 %copy-start.4 = (bf16[4,4,512]{2,1,0:T(4,128)(2,1)S(1)}, bf16[4,4,512]{2,1,0:T(4,128)(2,1)}, u32[]{:S(2)}) copy-start(bf16[4,4,512]{2,1,0:T(4,128)(2,1)} %slice.7) | copy-start | bytes 49156
  97.4 2.3 %copy-start.6 = (f32[4,4,8]{2,1,0:T(4,128)S(1)}, f32[4,4,8]{2,1,0:T(4,128)}, u32[]{:S(2)}) copy-start(f32[4,4,8]{2,1,0:T(4,128)} %param.16) | copy-start | bytes 1540
where the time goes:
time: 103 us; the launch traced here: 102 us
  waiting for transfers between devices  40.2 us (39%)
  starting transfers between devices  23 us (22%)
  local copies, waits for them, and re-layouts  14.8 us (14%)
  matrix products  13.3 us (13%)
  other arithmetic  10.1 us (10%)
    all_to_all x1, waiting for transfers between devices, expert_layer(): lax.all_to_all(expert_out, 'seq', split_axis=0, concat_axis=0, tiled=True)  26 us
    all_to_all x1, waiting for transfers between devices, expert_layer(): lax.all_to_all(outbox, 'seq', split_axis=0, concat_axis=0, tiled=True)  11.2 us
    all_to_all x1, starting transfers between devices, hand_over(): lax.all_to_all(labels, 'seq', split_axis=0, concat_axis=0, tiled=True)  6.55 us
    dot_general x1, matrix products, expert_layer(): jnp.einsum('dekh,ehm->dekm', lax.all_to_all(outbox, 'seq', split_axis=0,...  6.4 us
    all_to_all x1, starting transfers between devices, expert_layer(): lax.all_to_all(outbox, 'seq', split_axis=0, concat_axis=0, tiled=True)  6.1 us
    all_to_all x1, starting transfers between devices, expert_layer(): lax.all_to_all(expert_out, 'seq', split_axis=0, concat_axis=0, tiled=True)  5.37 us
    all_to_all x1, starting transfers between devices, hand_over(): lax.all_to_all(outbox, 'seq', split_axis=0, concat_axis=0, tiled=True)  4.93 us
    gather x3, local copies, waits for them, and re-layouts, fill_slots(): taken = jnp.take(values, jnp.maximum(sources, 0), axis=0)  4.24 us
  transfers between devices with their start and end apart: 4, of which 3 were waited for; matrix products, arithmetic and copies ran while one was open for 28% of the time, Pallas kernels for 0%

commit v1 on v0

--- a/solution.py
+++ b/solution.py
@@ -1,6 +1,10 @@
+import functools
+
 import jax
 import jax.numpy as jnp
 from jax import lax
+from jax.experimental import pallas as pl
+from jax.experimental.pallas import tpu as pltpu
 from jax.sharding import PartitionSpec as P
 
 ROPE = 64
@@ -130,7 +134,7 @@
     return moe_out.astype(jnp.bfloat16)
 
 
-def per_device(
+def per_device_general(
     prefill_kv,
     lengths,
     assignment,
@@ -147,6 +151,319 @@
     return (context, moe_out)
 
 
+BLOCK = 16
+
+
+def as_column(row):
+    size = row.shape[1]
+    eye = lax.broadcasted_iota(jnp.int32, (size, size), 0) == lax.broadcasted_iota(
+        jnp.int32, (size, size), 1
+    )
+    return jnp.sum(jnp.where(eye, row, 0), axis=1, keepdims=True)
+
+
+def flat_row(table, tokens, top):
+    lanes = tokens * top
+    place = lax.broadcasted_iota(jnp.int32, (top, lanes), 1) % top
+    spread = (place == lax.broadcasted_iota(jnp.int32, (top, lanes), 0)).astype(jnp.float32)
+    wide = jnp.dot(
+        table, spread, precision=lax.Precision.HIGHEST, preferred_element_type=jnp.float32
+    )
+    owner = lax.broadcasted_iota(jnp.int32, (tokens, lanes), 1) // top
+    mine = owner == lax.broadcasted_iota(jnp.int32, (tokens, lanes), 0)
+    return jnp.sum(jnp.where(mine, wide, 0.0), axis=0, keepdims=True)
+
+
+def outbox_kernel(routes_ref, weights_ref, hidden_ref, out_ref):
+    rows, steps, top = routes_ref.shape
+    tokens = rows * steps
+    lanes = tokens * top
+    slots = out_ref.shape[0]
+    routes = jnp.concatenate([routes_ref[i] for i in range(rows)], axis=0).astype(jnp.float32)
+    weights = jnp.concatenate([weights_ref[i] for i in range(rows)], axis=0)
+    route_row = flat_row(routes, tokens, top).astype(jnp.int32)
+    weight_row = flat_row(weights, tokens, top)
+    slot = lax.broadcasted_iota(jnp.int32, (slots, lanes), 0)
+    lane = lax.broadcasted_iota(jnp.int32, (slots, lanes), 1)
+    pick = (lane // top == slot % tokens) & (route_row == slot // tokens)
+    scale = jnp.sum(jnp.where(pick, weight_row, 0.0), axis=1, keepdims=True)
+    chosen = jnp.where(pick, 1.0, 0.0).astype(jnp.bfloat16)
+    moved = jnp.dot(chosen, hidden_ref[...], preferred_element_type=jnp.float32)
+    out_ref[...] = (moved * scale).astype(jnp.bfloat16)
+
+
+def pack_hidden(routes, route_weights, expert_hidden, experts):
+    rows, steps, top, width = expert_hidden.shape
+    tokens = rows * steps
+    return pl.pallas_call(
+        outbox_kernel,
+        out_shape=jax.ShapeDtypeStruct((experts * tokens, width), jnp.bfloat16),
+        cost_estimate=pl.CostEstimate(
+            flops=2 * experts * tokens * tokens * top * width,
+            bytes_accessed=2 * width * tokens * (top + experts),
+            transcendentals=0,
+        ),
+        name="pack_hidden",
+    )(routes, route_weights, expert_hidden.reshape(tokens * top, width))
+
+
+def ceil_rows(position, source, devices):
+    return (position + (devices - 1) - source) // devices
+
+
+def kv_kernel(devices, per_owner, lengths_ref, assignment_ref, kv_ref, out_ref, tags_ref):
+    me = lax.axis_index("seq")
+    requests = lengths_ref.shape[1]
+    here = kv_ref.shape[1]
+    slots = out_ref.shape[0]
+    room = slots // devices
+    length_column = as_column(lengths_ref[...])
+    assignment = assignment_ref[...]
+    number = lax.broadcasted_iota(jnp.int32, (requests, requests), 0)
+    before = jnp.sum(jnp.where(number < assignment, length_column, 0), axis=0, keepdims=True)
+    own = jnp.sum(jnp.where(number == assignment, length_column, 0), axis=0, keepdims=True)
+    after = before + own
+    low = ceil_rows(before, me, devices)
+    count = ceil_rows(after, me, devices) - low
+    line = lax.broadcasted_iota(jnp.int32, (requests, requests), 1)
+    same = (number // per_owner == line // per_owner) & (number < line)
+    offset = jnp.sum(jnp.where(same, as_column(count), 0), axis=0, keepdims=True)
+    slot = lax.broadcasted_iota(jnp.int32, (slots, requests), 0)
+    decode = lax.broadcasted_iota(jnp.int32, (slots, requests), 1)
+    rank = slot % room - offset
+    held = (slot // room == decode // per_owner) & (rank >= 0) & (rank < count)
+    source = jnp.sum(jnp.where(held, low + rank + 1, 0), axis=1, keepdims=True) - 1
+    pick = source == lax.broadcasted_iota(jnp.int32, (slots, here), 1)
+    out_ref[...] = lax.dot_general(
+        jnp.where(pick, 1.0, 0.0).astype(jnp.bfloat16),
+        kv_ref[...],
+        (((1,), (1,)), ((), ())),
+        preferred_element_type=jnp.float32,
+    ).astype(jnp.bfloat16)
+    place = lax.broadcasted_iota(jnp.int32, (1, slots), 1)
+    sender, rank = place // room, place % room
+    tags = jnp.full((1, slots), -1, jnp.int32)
+    decode = lax.broadcasted_iota(jnp.int32, (1, requests), 1)
+    taken = jnp.zeros((1, slots), jnp.int32)
+    for q in range(per_owner):
+        mine = decode == me * per_owner + q
+        first = jnp.sum(jnp.where(mine, before, 0), axis=1, keepdims=True)
+        last = jnp.sum(jnp.where(mine, after, 0), axis=1, keepdims=True)
+        arriving = ceil_rows(last, sender, devices) - ceil_rows(first, sender, devices)
+        tags = jnp.where((rank >= taken) & (rank < taken + arriving), q, tags)
+        taken = taken + arriving
+    tags_ref[...] = tags
+
+
+def pack_kv(prefill_kv, lengths, assignment, devices, per_owner, room):
+    here, width = prefill_kv.shape
+    slots = devices * room
+    return pl.pallas_call(
+        functools.partial(kv_kernel, devices, per_owner),
+        out_shape=(
+            jax.ShapeDtypeStruct((slots, width), jnp.bfloat16),
+            jax.ShapeDtypeStruct((1, slots), jnp.int32),
+        ),
+        cost_estimate=pl.CostEstimate(
+            flops=2 * slots * here * width,
+            bytes_accessed=2 * width * (here + slots),
+            transcendentals=0,
+        ),
+        name="pack_kv",
+    )(lengths.reshape(1, -1), assignment.reshape(1, -1), prefill_kv.T)
+
+
+def attend_kernel(queries_ref, fresh_ref, cache_ref, tags_ref, out_ref):
+    mine = pl.program_id(0)
+    steps, _, heads, width = queries_ref.shape
+    latent = out_ref.shape[3]
+    per_owner = fresh_ref.shape[1]
+    rows = steps * heads
+    queries = queries_ref[...].reshape(rows, width)
+    cache = cache_ref[...]
+    fresh = jnp.concatenate([fresh_ref[u].astype(jnp.float32) for u in range(steps)], axis=0)
+    fresh = fresh.astype(jnp.bfloat16)
+    contract = (((1,), (1,)), ((), ()))
+    scores = (
+        lax.dot_general(queries, cache, contract, preferred_element_type=jnp.float32)
+        * score_scale
+    )
+    scores = jnp.where(tags_ref[...] == mine, scores, masked_score)
+    fresh_scores = (
+        lax.dot_general(queries, fresh, contract, preferred_element_type=jnp.float32)
+        * score_scale
+    )
+    step = lax.broadcasted_iota(jnp.int32, (rows, steps * per_owner), 0) // heads
+    other = lax.broadcasted_iota(jnp.int32, (rows, steps * per_owner), 1)
+    seen = (other % per_owner == mine) & (other // per_owner <= step)
+    fresh_scores = jnp.where(seen, fresh_scores, masked_score)
+    top_score = jnp.maximum(
+        jnp.max(scores, axis=1, keepdims=True), jnp.max(fresh_scores, axis=1, keepdims=True)
+    )
+    weights = jnp.exp(scores - top_score)
+    fresh_weights = jnp.exp(fresh_scores - top_score)
+    denominator = jnp.sum(weights, axis=1, keepdims=True) + jnp.sum(
+        fresh_weights, axis=1, keepdims=True
+    )
+    summed = jnp.dot(
+        weights.astype(jnp.bfloat16), cache[:, :latent], preferred_element_type=jnp.float32
+    ) + jnp.dot(
+        fresh_weights.astype(jnp.bfloat16),
+        fresh[:, :latent],
+        preferred_element_type=jnp.float32,
+    )
+    context = (summed / denominator).astype(jnp.bfloat16)
+    out_ref[...] = context.reshape(steps, 1, heads, latent)
+
+
+def attend(queries, new_kv, kv_cache, tags):
+    steps, per_owner, heads, width = queries.shape
+    slots = kv_cache.shape[0]
+    latent = width - ROPE
+    return pl.pallas_call(
+        attend_kernel,
+        grid=(per_owner,),
+        in_specs=[
+            pl.BlockSpec((steps, 1, heads, width), lambda q: (0, q, 0, 0)),
+            pl.BlockSpec((steps, per_owner, width), lambda q: (0, 0, 0)),
+            pl.BlockSpec((slots, width), lambda q: (0, 0)),
+            pl.BlockSpec((1, slots), lambda q: (0, 0)),
+        ],
+        out_specs=pl.BlockSpec((steps, 1, heads, latent), lambda q: (0, q, 0, 0)),
+        out_shape=jax.ShapeDtypeStruct((steps, per_owner, heads, latent), jnp.bfloat16),
+        cost_estimate=pl.CostEstimate(
+            flops=2 * steps * per_owner * heads * slots * (width + latent),
+            bytes_accessed=2 * steps * per_owner * heads * (width + latent),
+            transcendentals=steps * per_owner * heads * slots,
+        ),
+        name="attend",
+    )(queries, new_kv, kv_cache, tags)
+
+
+def expert_kernel(bits, arrived_ref, down_ref, keep_ref, send_ref, sorted_ref):
+    me = lax.axis_index("seq")
+    blocks = 1 << len(bits)
+    half = keep_ref.shape[0]
+
+    @pl.when(pl.program_id(0) == 0)
+    def _():
+        for place in range(blocks):
+            apart = 0
+            for i, bit in enumerate(bits):
+                if place >> (len(bits) - 1 - i) & 1:
+                    apart |= bit
+            start = pl.multiple_of((me ^ apart) * BLOCK, BLOCK)
+            sorted_ref[place * BLOCK : (place + 1) * BLOCK, :] = arrived_ref[
+                pl.ds(start, BLOCK), :
+            ]
+
+    result = jnp.dot(sorted_ref[...], down_ref[0], preferred_element_type=jnp.float32)
+    keep_ref[...] = result[:half]
+    send_ref[...] = result[half:].astype(jnp.bfloat16)
+
+
+def expert_part(arrived, expert_down, bits, part, parts, tile):
+    slots, hidden_width = arrived.shape
+    width = expert_down.shape[2] // parts
+    half = slots // 2
+    tiles = width // tile
+    return pl.pallas_call(
+        functools.partial(expert_kernel, bits),
+        grid=(tiles,),
+        in_specs=[
+            pl.BlockSpec((slots, hidden_width), lambda i: (0, 0)),
+            pl.BlockSpec((1, hidden_width, tile), lambda i: (0, 0, i + part * tiles)),
+        ],
+        out_specs=[
+            pl.BlockSpec((half, tile), lambda i: (0, i)),
+            pl.BlockSpec((half, tile), lambda i: (0, i)),
+        ],
+        out_shape=(
+            jax.ShapeDtypeStruct((half, width), jnp.float32),
+            jax.ShapeDtypeStruct((half, width), jnp.bfloat16),
+        ),
+        scratch_shapes=[pltpu.VMEM((slots, hidden_width), jnp.bfloat16)],
+        cost_estimate=pl.CostEstimate(
+            flops=2 * slots * hidden_width * width,
+            bytes_accessed=2 * hidden_width * width + 6 * half * width,
+            transcendentals=0,
+        ),
+        name="expert_part",
+    )(arrived, expert_down)
+
+
+def swap(values, bit, devices):
+    return lax.ppermute(values, "seq", [(i, i ^ bit) for i in range(devices)])
+
+
+def fold(kept, received):
+    total = kept + received.astype(jnp.float32)
+    half = total.shape[0] // 2
+    return total[:half], total[half:].astype(jnp.bfloat16)
+
+
+def per_device_dense(
+    prefill_kv,
+    lengths,
+    assignment,
+    queries,
+    new_kv,
+    expert_hidden,
+    routes,
+    route_weights,
+    expert_down,
+):
+    devices = lax.axis_size("seq")
+    steps, per_owner = queries.shape[:2]
+    rows, _, top, hidden_width = expert_hidden.shape
+    model_width = expert_down.shape[2]
+    outbox = pack_hidden(routes, route_weights, expert_hidden, devices)
+    arrived = lax.all_to_all(
+        outbox.reshape(devices, BLOCK, hidden_width), "seq", split_axis=0, concat_axis=0, tiled=True
+    ).reshape(devices * BLOCK, hidden_width)
+    kv_outbox, tags = pack_kv(
+        prefill_kv, lengths, assignment, devices, per_owner, 2 * HALF * per_owner
+    )
+
+    orders = ((1, 2, 4, 8), (1, 4, 2, 8))
+    parts = len(orders)
+    flows = []
+    for part, bits in enumerate(orders):
+        kept, sent = expert_part(arrived, expert_down, bits, part, parts, 256)
+        flows.append((kept, sent, swap(sent, bits[0], devices)))
+    flows = [fold(kept, received) for kept, _, received in flows]
+    received = [swap(sent, bits[1], devices) for (_, sent), bits in zip(flows, orders)]
+
+    kv_outbox, _ = lax.optimization_barrier((kv_outbox, [sent for _, sent in flows]))
+    kv_cache = lax.all_to_all(
+        kv_outbox.reshape(devices, -1, kv_outbox.shape[1]),
+        "seq",
+        split_axis=0,
+        concat_axis=0,
+        tiled=True,
+    ).reshape(kv_outbox.shape)
+    context = attend(queries, new_kv, kv_cache, tags)
+
+    for level in (2, 3):
+        flows = [fold(kept, got) for (kept, _), got in zip(flows, received)]
+        received = [swap(sent, bits[level], devices) for (_, sent), bits in zip(flows, orders)]
+    final = [kept + got.astype(jnp.float32) for (kept, _), got in zip(flows, received)]
+    moe_out = jnp.concatenate(final, axis=1).astype(jnp.bfloat16)
+    return context, moe_out.reshape(rows, steps, model_width)
+
+
+def per_device(*arrays):
+    expert_hidden, expert_down = arrays[5], arrays[8]
+    devices = lax.axis_size("seq")
+    rows, steps, top = expert_hidden.shape[:3]
+    tokens = rows * steps
+    experts = expert_down.shape[0] * devices
+    bound = max(2, 2 * tokens * top // experts)
+    if devices == 16 and experts == devices and tokens == BLOCK and bound == tokens:
+        return per_device_dense(*arrays)
+    return per_device_general(*arrays)
+
+
 def solution(mesh):
     placed = (
         P(("groups", "seq"), None),

time: 103 us -> 75.7 us (0.73)
  the two profiles are of different devices: /device:TPU:15 before, /device:TPU:0 now
where the time goes in v1:
time: 75.7 us; the launch traced here: 75 us
  Pallas kernels  23.2 us (31%)
  blocking collectives  22 us (29%)
  waiting for transfers between devices  13.7 us (18%)
  starting transfers between devices  12.3 us (16%)
  other arithmetic  2.18 us (3%)
  local copies, waits for them, and re-layouts  0.86 us (1%)
    all_to_all x1, blocking collectives, per_device_dense(): lax.all_to_all(outbox.reshape(devices, BLOCK, hidden_width), 'seq', split...  22 us
    ppermute x8, waiting for transfers between devices, swap(): return lax.ppermute(values, 'seq', [(i, i ^ bit) for i in range(devices)])  13.7 us
    pallas_call x2, Pallas kernels, expert_part(): pl.pallas_call(functools.partial(expert_kernel, bits), grid=(tiles,), in_...  13 us
    ppermute x8, starting transfers between devices, swap(): return lax.ppermute(values, 'seq', [(i, i ^ bit) for i in range(devices)])  8.8 us
    pallas_call x1, Pallas kernels, attend(): pl.pallas_call(attend_kernel, grid=(per_owner,), in_specs=[pl.BlockSpec((...  5.73 us
    all_to_all x1, starting transfers between devices, per_device_dense(): lax.all_to_all(kv_outbox.reshape(devices, -1, kv_outbox.shape[1]), 'seq',...  3.54 us
    pallas_call x1, Pallas kernels, pack_kv(): pl.pallas_call(functools.partial(kv_kernel, devices, per_owner), out_shap...  2.29 us
    pallas_call x1, Pallas kernels, pack_hidden(): pl.pallas_call(outbox_kernel, out_shape=jax.ShapeDtypeStruct((experts * t...  2.2 us
  transfers between devices with their start and end apart: 9, of which 5 were waited for; matrix products, arithmetic and copies ran while one was open for 3% of the time, Pallas kernels for 12%

profile of v1, /device:TPU:0, one launch (start us, length us, event | category | flops | bytes accessed | tf_op | source)
XLA Modules:
  0.0 75.0 jit_solution(10128160543650990489)
XLA Ops:
  0.6 2.2 %pack_hidden.1 = bf16[256,1024]{1,0:T(8,128)(2,1)} custom-call(s32[4,4,8]{2,1,0:T(4,128)} %routes_ref.1, f32[4,4,8]{2,1,0:T(4,128)} %weights_ref.1, bf16[128,1024]{1,0:T(8,128)(2,1)} %bitcast.12), custom_call_target="tpu_custom_call" | custom-call | flops 67108864 | bytes 786432 | tf_op jit(solution)/shard_map/pack_hidden/pallas_call | solution.py:198
  2.8 22.0 %all_to_all.10 = bf16[16,16,1024]{2,1,0:T(8,128)(2,1)} all-to-all(bf16[16,16,1024]{2,1,0:T(8,128)(2,1)} %bitcast.10), channel_id=1, replica_groups=mesh['groups'=2,'seq'=16] {'seq'}, dimensions={0} | all-to-all | bytes 1048576 | tf_op jit(solution)/shard_map/all_to_all | solution.py:421
  24.8 6.5 %expert_part.2 = (f32[128,1792]{1,0:T(8,128)}, bf16[128,1792]{1,0:T(8,128)(2,1)}) custom-call(bf16[256,1024]{1,0:T(8,128)(2,1)} %bitcast.8, bf16[1,1024,3584]{2,1,0:T(8,128)(2,1)} %down_ref.3), custom_call_target="tpu_custom_call" | custom-call | flops 939524096 | bytes 5046272 | tf_op jit(solution)/shard_map/expert_part/pallas_call | solution.py:370
  31.3 0.0 copy-start.1
  31.3 0.0 collective-permute-start
  31.3 2.3 %pack_kv.1 = (bf16[256,576]{1,0:T(8,128)(2,1)}, s32[1,256]{1,0:T(1,128)}) custom-call(s32[1,64]{1,0:T(1,128)} %bitcast.14, s32[1,64]{1,0:T(1,128)} %bitcast.15, bf16[576,128]{1,0:T(8,128)(2,1)} %bitcast.13), custom_call_target="tpu_custom_call" | custom-call | flops 37748736 | bytes 442368 | tf_op jit(solution)/shard_map/pack_kv/pallas_call | solution.py:261
  33.6 6.5 %expert_part.3 = (f32[128,1792]{1,0:T(8,128)}, bf16[128,1792]{1,0:T(8,128)(2,1)}) custom-call(bf16[256,1024]{1,0:T(8,128)(2,1)} %bitcast.9, bf16[1,1024,3584]{2,1,0:T(8,128)(2,1)} %down_ref.3), custom_call_target="tpu_custom_call" | custom-call | flops 939524096 | bytes 5046272 | tf_op jit(solution)/shard_map/expert_part/pallas_call | solution.py:370
  40.1 0.4 collective-permute-start.1
  40.5 0.0 collective-permute-done
  40.5 0.0 copy-done.1
  40.5 0.1 convert_add_fusion.1
  40.6 0.8 %collective-permute-start.2 = (bf16[64,1792]{1,0:T(8,128)(2,1)S(1)}, bf16[64,1792]{1,0:T(8,128)(2,1)S(1)}, u32[]{:S(2)}, u32[]{:S(2)}) collective-permute-start(bf16[64,1792]{1,0:T(8,128)(2,1)S(1)} %slice.83), channel_id=1, source_target_pairs={{0,2},{1,3},{2,0},{3,1},{4,6},{5,7},{6,4},{7,5},{8,10},{9,11},{10,... | collective-permute-start | bytes 688136 | tf_op jit(solution)/shard_map/ppermute | solution.py:396
  41.4 0.7 collective-permute-done.1
  42.1 1.3 %convert_add_fusion = f32[128,1792]{1,0:T(8,128)S(1)} fusion(f32[128,1792]{1,0:T(8,128)} %get-tuple-element.12, bf16[128,1792]{1,0:T(8,128)(2,1)S(1)} %collective-permute-done.1), kind=kLoop, calls=%fused_computation | loop fusion | flops 458752 | bytes 2293760 | tf_op jit(solution)/shard_map/add | solution.py:400
  43.4 1.7 %collective-permute-start.5 = (bf16[64,1792]{1,0:T(8,128)(2,1)S(1)}, bf16[64,1792]{1,0:T(8,128)(2,1)S(1)}, u32[]{:S(2)}, u32[]{:S(2)}) collective-permute-start(bf16[64,1792]{1,0:T(8,128)(2,1)S(1)} %slice.82), channel_id=1, source_target_pairs={{0,4},{1,5},{2,6},{3,7},{4,0},{5,1},{6,2},{7,3},{8,12},{9,13},{10,... | collective-permute-start | bytes 688136 | tf_op jit(solution)/shard_map/ppermute | solution.py:396
  45.1 3.5 %all-to-all-start.1 = ((bf16[16,16,576]{2,1,0:T(8,128)(2,1)}), bf16[16,16,576]{2,1,0:T(8,128)(2,1)S(1)}, u32[]{:S(2)}, u32[]{:S(2)}) async-start(bf16[16,16,576]{2,1,0:T(8,128)(2,1)} %bitcast.6), calls=%async_computation.1 | async-start | bytes 655360 | tf_op jit(solution)/shard_map/all_to_all | solution.py:438
  48.7 0.0 collective-permute-done.2
  48.8 1.9 %collective-permute-start.3 = (bf16[32,1792]{1,0:T(8,128)(2,1)S(1)}, bf16[32,1792]{1,0:T(8,128)(2,1)S(1)}, u32[]{:S(2)}, u32[]{:S(2)}) collective-permute-start(bf16[32,1792]{1,0:T(8,128)(2,1)S(1)} %slice.85), channel_id=1, source_target_pairs={{0,4},{1,5},{2,6},{3,7},{4,0},{5,1},{6,2},{7,3},{8,12},{9,13},{10,... | collective-permute-start | bytes 344072 | tf_op jit(solution)/shard_map/ppermute | solution.py:396
  50.7 0.7 collective-permute-done.5
  51.5 0.9 %collective-permute-start.6 = (bf16[32,1792]{1,0:T(8,128)(2,1)S(1)}, bf16[32,1792]{1,0:T(8,128)(2,1)S(1)}, u32[]{:S(2)}, u32[]{:S(2)}) collective-permute-start(bf16[32,1792]{1,0:T(8,128)(2,1)S(1)} %slice.84), channel_id=1, source_target_pairs={{0,2},{1,3},{2,0},{3,1},{4,6},{5,7},{6,4},{7,5},{8,10},{9,11},{10,... | collective-permute-start | bytes 344072 | tf_op jit(solution)/shard_map/ppermute | solution.py:396
  52.3 7.2 %collective-permute-done.3 = bf16[32,1792]{1,0:T(8,128)(2,1)S(1)} collective-permute-done((bf16[32,1792]{1,0:T(8,128)(2,1)S(1)}, bf16[32,1792]{1,0:T(8,128)(2,1)S(1)}, u32[]{:S(2)}, u32[]{:S(2)}) %collective-permute-start.3) | collective-permute-done | bytes 114720 | tf_op jit(solution)/shard_map/ppermute | solution.py:396
  59.5 2.5 %collective-permute-start.4 = (bf16[16,1792]{1,0:T(8,128)(2,1)S(1)}, bf16[16,1792]{1,0:T(8,128)(2,1)S(1)}, u32[]{:S(2)}, u32[]{:S(2)}) collective-permute-start(bf16[16,1792]{1,0:T(8,128)(2,1)S(1)} %slice.87), channel_id=1, source_target_pairs={{0,8},{1,9},{2,10},{3,11},{4,12},{5,13},{6,14},{7,15},{8,0},{9,1},... | collective-permute-start | bytes 172040 | tf_op jit(solution)/shard_map/ppermute | solution.py:396
  62.0 0.0 collective-permute-done.6
  62.1 0.6 collective-permute-start.7
  62.6 3.4 %collective-permute-done.4 = bf16[16,1792]{1,0:T(8,128)(2,1)S(1)} collective-permute-done((bf16[16,1792]{1,0:T(8,128)(2,1)S(1)}, bf16[16,1792]{1,0:T(8,128)(2,1)S(1)}, u32[]{:S(2)}, u32[]{:S(2)}) %collective-permute-start.4) | collective-permute-done | bytes 57376 | tf_op jit(solution)/shard_map/ppermute | solution.py:396
  66.0 1.8 %collective-permute-done.7 = bf16[16,1792]{1,0:T(8,128)(2,1)S(1)} collective-permute-done((bf16[16,1792]{1,0:T(8,128)(2,1)S(1)}, bf16[16,1792]{1,0:T(8,128)(2,1)S(1)}, u32[]{:S(2)}, u32[]{:S(2)}) %collective-permute-start.7) | collective-permute-done | bytes 57376 | tf_op jit(solution)/shard_map/ppermute | solution.py:396
  67.8 0.7 pad_maximum_fusion
  68.5 0.0 all-to-all-done.1
  68.5 0.0 copy-start
  68.5 0.7 copy-done
  69.3 5.7 %attend.1 = bf16[4,4,64,512]{3,2,1,0:T(8,128)(2,1)} custom-call(bf16[4,4,64,576]{3,2,1,0:T(8,128)(2,1)} %queries_ref.1, bf16[4,4,576]{2,1,0:T(4,128)(2,1)} %fresh_ref.1, bf16[256,576]{1,0:T(8,128)(2,1)} %bitcast.11, s32[1,256]{1,0:T(1,128)} %get-tuple-element.15.tags_ref), custom_call_target="tpu_custom_call" | custom-call | flops 570425344 | bytes 2228224 | tf_op jit(solution)/shard_map/attend/pallas_call | solution.py:323
  (14 shorter events, 0.3 us)
Async XLA Ops:
  31.3 9.2 %copy-start.1 = (f32[128,1792]{1,0:T(8,128)S(1)}, f32[128,1792]{1,0:T(8,128)}, u32[]{:S(2)}) copy-start(f32[128,1792]{1,0:T(8,128)} %get-tuple-element.10) | copy-start | bytes 2752516
  31.3 9.2 %collective-permute-start = (bf16[128,1792]{1,0:T(8,128)(2,1)}, bf16[128,1792]{1,0:T(8,128)(2,1)S(1)}, u32[]{:S(2)}, u32[]{:S(2)}) collective-permute-start(bf16[128,1792]{1,0:T(8,128)(2,1)} %get-tuple-element.11), channel_id=1, source_target_pairs={{0,1},{1,0},{2,3},{3,2},{4,5},{5,4},{6,7},{7,6},{8,9},{9,8},{10,11... | collective-permute-start | bytes 1376264 | tf_op jit(solution)/shard_map/ppermute | solution.py:396
  40.1 2.1 %collective-permute-start.1 = (bf16[128,1792]{1,0:T(8,128)(2,1)}, bf16[128,1792]{1,0:T(8,128)(2,1)S(1)}, u32[]{:S(2)}, u32[]{:S(2)}) collective-permute-start(bf16[128,1792]{1,0:T(8,128)(2,1)} %get-tuple-element.13), channel_id=1, source_target_pairs={{0,1},{1,0},{2,3},{3,2},{4,5},{5,4},{6,7},{7,6},{8,9},{9,8},{10,11... | collective-permute-start | bytes 1376264 | tf_op jit(solution)/shard_map/ppermute | solution.py:396
  40.6 8.1 %collective-permute-start.2 = (bf16[64,1792]{1,0:T(8,128)(2,1)S(1)}, bf16[64,1792]{1,0:T(8,128)(2,1)S(1)}, u32[]{:S(2)}, u32[]{:S(2)}) collective-permute-start(bf16[64,1792]{1,0:T(8,128)(2,1)S(1)} %slice.83), channel_id=1, source_target_pairs={{0,2},{1,3},{2,0},{3,1},{4,6},{5,7},{6,4},{7,5},{8,10},{9,11},{10,... | collective-permute-start | bytes 688136 | tf_op jit(solution)/shard_map/ppermute | solution.py:396
  43.4 7.9 %collective-permute-start.5 = (bf16[64,1792]{1,0:T(8,128)(2,1)S(1)}, bf16[64,1792]{1,0:T(8,128)(2,1)S(1)}, u32[]{:S(2)}, u32[]{:S(2)}) collective-permute-start(bf16[64,1792]{1,0:T(8,128)(2,1)S(1)} %slice.82), channel_id=1, source_target_pairs={{0,4},{1,5},{2,6},{3,7},{4,0},{5,1},{6,2},{7,3},{8,12},{9,13},{10,... | collective-permute-start | bytes 688136 | tf_op jit(solution)/shard_map/ppermute | solution.py:396
  45.1 23.4 %all-to-all-start.1 = ((bf16[16,16,576]{2,1,0:T(8,128)(2,1)}), bf16[16,16,576]{2,1,0:T(8,128)(2,1)S(1)}, u32[]{:S(2)}, u32[]{:S(2)}) async-start(bf16[16,16,576]{2,1,0:T(8,128)(2,1)} %bitcast.6), calls=%async_computation.1 | async-start | bytes 655360 | tf_op jit(solution)/shard_map/all_to_all | solution.py:438
  48.8 10.7 %collective-permute-start.3 = (bf16[32,1792]{1,0:T(8,128)(2,1)S(1)}, bf16[32,1792]{1,0:T(8,128)(2,1)S(1)}, u32[]{:S(2)}, u32[]{:S(2)}) collective-permute-start(bf16[32,1792]{1,0:T(8,128)(2,1)S(1)} %slice.85), channel_id=1, source_target_pairs={{0,4},{1,5},{2,6},{3,7},{4,0},{5,1},{6,2},{7,3},{8,12},{9,13},{10,... | collective-permute-start | bytes 344072 | tf_op jit(solution)/shard_map/ppermute | solution.py:396
  51.5 10.6 %collective-permute-start.6 = (bf16[32,1792]{1,0:T(8,128)(2,1)S(1)}, bf16[32,1792]{1,0:T(8,128)(2,1)S(1)}, u32[]{:S(2)}, u32[]{:S(2)}) collective-permute-start(bf16[32,1792]{1,0:T(8,128)(2,1)S(1)} %slice.84), channel_id=1, source_target_pairs={{0,2},{1,3},{2,0},{3,1},{4,6},{5,7},{6,4},{7,5},{8,10},{9,11},{10,... | collective-permute-start | bytes 344072 | tf_op jit(solution)/shard_map/ppermute | solution.py:396
  59.5 6.5 %collective-permute-start.4 = (bf16[16,1792]{1,0:T(8,128)(2,1)S(1)}, bf16[16,1792]{1,0:T(8,128)(2,1)S(1)}, u32[]{:S(2)}, u32[]{:S(2)}) collective-permute-start(bf16[16,1792]{1,0:T(8,128)(2,1)S(1)} %slice.87), channel_id=1, source_target_pairs={{0,8},{1,9},{2,10},{3,11},{4,12},{5,13},{6,14},{7,15},{8,0},{9,1},... | collective-permute-start | bytes 172040 | tf_op jit(solution)/shard_map/ppermute | solution.py:396
  62.1 5.7 %collective-permute-start.7 = (bf16[16,1792]{1,0:T(8,128)(2,1)S(1)}, bf16[16,1792]{1,0:T(8,128)(2,1)S(1)}, u32[]{:S(2)}, u32[]{:S(2)}) collective-permute-start(bf16[16,1792]{1,0:T(8,128)(2,1)S(1)} %slice.86), channel_id=1, source_target_pairs={{0,8},{1,9},{2,10},{3,11},{4,12},{5,13},{6,14},{7,15},{8,0},{9,1},... | collective-permute-start | bytes 172040 | tf_op jit(solution)/shard_map/ppermute | solution.py:396
  68.5 0.7 copy-start

commit v2 on v1

--- a/solution.py
+++ b/solution.py
@@ -152,6 +152,7 @@
 
 
 BLOCK = 16
+SCOPED_BYTES = 16 * 2**20
 
 
 def as_column(row):
@@ -211,27 +212,43 @@
     return (position + (devices - 1) - source) // devices
 
 
-def kv_kernel(devices, per_owner, lengths_ref, assignment_ref, kv_ref, out_ref, tags_ref):
-    me = lax.axis_index("seq")
+def request_spans(lengths_ref, assignment_ref):
     requests = lengths_ref.shape[1]
-    here = kv_ref.shape[1]
-    slots = out_ref.shape[0]
-    room = slots // devices
     length_column = as_column(lengths_ref[...])
     assignment = assignment_ref[...]
     number = lax.broadcasted_iota(jnp.int32, (requests, requests), 0)
     before = jnp.sum(jnp.where(number < assignment, length_column, 0), axis=0, keepdims=True)
     own = jnp.sum(jnp.where(number == assignment, length_column, 0), axis=0, keepdims=True)
-    after = before + own
+    return before, before + own
+
+
+def apart_of(place, bits):
+    apart = place * 0
+    for i, bit in enumerate(bits):
+        digit = (place // (1 << (len(bits) - 1 - i))) % 2
+        apart = apart + digit * bit
+    return apart
+
+
+def kv_kernel(bits, per_owner, lengths_ref, assignment_ref, kv_ref, out_ref):
+    me = lax.axis_index("seq")
+    devices = 1 << len(bits)
+    requests = lengths_ref.shape[1]
+    here = kv_ref.shape[1]
+    slots = out_ref.shape[0]
+    room = slots // devices
+    before, after = request_spans(lengths_ref, assignment_ref)
     low = ceil_rows(before, me, devices)
     count = ceil_rows(after, me, devices) - low
+    number = lax.broadcasted_iota(jnp.int32, (requests, requests), 0)
     line = lax.broadcasted_iota(jnp.int32, (requests, requests), 1)
     same = (number // per_owner == line // per_owner) & (number < line)
     offset = jnp.sum(jnp.where(same, as_column(count), 0), axis=0, keepdims=True)
     slot = lax.broadcasted_iota(jnp.int32, (slots, requests), 0)
     decode = lax.broadcasted_iota(jnp.int32, (slots, requests), 1)
+    owner = me ^ apart_of(slot // room, bits)
     rank = slot % room - offset
-    held = (slot // room == decode // per_owner) & (rank >= 0) & (rank < count)
+    held = (owner == decode // per_owner) & (rank >= 0) & (rank < count)
     source = jnp.sum(jnp.where(held, low + rank + 1, 0), axis=1, keepdims=True) - 1
     pick = source == lax.broadcasted_iota(jnp.int32, (slots, here), 1)
     out_ref[...] = lax.dot_general(
@@ -240,8 +257,32 @@
         (((1,), (1,)), ((), ())),
         preferred_element_type=jnp.float32,
     ).astype(jnp.bfloat16)
+
+
+def pack_kv(prefill_kv, lengths, assignment, bits, per_owner, room):
+    here, width = prefill_kv.shape
+    slots = room << len(bits)
+    return pl.pallas_call(
+        functools.partial(kv_kernel, bits, per_owner),
+        out_shape=jax.ShapeDtypeStruct((slots, width), jnp.bfloat16),
+        compiler_params=pltpu.CompilerParams(vmem_limit_bytes=SCOPED_BYTES),
+        cost_estimate=pl.CostEstimate(
+            flops=2 * slots * here * width,
+            bytes_accessed=20 * 2**20,
+            transcendentals=0,
+        ),
+        name="pack_kv",
+    )(lengths.reshape(1, -1), assignment.reshape(1, -1), prefill_kv.T)
+
+
+def tags_kernel(devices, per_owner, lengths_ref, assignment_ref, tags_ref):
+    me = lax.axis_index("seq")
+    requests = lengths_ref.shape[1]
+    slots = tags_ref.shape[1]
+    room = slots // devices
+    before, after = request_spans(lengths_ref, assignment_ref)
     place = lax.broadcasted_iota(jnp.int32, (1, slots), 1)
-    sender, rank = place // room, place % room
+    sender, rank = me ^ (place // room), place % room
     tags = jnp.full((1, slots), -1, jnp.int32)
     decode = lax.broadcasted_iota(jnp.int32, (1, requests), 1)
     taken = jnp.zeros((1, slots), jnp.int32)
@@ -255,22 +296,14 @@
     tags_ref[...] = tags
 
 
-def pack_kv(prefill_kv, lengths, assignment, devices, per_owner, room):
-    here, width = prefill_kv.shape
-    slots = devices * room
+def slot_tags(lengths, assignment, devices, per_owner, slots):
     return pl.pallas_call(
-        functools.partial(kv_kernel, devices, per_owner),
-        out_shape=(
-            jax.ShapeDtypeStruct((slots, width), jnp.bfloat16),
-            jax.ShapeDtypeStruct((1, slots), jnp.int32),
-        ),
-        cost_estimate=pl.CostEstimate(
-            flops=2 * slots * here * width,
-            bytes_accessed=2 * width * (here + slots),
-            transcendentals=0,
-        ),
-        name="pack_kv",
-    )(lengths.reshape(1, -1), assignment.reshape(1, -1), prefill_kv.T)
+        functools.partial(tags_kernel, devices, per_owner),
+        out_shape=jax.ShapeDtypeStruct((1, slots), jnp.int32),
+        compiler_params=pltpu.CompilerParams(vmem_limit_bytes=SCOPED_BYTES),
+        cost_estimate=pl.CostEstimate(flops=0, bytes_accessed=8192, transcendentals=0),
+        name="slot_tags",
+    )(lengths.reshape(1, -1), assignment.reshape(1, -1))
 
 
 def attend_kernel(queries_ref, fresh_ref, cache_ref, tags_ref, out_ref):
@@ -331,6 +364,7 @@
         ],
         out_specs=pl.BlockSpec((steps, 1, heads, latent), lambda q: (0, q, 0, 0)),
         out_shape=jax.ShapeDtypeStruct((steps, per_owner, heads, latent), jnp.bfloat16),
+        compiler_params=pltpu.CompilerParams(vmem_limit_bytes=SCOPED_BYTES),
         cost_estimate=pl.CostEstimate(
             flops=2 * steps * per_owner * heads * slots * (width + latent),
             bytes_accessed=2 * steps * per_owner * heads * (width + latent),
@@ -340,56 +374,92 @@
     )(queries, new_kv, kv_cache, tags)
 
 
-def expert_kernel(bits, arrived_ref, down_ref, keep_ref, send_ref, sorted_ref):
+def sort_blocks(bits, arrived_ref, sorted_ref):
     me = lax.axis_index("seq")
-    blocks = 1 << len(bits)
+    for place in range(1 << len(bits)):
+        start = pl.multiple_of((me ^ apart_of(place, bits)) * BLOCK, BLOCK)
+        sorted_ref[place * BLOCK : (place + 1) * BLOCK, :] = arrived_ref[pl.ds(start, BLOCK), :]
+
+
+def first_half_kernel(
+    bits, pieces, arrived_ref, down_ref, keep_ref, send_ref, rest_ref, sorted_ref, own_ref, sems
+):
+    half, width = keep_ref.shape
+    piece = width // pieces
+    copies = []
+    for i in range(pieces):
+        columns = slice(i * piece, (i + 1) * piece)
+        copies.append(
+            pltpu.make_async_copy(down_ref.at[0, :, columns], own_ref.at[:, columns], sems.at[i])
+        )
+    copies.append(pltpu.make_async_copy(down_ref.at[0, :, width:], rest_ref, sems.at[pieces]))
+    for copy in copies:
+        copy.start()
+    sort_blocks(bits, arrived_ref, sorted_ref)
+    for i in range(pieces):
+        columns = slice(i * piece, (i + 1) * piece)
+        copies[i].wait()
+        result = jnp.dot(
+            sorted_ref[...], own_ref[:, columns], preferred_element_type=jnp.float32
+        )
+        keep_ref[:, columns] = result[:half]
+        send_ref[:, columns] = result[half:].astype(jnp.bfloat16)
+    copies[pieces].wait()
+
+
+def second_half_kernel(bits, arrived_ref, rest_ref, keep_ref, send_ref, sorted_ref):
     half = keep_ref.shape[0]
-
-    @pl.when(pl.program_id(0) == 0)
-    def _():
-        for place in range(blocks):
-            apart = 0
-            for i, bit in enumerate(bits):
-                if place >> (len(bits) - 1 - i) & 1:
-                    apart |= bit
-            start = pl.multiple_of((me ^ apart) * BLOCK, BLOCK)
-            sorted_ref[place * BLOCK : (place + 1) * BLOCK, :] = arrived_ref[
-                pl.ds(start, BLOCK), :
-            ]
-
-    result = jnp.dot(sorted_ref[...], down_ref[0], preferred_element_type=jnp.float32)
+    sort_blocks(bits, arrived_ref, sorted_ref)
+    result = jnp.dot(sorted_ref[...], rest_ref[...], preferred_element_type=jnp.float32)
     keep_ref[...] = result[:half]
     send_ref[...] = result[half:].astype(jnp.bfloat16)
 
 
-def expert_part(arrived, expert_down, bits, part, parts, tile):
+def expert_halves(arrived, expert_down, orders):
     slots, hidden_width = arrived.shape
-    width = expert_down.shape[2] // parts
+    width = expert_down.shape[2] // 2
     half = slots // 2
-    tiles = width // tile
-    return pl.pallas_call(
-        functools.partial(expert_kernel, bits),
-        grid=(tiles,),
-        in_specs=[
-            pl.BlockSpec((slots, hidden_width), lambda i: (0, 0)),
-            pl.BlockSpec((1, hidden_width, tile), lambda i: (0, 0, i + part * tiles)),
+    pieces = 2
+    vmem = pl.BlockSpec(memory_space=pltpu.VMEM)
+    shapes = (
+        jax.ShapeDtypeStruct((half, width), jnp.float32),
+        jax.ShapeDtypeStruct((half, width), jnp.bfloat16),
+    )
+    params = pltpu.CompilerParams(vmem_limit_bytes=SCOPED_BYTES)
+    cost = pl.CostEstimate(
+        flops=2 * slots * hidden_width * width,
+        bytes_accessed=2 * hidden_width * width,
+        transcendentals=0,
+    )
+    down = pltpu.with_memory_space_constraint(expert_down, pltpu.HBM)
+    kept_first, sent_first, rest = pl.pallas_call(
+        functools.partial(first_half_kernel, orders[0], pieces),
+        in_specs=[vmem, pl.BlockSpec(memory_space=pltpu.HBM)],
+        out_specs=[vmem] * 3,
+        out_shape=shapes + (pltpu.VMEM((hidden_width, width), jnp.bfloat16),),
+        scratch_shapes=[
+            pltpu.VMEM((slots, hidden_width), jnp.bfloat16),
+            pltpu.VMEM((hidden_width, width), jnp.bfloat16),
+            pltpu.SemaphoreType.DMA((pieces + 1,)),
         ],
-        out_specs=[
-            pl.BlockSpec((half, tile), lambda i: (0, i)),
-            pl.BlockSpec((half, tile), lambda i: (0, i)),
-        ],
-        out_shape=(
-            jax.ShapeDtypeStruct((half, width), jnp.float32),
-            jax.ShapeDtypeStruct((half, width), jnp.bfloat16),
-        ),
+        compiler_params=params,
+        cost_estimate=cost,
+        name="expert_first",
+    )(arrived, down)
+    kept_second, sent_second = pl.pallas_call(
+        functools.partial(second_half_kernel, orders[1]),
+        in_specs=[vmem] * 2,
+        out_specs=[vmem] * 2,
+        out_shape=shapes,
         scratch_shapes=[pltpu.VMEM((slots, hidden_width), jnp.bfloat16)],
-        cost_estimate=pl.CostEstimate(
-            flops=2 * slots * hidden_width * width,
-            bytes_accessed=2 * hidden_width * width + 6 * half * width,
-            transcendentals=0,
-        ),
-        name="expert_part",
-    )(arrived, expert_down)
+        compiler_params=params,
+        cost_estimate=cost,
+        name="expert_second",
+    )(arrived, rest)
+    return (kept_first, sent_first), (kept_second, sent_second)
+
+
+after = lax.optimization_barrier
 
 
 def swap(values, bit, devices):
@@ -421,34 +491,44 @@
     arrived = lax.all_to_all(
         outbox.reshape(devices, BLOCK, hidden_width), "seq", split_axis=0, concat_axis=0, tiled=True
     ).reshape(devices * BLOCK, hidden_width)
-    kv_outbox, tags = pack_kv(
-        prefill_kv, lengths, assignment, devices, per_owner, 2 * HALF * per_owner
-    )
+
+    room = 2 * HALF * per_owner
+    kv_bits = (1, 2, 4, 8)
+    held = pack_kv(prefill_kv, lengths, assignment, kv_bits, per_owner, room)
+    tags = slot_tags(lengths, assignment, devices, per_owner, devices * room)
+    held = held.reshape(1, held.shape[0], held.shape[1])
+
+    def split(held):
+        half = held.shape[1] // 2
+        return held[:, :half], held[:, half:]
+
+    for bit in kv_bits[:2]:
+        kept, sent = split(held)
+        held = jnp.concatenate([kept, swap(sent, bit, devices)], axis=0)
+    kv_kept, kv_sent = split(held)
+    kv_got = swap(kv_sent, kv_bits[2], devices)
+    arrived, _, _ = after((arrived, kv_sent, tags))
 
     orders = ((1, 2, 4, 8), (1, 4, 2, 8))
-    parts = len(orders)
     flows = []
-    for part, bits in enumerate(orders):
-        kept, sent = expert_part(arrived, expert_down, bits, part, parts, 256)
-        flows.append((kept, sent, swap(sent, bits[0], devices)))
-    flows = [fold(kept, received) for kept, _, received in flows]
+    for (kept, sent), bits in zip(expert_halves(arrived, expert_down, orders), orders):
+        flows.append((kept, swap(sent, bits[0], devices)))
+    flows = [fold(kept, received) for kept, received in flows]
     received = [swap(sent, bits[1], devices) for (_, sent), bits in zip(flows, orders)]
 
-    kv_outbox, _ = lax.optimization_barrier((kv_outbox, [sent for _, sent in flows]))
-    kv_cache = lax.all_to_all(
-        kv_outbox.reshape(devices, -1, kv_outbox.shape[1]),
-        "seq",
-        split_axis=0,
-        concat_axis=0,
-        tiled=True,
-    ).reshape(kv_outbox.shape)
-    context = attend(queries, new_kv, kv_cache, tags)
-
-    for level in (2, 3):
-        flows = [fold(kept, got) for (kept, _), got in zip(flows, received)]
-        received = [swap(sent, bits[level], devices) for (_, sent), bits in zip(flows, orders)]
-    final = [kept + got.astype(jnp.float32) for (kept, _), got in zip(flows, received)]
-    moe_out = jnp.concatenate(final, axis=1).astype(jnp.bfloat16)
+    kv_got, _ = after((kv_got, [sent for _, sent in flows]))
+    kv_kept, kv_sent = split(jnp.concatenate([kv_kept, kv_got], axis=0))
+    held = jnp.concatenate([kv_kept, swap(kv_sent, kv_bits[3], devices)], axis=0)
+    context = attend(queries, new_kv, held.reshape(devices * room, -1), tags)
+
+    flows = [fold(kept, got) for (kept, _), got in zip(flows, received)]
+    received = [swap(sent, bits[2], devices) for (_, sent), bits in zip(flows, orders)]
+    flows = [fold(kept, got) for (kept, _), got in zip(flows, received)]
+    kept = jnp.concatenate([kept for kept, _ in flows], axis=1)
+    sent = jnp.concatenate([sent for _, sent in flows], axis=1)
+    received = swap(sent, orders[0][-1], devices)
+    received, context = lax.optimization_barrier((received, context))
+    moe_out = (kept + received.astype(jnp.float32)).astype(jnp.bfloat16)
     return context, moe_out.reshape(rows, steps, model_width)
 
 

time: 75.7 us -> 57 us (0.75)
  blocking collectives: 22 us -> 0 us
  Pallas kernels: 23.2 us -> 12 us
  waiting for transfers between devices: 13.7 us -> 23.1 us
  starting transfers between devices: 12.3 us -> 17.1 us
  local copies, waits for them, and re-layouts: 0.86 us -> 3.08 us
  other arithmetic: 2.18 us -> 0.48 us
    all_to_all x1 -> x0, blocking collectives: 22 us -> none  [per_device_dense(): lax.all_to_all(outbox.reshape(devices, BLOCK, hidden_width), 'seq', split...]
    pallas_call x3 -> x4, Pallas kernels: 15.3 us -> 5.17 us  [the longest x1 3.2 us: expert_halves(): pl.pallas_call(functools.partial(first_half_kernel, orders[0], pieces), i...]
    ppermute x8 -> x11, waiting for transfers between devices: 13.7 us -> 20.9 us  [swap(): return lax.ppermute(values, 'seq', [(i, i ^ bit) for i in range(devices)])]
    all_to_all x1, starting transfers between devices: 3.54 us -> 7.38 us  [per_device_dense(): lax.all_to_all(outbox.reshape(devices, BLOCK, hidden_width), 'seq', split...]
    all_to_all x1, waiting for transfers between devices: 0.01 us -> 2.2 us  [per_device_dense(): lax.all_to_all(outbox.reshape(devices, BLOCK, hidden_width), 'seq', split...]
    unnamed x4 -> x10, local copies, waits for them, and re-layouts: 0.73 us -> 2.23 us
    add x6, other arithmetic: 1.46 us -> 0.3 us  [fold(): total = kept + received.astype(jnp.float32)]
    pallas_call x1, Pallas kernels: 5.73 us -> 4.67 us  [attend(): pl.pallas_call(attend_kernel, grid=(per_owner,), in_specs=[pl.BlockSpec((...]
  transfers between devices with their start and end apart: 9 -> 12, of which waited for: 5 -> 10; matrix products, arithmetic and copies ran while one was open for 3% -> 1% of each run, Pallas kernels for 12% -> 12%
where the time goes in v2:
time: 57 us; the launch traced here: 56.7 us
  waiting for transfers between devices  23.1 us (41%)
  starting transfers between devices  17.1 us (30%)
  Pallas kernels  12 us (21%)
  local copies, waits for them, and re-layouts  3.08 us (5%)
  between operations  0.88 us (2%)
    ppermute x11, waiting for transfers between devices, swap(): return lax.ppermute(values, 'seq', [(i, i ^ bit) for i in range(devices)])  20.9 us
    ppermute x11, starting transfers between devices, swap(): return lax.ppermute(values, 'seq', [(i, i ^ bit) for i in range(devices)])  9.71 us
    all_to_all x1, starting transfers between devices, per_device_dense(): lax.all_to_all(outbox.reshape(devices, BLOCK, hidden_width), 'seq', split...  7.38 us
    pallas_call x1, Pallas kernels, attend(): pl.pallas_call(attend_kernel, grid=(per_owner,), in_specs=[pl.BlockSpec((...  4.67 us
    pallas_call x1, Pallas kernels, expert_halves(): pl.pallas_call(functools.partial(first_half_kernel, orders[0], pieces), i...  3.2 us
    unnamed x10, local copies, waits for them, and re-layouts  2.23 us
    all_to_all x1, waiting for transfers between devices, per_device_dense(): lax.all_to_all(outbox.reshape(devices, BLOCK, hidden_width), 'seq', split...  2.2 us
    pallas_call x1, Pallas kernels, pack_hidden(): pl.pallas_call(outbox_kernel, out_shape=jax.ShapeDtypeStruct((experts * t...  2.2 us
  transfers between devices with their start and end apart: 12, of which 10 were waited for; matrix products, arithmetic and copies ran while one was open for 1% of the time, Pallas kernels for 12%

profile of v2, /device:TPU:0, one launch (start us, length us, event | category | flops | bytes accessed | tf_op | source)
XLA Modules:
  0.0 56.7 jit_solution(3611048319080270532)
XLA Ops:
  0.6 2.2 %pack_hidden.1 = bf16[256,1024]{1,0:T(8,128)(2,1)} custom-call(s32[4,4,8]{2,1,0:T(4,128)} %routes_ref.1, f32[4,4,8]{2,1,0:T(4,128)} %weights_ref.1, bf16[128,1024]{1,0:T(8,128)(2,1)} %bitcast.18), custom_call_target="tpu_custom_call" | custom-call | flops 67108864 | bytes 786432 | tf_op jit(solution)/shard_map/pack_hidden/pallas_call | solution.py:199
  2.8 7.4 %all-to-all-start = ((bf16[16,16,1024]{2,1,0:T(8,128)(2,1)}), bf16[16,16,1024]{2,1,0:T(8,128)(2,1)S(1)}, u32[]{:S(2)}, u32[]{:S(2)}) async-start(bf16[16,16,1024]{2,1,0:T(8,128)(2,1)} %bitcast.17), calls=%async_computation | async-start | bytes 1048576 | tf_op jit(solution)/shard_map/all_to_all | solution.py:491
  10.2 0.0 copy-start.1
  10.2 0.9 %copy-done.1 = bf16[128,576]{0,1:T(8,128)(2,1)S(1)} copy-done((bf16[128,576]{0,1:T(8,128)(2,1)S(1)}, bf16[128,576]{0,1:T(8,128)(2,1)}, u32[]{:S(2)}) %copy-start.1) | copy-done | bytes 147480
  11.1 0.0 copy-start.3
  11.1 0.7 %copy-done.3 = s32[64]{0:T(128)S(1)} copy-done((s32[64]{0:T(128)S(1)}, s32[64]{0:T(128)}, u32[]{:S(2)}) %copy-start.3) | copy-done | bytes 280
  11.8 0.0 copy-start.4
  11.8 0.7 %copy-done.4 = s32[64]{0:T(128)S(1)} copy-done((s32[64]{0:T(128)S(1)}, s32[64]{0:T(128)}, u32[]{:S(2)}) %copy-start.4) | copy-done | bytes 280
  12.5 0.6 %pack_kv.1 = bf16[256,576]{1,0:T(8,128)(2,1)S(1)} custom-call(s32[1,64]{1,0:T(1,128)S(1)} %bitcast.13, s32[1,64]{1,0:T(1,128)S(1)} %bitcast.15, bf16[576,128]{1,0:T(8,128)(2,1)S(1)} %bitcast.12), custom_call_target="tpu_custom_call" | custom-call | flops 37748736 | bytes 20971520 | tf_op jit(solution)/shard_map/pack_kv/pallas_call | solution.py:265
  13.1 0.5 collective-permute-start
  13.6 1.0 %collective-permute-done = bf16[1,128,576]{2,1,0:T(8,128)(2,1)S(1)} collective-permute-done((bf16[1,128,576]{2,1,0:T(8,128)(2,1)S(1)}, bf16[1,128,576]{2,1,0:T(8,128)(2,1)S(1)}, u32[]{:S(2)}, u32[]{:S(2)}) %collective-permute-start) | collective-permute-done | bytes 147488 | tf_op jit(solution)/shard_map/ppermute | solution.py:466
  14.6 1.9 %collective-permute-start.1 = (bf16[2,64,576]{2,1,0:T(8,128)(2,1)S(1)}, bf16[2,64,576]{2,1,0:T(8,128)(2,1)S(1)}, u32[]{:S(2)}, u32[]{:S(2)}) collective-permute-start(bf16[2,64,576]{2,1,0:T(8,128)(2,1)S(1)} %get-tuple-element.22), channel_id=1, source_target_pairs={{0,2},{1,3},{2,0},{3,1},{4,6},{5,7},{6,4},{7,5},{8,10},{9,11},{10,... | collective-permute-start | bytes 442376 | tf_op jit(solution)/shard_map/ppermute | solution.py:466
  16.6 0.2 slot_tags.1.tags_ref
  16.8 5.6 %collective-permute-done.1 = bf16[2,64,576]{2,1,0:T(8,128)(2,1)S(1)} collective-permute-done((bf16[2,64,576]{2,1,0:T(8,128)(2,1)S(1)}, bf16[2,64,576]{2,1,0:T(8,128)(2,1)S(1)}, u32[]{:S(2)}, u32[]{:S(2)}) %collective-permute-start.1) | collective-permute-done | bytes 147488 | tf_op jit(solution)/shard_map/ppermute | solution.py:466
  22.5 2.2 %all-to-all-done = bf16[16,16,1024]{2,1,0:T(8,128)(2,1)S(1)} async-done(((bf16[16,16,1024]{2,1,0:T(8,128)(2,1)}), bf16[16,16,1024]{2,1,0:T(8,128)(2,1)S(1)}, u32[]{:S(2)}, u32[]{:S(2)}) %all-to-all-start) | async-done | bytes 524320 | tf_op jit(solution)/shard_map/all_to_all | solution.py:491
  24.7 3.2 %expert_first.1 = (f32[128,1792]{1,0:T(8,128)S(1)}, bf16[128,1792]{1,0:T(8,128)(2,1)S(1)}, bf16[1024,1792]{1,0:T(8,128)(2,1)S(1)}) custom-call(bf16[256,1024]{1,0:T(8,128)(2,1)S(1)} %bitcast.8, bf16[1,1024,3584]{2,1,0:T(8,128)(2,1)} %down_ref.1), custom_call_target="tpu_custom_call" | custom-call | flops 939524096 | bytes 3670016 | tf_op jit(solution)/shard_map/expert_first/pallas_call | solution.py:435
  27.9 0.1 collective-permute-start.2
  28.0 1.7 %collective-permute-start.9 = (bf16[4,32,576]{2,1,0:T(8,128)(2,1)S(1)}, bf16[4,32,576]{2,1,0:T(8,128)(2,1)S(1)}, u32[]{:S(2)}, u32[]{:S(2)}) collective-permute-start(bf16[4,32,576]{2,1,0:T(8,128)(2,1)S(1)} %fusion.2), channel_id=1, source_target_pairs={{0,4},{1,5},{2,6},{3,7},{4,0},{5,1},{6,2},{7,3},{8,12},{9,13},{10,... | collective-permute-start | bytes 442376 | tf_op jit(solution)/shard_map/ppermute | solution.py:466
  29.7 1.1 %expert_second.1 = (f32[128,1792]{1,0:T(8,128)S(1)}, bf16[128,1792]{1,0:T(8,128)(2,1)S(1)}) custom-call(bf16[256,1024]{1,0:T(8,128)(2,1)S(1)} %bitcast.9, bf16[1024,1792]{1,0:T(8,128)(2,1)S(1)} %get-tuple-element.14.rest_ref), custom_call_target="tpu_custom_call" | custom-call | flops 939524096 | bytes 3670016 | tf_op jit(solution)/shard_map/expert_second/pallas_call | solution.py:449
  30.8 0.1 collective-permute-start.5
  30.9 0.0 collective-permute-done.2
  30.9 0.1 convert_add_fusion.1
  31.1 1.0 %collective-permute-start.3 = (bf16[64,1792]{1,0:T(8,128)(2,1)S(1)}, bf16[64,1792]{1,0:T(8,128)(2,1)S(1)}, u32[]{:S(2)}, u32[]{:S(2)}) collective-permute-start(bf16[64,1792]{1,0:T(8,128)(2,1)S(1)} %slice.129), channel_id=1, source_target_pairs={{0,2},{1,3},{2,0},{3,1},{4,6},{5,7},{6,4},{7,5},{8,10},{9,11},{10,... | collective-permute-start | bytes 688136 | tf_op jit(solution)/shard_map/ppermute | solution.py:466
  32.0 0.7 %collective-permute-done.5 = bf16[128,1792]{1,0:T(8,128)(2,1)S(1)} collective-permute-done((bf16[128,1792]{1,0:T(8,128)(2,1)S(1)}, bf16[128,1792]{1,0:T(8,128)(2,1)S(1)}, u32[]{:S(2)}, u32[]{:S(2)}) %collective-permute-start.5) | collective-permute-done | bytes 458784 | tf_op jit(solution)/shard_map/ppermute | solution.py:466
  32.7 0.1 convert_add_fusion
  32.8 0.0 copy-start
  32.8 0.0 copy-start.2
  32.9 0.4 collective-permute-start.6
  33.3 1.3 %collective-permute-done.9 = bf16[4,32,576]{2,1,0:T(8,128)(2,1)S(1)} collective-permute-done((bf16[4,32,576]{2,1,0:T(8,128)(2,1)S(1)}, bf16[4,32,576]{2,1,0:T(8,128)(2,1)S(1)}, u32[]{:S(2)}, u32[]{:S(2)}) %collective-permute-start.9) | collective-permute-done | bytes 147488 | tf_op jit(solution)/shard_map/ppermute | solution.py:466
  34.7 2.5 %collective-permute-start.10 = (bf16[8,16,576]{2,1,0:T(8,128)(2,1)S(1)}, bf16[8,16,576]{2,1,0:T(8,128)(2,1)S(1)}, u32[]{:S(2)}, u32[]{:S(2)}) collective-permute-start(bf16[8,16,576]{2,1,0:T(8,128)(2,1)S(1)} %get-tuple-element.21), channel_id=1, source_target_pairs={{0,8},{1,9},{2,10},{3,11},{4,12},{5,13},{6,14},{7,15},{8,0},{9,1},... | collective-permute-start | bytes 442376 | tf_op jit(solution)/shard_map/ppermute | solution.py:466
  37.2 1.9 %collective-permute-done.3 = bf16[64,1792]{1,0:T(8,128)(2,1)S(1)} collective-permute-done((bf16[64,1792]{1,0:T(8,128)(2,1)S(1)}, bf16[64,1792]{1,0:T(8,128)(2,1)S(1)}, u32[]{:S(2)}, u32[]{:S(2)}) %collective-permute-start.3) | collective-permute-done | bytes 229408 | tf_op jit(solution)/shard_map/ppermute | solution.py:466
  39.1 0.1 slice_add_fusion.1
  39.2 0.4 collective-permute-start.4
  39.6 5.3 %collective-permute-done.6 = bf16[64,1792]{1,0:T(8,128)(2,1)S(1)} collective-permute-done((bf16[64,1792]{1,0:T(8,128)(2,1)S(1)}, bf16[64,1792]{1,0:T(8,128)(2,1)S(1)}, u32[]{:S(2)}, u32[]{:S(2)}) %collective-permute-start.6) | collective-permute-done | bytes 229408 | tf_op jit(solution)/shard_map/ppermute | solution.py:466
  44.9 0.1 slice_add_fusion
  45.0 1.0 %collective-permute-start.7 = (bf16[32,1792]{1,0:T(8,128)(2,1)S(1)}, bf16[32,1792]{1,0:T(8,128)(2,1)S(1)}, u32[]{:S(2)}, u32[]{:S(2)}) collective-permute-start(bf16[32,1792]{1,0:T(8,128)(2,1)S(1)} %slice.130), channel_id=1, source_target_pairs={{0,2},{1,3},{2,0},{3,1},{4,6},{5,7},{6,4},{7,5},{8,10},{9,11},{10,... | collective-permute-start | bytes 344072 | tf_op jit(solution)/shard_map/ppermute | solution.py:466
  45.9 0.6 %collective-permute-done.4 = bf16[32,1792]{1,0:T(8,128)(2,1)S(1)} collective-permute-done((bf16[32,1792]{1,0:T(8,128)(2,1)S(1)}, bf16[32,1792]{1,0:T(8,128)(2,1)S(1)}, u32[]{:S(2)}, u32[]{:S(2)}) %collective-permute-start.4) | collective-permute-done | bytes 114720 | tf_op jit(solution)/shard_map/ppermute | solution.py:466
  46.6 3.2 %collective-permute-done.7 = bf16[32,1792]{1,0:T(8,128)(2,1)S(1)} collective-permute-done((bf16[32,1792]{1,0:T(8,128)(2,1)S(1)}, bf16[32,1792]{1,0:T(8,128)(2,1)S(1)}, u32[]{:S(2)}, u32[]{:S(2)}) %collective-permute-start.7) | collective-permute-done | bytes 114720 | tf_op jit(solution)/shard_map/ppermute | solution.py:466
  49.9 0.1 collective-permute-start.8
  50.0 0.0 collective-permute-done.10
  50.0 0.1 pad_maximum_fusion.1
  50.0 0.0 copy-done
  50.0 0.0 copy-done.2
  50.1 4.7 %attend.1 = bf16[4,4,64,512]{3,2,1,0:T(8,128)(2,1)} custom-call(bf16[4,4,64,576]{3,2,1,0:T(8,128)(2,1)S(1)} %copy-done, bf16[4,4,576]{2,1,0:T(4,128)(2,1)S(1)} %copy-done.2, bf16[256,576]{1,0:T(8,128)(2,1)S(1)} %bitcast.10, s32[1,256]{1,0:T(1,128)S(1)} %slot_tags.1.tags_ref), custom_call_target="tpu_custom_call" | custom-call | flops 570425344 | bytes 2228224 | tf_op jit(solution)/shard_map/attend/pallas_call | solution.py:356
  54.8 1.2 %collective-permute-done.8 = bf16[16,3584]{1,0:T(8,128)(2,1)S(1)} collective-permute-done((bf16[16,3584]{1,0:T(8,128)(2,1)S(1)}, bf16[16,3584]{1,0:T(8,128)(2,1)S(1)}, u32[]{:S(2)}, u32[]{:S(2)}) %collective-permute-start.8) | collective-permute-done | bytes 114720 | tf_op jit(solution)/shard_map/ppermute | solution.py:466
  56.0 0.7 %reshape.37 = bf16[4,4,3584]{2,1,0:T(4,128)(2,1)} reshape(bf16[16,3584]{1,0:T(8,128)(2,1)S(1)} %fusion.1) | data formatting | bytes 229376 | tf_op jit(solution)/shard_map/reshape | solution.py:532
  (17 shorter events, 0.3 us)
Async XLA Ops:
  2.8 21.9 %all-to-all-start = ((bf16[16,16,1024]{2,1,0:T(8,128)(2,1)}), bf16[16,16,1024]{2,1,0:T(8,128)(2,1)S(1)}, u32[]{:S(2)}, u32[]{:S(2)}) async-start(bf16[16,16,1024]{2,1,0:T(8,128)(2,1)} %bitcast.17), calls=%async_computation | async-start | bytes 1048576 | tf_op jit(solution)/shard_map/all_to_all | solution.py:491
  10.2 0.9 %copy-start.1 = (bf16[128,576]{0,1:T(8,128)(2,1)S(1)}, bf16[128,576]{0,1:T(8,128)(2,1)}, u32[]{:S(2)}) copy-start(bf16[128,576]{0,1:T(8,128)(2,1)} %param.9) | copy-start | bytes 442372
  11.1 0.7 %copy-start.3 = (s32[64]{0:T(128)S(1)}, s32[64]{0:T(128)}, u32[]{:S(2)}) copy-start(s32[64]{0:T(128)} %param.10) | copy-start | bytes 772
  11.8 0.7 %copy-start.4 = (s32[64]{0:T(128)S(1)}, s32[64]{0:T(128)}, u32[]{:S(2)}) copy-start(s32[64]{0:T(128)} %param.11) | copy-start | bytes 772
  13.1 1.5 %collective-permute-start = (bf16[1,128,576]{2,1,0:T(8,128)(2,1)S(1)}, bf16[1,128,576]{2,1,0:T(8,128)(2,1)S(1)}, u32[]{:S(2)}, u32[]{:S(2)}) collective-permute-start(bf16[1,128,576]{2,1,0:T(8,128)(2,1)S(1)} %get-tuple-element.24), channel_id=1, source_target_pairs={{0,1},{1,0},{2,3},{3,2},{4,5},{5,4},{6,7},{7,6},{8,9},{9,8},{10,11... | collective-permute-start | bytes 442376 | tf_op jit(solution)/shard_map/ppermute | solution.py:466
  14.6 7.8 %collective-permute-start.1 = (bf16[2,64,576]{2,1,0:T(8,128)(2,1)S(1)}, bf16[2,64,576]{2,1,0:T(8,128)(2,1)S(1)}, u32[]{:S(2)}, u32[]{:S(2)}) collective-permute-start(bf16[2,64,576]{2,1,0:T(8,128)(2,1)S(1)} %get-tuple-element.22), channel_id=1, source_target_pairs={{0,2},{1,3},{2,0},{3,1},{4,6},{5,7},{6,4},{7,5},{8,10},{9,11},{10,... | collective-permute-start | bytes 442376 | tf_op jit(solution)/shard_map/ppermute | solution.py:466
  27.9 3.0 %collective-permute-start.2 = (bf16[128,1792]{1,0:T(8,128)(2,1)S(1)}, bf16[128,1792]{1,0:T(8,128)(2,1)S(1)}, u32[]{:S(2)}, u32[]{:S(2)}) collective-permute-start(bf16[128,1792]{1,0:T(8,128)(2,1)S(1)} %get-tuple-element.13), channel_id=1, source_target_pairs={{0,1},{1,0},{2,3},{3,2},{4,5},{5,4},{6,7},{7,6},{8,9},{9,8},{10,11... | collective-permute-start | bytes 1376264 | tf_op jit(solution)/shard_map/ppermute | solution.py:466
  28.0 6.6 %collective-permute-start.9 = (bf16[4,32,576]{2,1,0:T(8,128)(2,1)S(1)}, bf16[4,32,576]{2,1,0:T(8,128)(2,1)S(1)}, u32[]{:S(2)}, u32[]{:S(2)}) collective-permute-start(bf16[4,32,576]{2,1,0:T(8,128)(2,1)S(1)} %fusion.2), channel_id=1, source_target_pairs={{0,4},{1,5},{2,6},{3,7},{4,0},{5,1},{6,2},{7,3},{8,12},{9,13},{10,... | collective-permute-start | bytes 442376 | tf_op jit(solution)/shard_map/ppermute | solution.py:466
  30.8 1.9 %collective-permute-start.5 = (bf16[128,1792]{1,0:T(8,128)(2,1)S(1)}, bf16[128,1792]{1,0:T(8,128)(2,1)S(1)}, u32[]{:S(2)}, u32[]{:S(2)}) collective-permute-start(bf16[128,1792]{1,0:T(8,128)(2,1)S(1)} %get-tuple-element.16), channel_id=1, source_target_pairs={{0,1},{1,0},{2,3},{3,2},{4,5},{5,4},{6,7},{7,6},{8,9},{9,8},{10,11... | collective-permute-start | bytes 1376264 | tf_op jit(solution)/shard_map/ppermute | solution.py:466
  31.1 8.1 %collective-permute-start.3 = (bf16[64,1792]{1,0:T(8,128)(2,1)S(1)}, bf16[64,1792]{1,0:T(8,128)(2,1)S(1)}, u32[]{:S(2)}, u32[]{:S(2)}) collective-permute-start(bf16[64,1792]{1,0:T(8,128)(2,1)S(1)} %slice.129), channel_id=1, source_target_pairs={{0,2},{1,3},{2,0},{3,1},{4,6},{5,7},{6,4},{7,5},{8,10},{9,11},{10,... | collective-permute-start | bytes 688136 | tf_op jit(solution)/shard_map/ppermute | solution.py:466
  32.8 17.2 %copy-start = (bf16[4,4,64,576]{3,2,1,0:T(8,128)(2,1)S(1)}, bf16[4,4,64,576]{3,2,1,0:T(8,128)(2,1)}, u32[]{:S(2)}) copy-start(bf16[4,4,64,576]{3,2,1,0:T(8,128)(2,1)} %queries_ref.1) | copy-start | bytes 3538948
  32.8 17.2 %copy-start.2 = (bf16[4,4,576]{2,1,0:T(4,128)(2,1)S(1)}, bf16[4,4,576]{2,1,0:T(4,128)(2,1)}, u32[]{:S(2)}) copy-start(bf16[4,4,576]{2,1,0:T(4,128)(2,1)} %fresh_ref.1) | copy-start | bytes 55300
  32.9 12.0 %collective-permute-start.6 = (bf16[64,1792]{1,0:T(8,128)(2,1)S(1)}, bf16[64,1792]{1,0:T(8,128)(2,1)S(1)}, u32[]{:S(2)}, u32[]{:S(2)}) collective-permute-start(bf16[64,1792]{1,0:T(8,128)(2,1)S(1)} %slice.128), channel_id=1, source_target_pairs={{0,4},{1,5},{2,6},{3,7},{4,0},{5,1},{6,2},{7,3},{8,12},{9,13},{10,... | collective-permute-start | bytes 688136 | tf_op jit(solution)/shard_map/ppermute | solution.py:466
  34.7 15.3 %collective-permute-start.10 = (bf16[8,16,576]{2,1,0:T(8,128)(2,1)S(1)}, bf16[8,16,576]{2,1,0:T(8,128)(2,1)S(1)}, u32[]{:S(2)}, u32[]{:S(2)}) collective-permute-start(bf16[8,16,576]{2,1,0:T(8,128)(2,1)S(1)} %get-tuple-element.21), channel_id=1, source_target_pairs={{0,8},{1,9},{2,10},{3,11},{4,12},{5,13},{6,14},{7,15},{8,0},{9,1},... | collective-permute-start | bytes 442376 | tf_op jit(solution)/shard_map/ppermute | solution.py:466
  39.2 7.4 %collective-permute-start.4 = (bf16[32,1792]{1,0:T(8,128)(2,1)S(1)}, bf16[32,1792]{1,0:T(8,128)(2,1)S(1)}, u32[]{:S(2)}, u32[]{:S(2)}) collective-permute-start(bf16[32,1792]{1,0:T(8,128)(2,1)S(1)} %slice.131), channel_id=1, source_target_pairs={{0,4},{1,5},{2,6},{3,7},{4,0},{5,1},{6,2},{7,3},{8,12},{9,13},{10,... | collective-permute-start | bytes 344072 | tf_op jit(solution)/shard_map/ppermute | solution.py:466
  45.0 4.9 %collective-permute-start.7 = (bf16[32,1792]{1,0:T(8,128)(2,1)S(1)}, bf16[32,1792]{1,0:T(8,128)(2,1)S(1)}, u32[]{:S(2)}, u32[]{:S(2)}) collective-permute-start(bf16[32,1792]{1,0:T(8,128)(2,1)S(1)} %slice.130), channel_id=1, source_target_pairs={{0,2},{1,3},{2,0},{3,1},{4,6},{5,7},{6,4},{7,5},{8,10},{9,11},{10,... | collective-permute-start | bytes 344072 | tf_op jit(solution)/shard_map/ppermute | solution.py:466
  49.9 6.1 %collective-permute-start.8 = (bf16[16,3584]{1,0:T(8,128)(2,1)S(1)}, bf16[16,3584]{1,0:T(8,128)(2,1)S(1)}, u32[]{:S(2)}, u32[]{:S(2)}) collective-permute-start(bf16[16,3584]{1,0:T(8,128)(2,1)S(1)} %pad_maximum_fusion.3), channel_id=1, source_target_pairs={{0,8},{1,9},{2,10},{3,11},{4,12},{5,13},{6,14},{7,15},{8,0},{9,1},... | collective-permute-start | bytes 344072 | tf_op jit(solution)/shard_map/ppermute | solution.py:466

commit v3 on v1

--- a/solution.py
+++ b/solution.py
@@ -152,6 +152,7 @@
 
 
 BLOCK = 16
+SCOPED_BYTES = 16 * 2**20
 
 
 def as_column(row):
@@ -174,74 +175,137 @@
     return jnp.sum(jnp.where(mine, wide, 0.0), axis=0, keepdims=True)
 
 
-def outbox_kernel(routes_ref, weights_ref, hidden_ref, out_ref):
+def ceil_rows(position, source, devices):
+    return (position + (devices - 1) - source) // devices
+
+
+def request_spans(lengths_ref, assignment_ref):
+    requests = lengths_ref.shape[1]
+    length_column = as_column(lengths_ref[...])
+    assignment = assignment_ref[...]
+    number = lax.broadcasted_iota(jnp.int32, (requests, requests), 0)
+    before = jnp.sum(jnp.where(number < assignment, length_column, 0), axis=0, keepdims=True)
+    own = jnp.sum(jnp.where(number == assignment, length_column, 0), axis=0, keepdims=True)
+    return before, before + own
+
+
+def apart_of(place, bits):
+    apart = place * 0
+    for i, bit in enumerate(bits):
+        digit = (place // (1 << (len(bits) - 1 - i))) % 2
+        apart = apart + digit * bit
+    return apart
+
+
+def outbox_kernel(
+    chips,
+    per_owner,
+    routes_ref,
+    weights_ref,
+    hidden_ref,
+    lengths_ref,
+    assignment_ref,
+    kv_ref,
+    near_ref,
+    far_ref,
+):
+    me = lax.axis_index("seq")
+    devices = 2 * chips
+    half = near_ref.shape[0]
+    slots = 2 * half
+    room = slots // devices
     rows, steps, top = routes_ref.shape
     tokens = rows * steps
     lanes = tokens * top
-    slots = out_ref.shape[0]
+    hidden_width = hidden_ref.shape[1]
     routes = jnp.concatenate([routes_ref[i] for i in range(rows)], axis=0).astype(jnp.float32)
     weights = jnp.concatenate([weights_ref[i] for i in range(rows)], axis=0)
     route_row = flat_row(routes, tokens, top).astype(jnp.int32)
     weight_row = flat_row(weights, tokens, top)
     slot = lax.broadcasted_iota(jnp.int32, (slots, lanes), 0)
     lane = lax.broadcasted_iota(jnp.int32, (slots, lanes), 1)
-    pick = (lane // top == slot % tokens) & (route_row == slot // tokens)
+    block = slot // room
+    target = me ^ (2 * (block % chips) + block // chips)
+    pick = (lane // top == slot % room) & (route_row == target)
     scale = jnp.sum(jnp.where(pick, weight_row, 0.0), axis=1, keepdims=True)
     chosen = jnp.where(pick, 1.0, 0.0).astype(jnp.bfloat16)
     moved = jnp.dot(chosen, hidden_ref[...], preferred_element_type=jnp.float32)
-    out_ref[...] = (moved * scale).astype(jnp.bfloat16)
-
-
-def pack_hidden(routes, route_weights, expert_hidden, experts):
-    rows, steps, top, width = expert_hidden.shape
-    tokens = rows * steps
-    return pl.pallas_call(
-        outbox_kernel,
-        out_shape=jax.ShapeDtypeStruct((experts * tokens, width), jnp.bfloat16),
-        cost_estimate=pl.CostEstimate(
-            flops=2 * experts * tokens * tokens * top * width,
-            bytes_accessed=2 * width * tokens * (top + experts),
-            transcendentals=0,
-        ),
-        name="pack_hidden",
-    )(routes, route_weights, expert_hidden.reshape(tokens * top, width))
-
-
-def ceil_rows(position, source, devices):
-    return (position + (devices - 1) - source) // devices
-
-
-def kv_kernel(devices, per_owner, lengths_ref, assignment_ref, kv_ref, out_ref, tags_ref):
-    me = lax.axis_index("seq")
+    moved = (moved * scale).astype(jnp.bfloat16)
+    near_ref[:, :hidden_width] = moved[:half]
+    far_ref[:, :hidden_width] = moved[half:]
+
     requests = lengths_ref.shape[1]
-    here = kv_ref.shape[1]
-    slots = out_ref.shape[0]
-    room = slots // devices
-    length_column = as_column(lengths_ref[...])
-    assignment = assignment_ref[...]
+    kv_width, here = kv_ref.shape
+    before, after_last = request_spans(lengths_ref, assignment_ref)
+    low = ceil_rows(before, me, devices)
+    count = ceil_rows(after_last, me, devices) - low
     number = lax.broadcasted_iota(jnp.int32, (requests, requests), 0)
-    before = jnp.sum(jnp.where(number < assignment, length_column, 0), axis=0, keepdims=True)
-    own = jnp.sum(jnp.where(number == assignment, length_column, 0), axis=0, keepdims=True)
-    after = before + own
-    low = ceil_rows(before, me, devices)
-    count = ceil_rows(after, me, devices) - low
     line = lax.broadcasted_iota(jnp.int32, (requests, requests), 1)
     same = (number // per_owner == line // per_owner) & (number < line)
     offset = jnp.sum(jnp.where(same, as_column(count), 0), axis=0, keepdims=True)
     slot = lax.broadcasted_iota(jnp.int32, (slots, requests), 0)
     decode = lax.broadcasted_iota(jnp.int32, (slots, requests), 1)
+    block = slot // room
+    target = me ^ (2 * (block % chips) + block // chips)
     rank = slot % room - offset
-    held = (slot // room == decode // per_owner) & (rank >= 0) & (rank < count)
+    held = (target == decode // per_owner) & (rank >= 0) & (rank < count)
     source = jnp.sum(jnp.where(held, low + rank + 1, 0), axis=1, keepdims=True) - 1
     pick = source == lax.broadcasted_iota(jnp.int32, (slots, here), 1)
-    out_ref[...] = lax.dot_general(
+    moved = lax.dot_general(
         jnp.where(pick, 1.0, 0.0).astype(jnp.bfloat16),
         kv_ref[...],
         (((1,), (1,)), ((), ())),
         preferred_element_type=jnp.float32,
     ).astype(jnp.bfloat16)
+    last = hidden_width + kv_width
+    empty = jnp.zeros((half, near_ref.shape[1] - last), jnp.bfloat16)
+    near_ref[:, hidden_width:last] = moved[:half]
+    far_ref[:, hidden_width:last] = moved[half:]
+    near_ref[:, last:] = empty
+    far_ref[:, last:] = empty
+
+
+def pack_outboxes(
+    routes, route_weights, expert_hidden, lengths, assignment, prefill_kv, devices
+):
+    rows, steps, top, hidden_width = expert_hidden.shape
+    here, kv_width = prefill_kv.shape
+    tokens = rows * steps
+    slots = tokens * devices
+    width = pl.cdiv(hidden_width + kv_width, 128) * 128
+    operands = (
+        routes,
+        route_weights,
+        expert_hidden.reshape(tokens * top, hidden_width),
+        lengths.reshape(1, -1),
+        assignment.reshape(1, -1),
+        prefill_kv.T,
+    )
+    return pl.pallas_call(
+        functools.partial(outbox_kernel, devices // 2, rows),
+        out_shape=(jax.ShapeDtypeStruct((slots // 2, width), jnp.bfloat16),) * 2,
+        compiler_params=pltpu.CompilerParams(vmem_limit_bytes=SCOPED_BYTES),
+        cost_estimate=pl.CostEstimate(
+            flops=2 * slots * (tokens * top * hidden_width + here * kv_width),
+            bytes_accessed=4 * slots * width,
+            transcendentals=0,
+        ),
+        name="pack_outboxes",
+    )(*(pltpu.with_memory_space_constraint(x, pltpu.HBM) for x in operands))
+
+
+def load_kernel(
+    devices, per_owner, lengths_ref, assignment_ref, down_ref, tags_ref, held_ref, sem
+):
+    copy = pltpu.make_async_copy(down_ref, held_ref, sem)
+    copy.start()
+    me = lax.axis_index("seq")
+    requests = lengths_ref.shape[1]
+    slots = tags_ref.shape[1]
+    room = slots // devices
+    before, after = request_spans(lengths_ref, assignment_ref)
     place = lax.broadcasted_iota(jnp.int32, (1, slots), 1)
-    sender, rank = place // room, place % room
+    sender, rank = me ^ (place // room), place % room
     tags = jnp.full((1, slots), -1, jnp.int32)
     decode = lax.broadcasted_iota(jnp.int32, (1, requests), 1)
     taken = jnp.zeros((1, slots), jnp.int32)
@@ -253,28 +317,42 @@
         tags = jnp.where((rank >= taken) & (rank < taken + arriving), q, tags)
         taken = taken + arriving
     tags_ref[...] = tags
-
-
-def pack_kv(prefill_kv, lengths, assignment, devices, per_owner, room):
-    here, width = prefill_kv.shape
-    slots = devices * room
+    copy.wait()
+
+
+def load_down(lengths, assignment, expert_down, devices, per_owner, slots):
+    vmem = pl.BlockSpec(memory_space=pltpu.VMEM)
     return pl.pallas_call(
-        functools.partial(kv_kernel, devices, per_owner),
+        functools.partial(load_kernel, devices, per_owner),
+        in_specs=[vmem, vmem, pl.BlockSpec(memory_space=pltpu.HBM)],
+        out_specs=[vmem, vmem],
         out_shape=(
-            jax.ShapeDtypeStruct((slots, width), jnp.bfloat16),
             jax.ShapeDtypeStruct((1, slots), jnp.int32),
+            pltpu.VMEM(expert_down.shape, expert_down.dtype),
         ),
+        scratch_shapes=[pltpu.SemaphoreType.DMA],
+        compiler_params=pltpu.CompilerParams(vmem_limit_bytes=SCOPED_BYTES),
         cost_estimate=pl.CostEstimate(
-            flops=2 * slots * here * width,
-            bytes_accessed=2 * width * (here + slots),
-            transcendentals=0,
+            flops=0, bytes_accessed=2 * expert_down.size, transcendentals=0
         ),
-        name="pack_kv",
-    )(lengths.reshape(1, -1), assignment.reshape(1, -1), prefill_kv.T)
-
-
-def attend_kernel(queries_ref, fresh_ref, cache_ref, tags_ref, out_ref):
+        name="load_down",
+    )(
+        pltpu.with_memory_space_constraint(lengths.reshape(1, -1), pltpu.HBM),
+        pltpu.with_memory_space_constraint(assignment.reshape(1, -1), pltpu.HBM),
+        pltpu.with_memory_space_constraint(expert_down, pltpu.HBM),
+    )
+
+
+def attend_kernel(first, pieces, queries_ref, fresh_ref, tags_ref, *refs):
+    arrived_refs, out_ref, cache_ref = refs[:pieces], refs[pieces], refs[pieces + 1]
     mine = pl.program_id(0)
+    rows, width = arrived_refs[0].shape[0], cache_ref.shape[1]
+
+    @pl.when(mine == 0)
+    def _():
+        for i, arrived_ref in enumerate(arrived_refs):
+            cache_ref[i * rows : (i + 1) * rows, :] = arrived_ref[:, first : first + width]
+
     steps, _, heads, width = queries_ref.shape
     latent = out_ref.shape[3]
     per_owner = fresh_ref.shape[1]
@@ -316,80 +394,77 @@
     out_ref[...] = context.reshape(steps, 1, heads, latent)
 
 
-def attend(queries, new_kv, kv_cache, tags):
+def attend(queries, new_kv, arrived, first, tags):
     steps, per_owner, heads, width = queries.shape
-    slots = kv_cache.shape[0]
+    slots = tags.shape[1]
     latent = width - ROPE
     return pl.pallas_call(
-        attend_kernel,
+        functools.partial(attend_kernel, first, len(arrived)),
         grid=(per_owner,),
         in_specs=[
             pl.BlockSpec((steps, 1, heads, width), lambda q: (0, q, 0, 0)),
             pl.BlockSpec((steps, per_owner, width), lambda q: (0, 0, 0)),
-            pl.BlockSpec((slots, width), lambda q: (0, 0)),
             pl.BlockSpec((1, slots), lambda q: (0, 0)),
-        ],
+        ]
+        + [pl.BlockSpec(piece.shape, lambda q: (0, 0)) for piece in arrived],
         out_specs=pl.BlockSpec((steps, 1, heads, latent), lambda q: (0, q, 0, 0)),
         out_shape=jax.ShapeDtypeStruct((steps, per_owner, heads, latent), jnp.bfloat16),
+        scratch_shapes=[pltpu.VMEM((slots, width), jnp.bfloat16)],
+        compiler_params=pltpu.CompilerParams(vmem_limit_bytes=SCOPED_BYTES),
         cost_estimate=pl.CostEstimate(
             flops=2 * steps * per_owner * heads * slots * (width + latent),
             bytes_accessed=2 * steps * per_owner * heads * (width + latent),
             transcendentals=steps * per_owner * heads * slots,
         ),
         name="attend",
-    )(queries, new_kv, kv_cache, tags)
-
-
-def expert_kernel(bits, arrived_ref, down_ref, keep_ref, send_ref, sorted_ref):
-    me = lax.axis_index("seq")
-    blocks = 1 << len(bits)
-    half = keep_ref.shape[0]
-
-    @pl.when(pl.program_id(0) == 0)
-    def _():
-        for place in range(blocks):
-            apart = 0
-            for i, bit in enumerate(bits):
-                if place >> (len(bits) - 1 - i) & 1:
-                    apart |= bit
-            start = pl.multiple_of((me ^ apart) * BLOCK, BLOCK)
-            sorted_ref[place * BLOCK : (place + 1) * BLOCK, :] = arrived_ref[
-                pl.ds(start, BLOCK), :
-            ]
-
-    result = jnp.dot(sorted_ref[...], down_ref[0], preferred_element_type=jnp.float32)
+    )(queries, new_kv, tags, *arrived)
+
+
+def expert_kernel(bits, first, pieces, down_ref, *refs):
+    arrived_refs, (keep_ref, send_ref, sorted_ref) = refs[:pieces], refs[pieces:]
+    half, width = keep_ref.shape
+    hidden_width = sorted_ref.shape[1]
+    per_piece = arrived_refs[0].shape[0] // BLOCK
+    for place in range(1 << len(bits)):
+        piece, block = divmod(apart_of(place, bits), per_piece)
+        sorted_ref[place * BLOCK : (place + 1) * BLOCK, :] = arrived_refs[piece][
+            block * BLOCK : (block + 1) * BLOCK, :hidden_width
+        ]
+    result = jnp.dot(
+        sorted_ref[...],
+        down_ref[0, :, first : first + width],
+        preferred_element_type=jnp.float32,
+    )
     keep_ref[...] = result[:half]
     send_ref[...] = result[half:].astype(jnp.bfloat16)
 
 
-def expert_part(arrived, expert_down, bits, part, parts, tile):
-    slots, hidden_width = arrived.shape
-    width = expert_down.shape[2] // parts
+def expert_part(arrived, expert_down, bits, part, parts):
+    slots = BLOCK << len(bits)
+    _, hidden_width, model_width = expert_down.shape
+    width = model_width // parts
     half = slots // 2
-    tiles = width // tile
+    vmem = pl.BlockSpec(memory_space=pltpu.VMEM)
     return pl.pallas_call(
-        functools.partial(expert_kernel, bits),
-        grid=(tiles,),
-        in_specs=[
-            pl.BlockSpec((slots, hidden_width), lambda i: (0, 0)),
-            pl.BlockSpec((1, hidden_width, tile), lambda i: (0, 0, i + part * tiles)),
-        ],
-        out_specs=[
-            pl.BlockSpec((half, tile), lambda i: (0, i)),
-            pl.BlockSpec((half, tile), lambda i: (0, i)),
-        ],
+        functools.partial(expert_kernel, bits, part * width, len(arrived)),
+        in_specs=[vmem] * (1 + len(arrived)),
+        out_specs=[vmem] * 2,
         out_shape=(
             jax.ShapeDtypeStruct((half, width), jnp.float32),
             jax.ShapeDtypeStruct((half, width), jnp.bfloat16),
         ),
         scratch_shapes=[pltpu.VMEM((slots, hidden_width), jnp.bfloat16)],
+        compiler_params=pltpu.CompilerParams(vmem_limit_bytes=SCOPED_BYTES),
         cost_estimate=pl.CostEstimate(
             flops=2 * slots * hidden_width * width,
-            bytes_accessed=2 * hidden_width * width + 6 * half * width,
+            bytes_accessed=2 * hidden_width * width,
             transcendentals=0,
         ),
         name="expert_part",
-    )(arrived, expert_down)
+    )(expert_down, *arrived)
+
+
+after = lax.optimization_barrier
 
 
 def swap(values, bit, devices):
@@ -417,38 +492,37 @@
     steps, per_owner = queries.shape[:2]
     rows, _, top, hidden_width = expert_hidden.shape
     model_width = expert_down.shape[2]
-    outbox = pack_hidden(routes, route_weights, expert_hidden, devices)
-    arrived = lax.all_to_all(
-        outbox.reshape(devices, BLOCK, hidden_width), "seq", split_axis=0, concat_axis=0, tiled=True
-    ).reshape(devices * BLOCK, hidden_width)
-    kv_outbox, tags = pack_kv(
-        prefill_kv, lengths, assignment, devices, per_owner, 2 * HALF * per_owner
-    )
+    near, far = pack_outboxes(
+        routes, route_weights, expert_hidden, lengths, assignment, prefill_kv, devices
+    )
+    crossed = swap(far, 1, devices)
+    chips = devices // 2
+    arrived = [None] * chips
+    for apart in (0, 4, 2, 6, 1, 5, 3, 7):
+        block = slice(apart * BLOCK, (apart + 1) * BLOCK)
+        piece = jnp.concatenate([near[block], crossed[block]], axis=0)
+        arrived[apart] = swap(piece, 2 * apart, devices) if apart else piece
+    late_lengths, _ = after((lengths, arrived[4]))
+    tags, down = load_down(
+        late_lengths, assignment, expert_down, devices, per_owner, devices * BLOCK
+    )
+    context = attend(queries, new_kv, arrived, hidden_width, tags)
 
     orders = ((1, 2, 4, 8), (1, 4, 2, 8))
-    parts = len(orders)
     flows = []
     for part, bits in enumerate(orders):
-        kept, sent = expert_part(arrived, expert_down, bits, part, parts, 256)
-        flows.append((kept, sent, swap(sent, bits[0], devices)))
-    flows = [fold(kept, received) for kept, _, received in flows]
+        kept, sent = expert_part(arrived, down, bits, part, len(orders))
+        flows.append((kept, swap(sent, bits[0], devices)))
+    flows = [fold(kept, received) for kept, received in flows]
     received = [swap(sent, bits[1], devices) for (_, sent), bits in zip(flows, orders)]
-
-    kv_outbox, _ = lax.optimization_barrier((kv_outbox, [sent for _, sent in flows]))
-    kv_cache = lax.all_to_all(
-        kv_outbox.reshape(devices, -1, kv_outbox.shape[1]),
-        "seq",
-        split_axis=0,
-        concat_axis=0,
-        tiled=True,
-    ).reshape(kv_outbox.shape)
-    context = attend(queries, new_kv, kv_cache, tags)
-
-    for level in (2, 3):
-        flows = [fold(kept, got) for (kept, _), got in zip(flows, received)]
-        received = [swap(sent, bits[level], devices) for (_, sent), bits in zip(flows, orders)]
-    final = [kept + got.astype(jnp.float32) for (kept, _), got in zip(flows, received)]
-    moe_out = jnp.concatenate(final, axis=1).astype(jnp.bfloat16)
+    flows = [fold(kept, got) for (kept, _), got in zip(flows, received)]
+    received = [swap(sent, bits[2], devices) for (_, sent), bits in zip(flows, orders)]
+    flows = [fold(kept, got) for (kept, _), got in zip(flows, received)]
+    kept = jnp.concatenate([kept for kept, _ in flows], axis=1)
+    sent = jnp.concatenate([sent for _, sent in flows], axis=1)
+    received = swap(sent, orders[0][-1], devices)
+    received, context = lax.optimization_barrier((received, context))
+    moe_out = (kept + received.astype(jnp.float32)).astype(jnp.bfloat16)
     return context, moe_out.reshape(rows, steps, model_width)
 
 

time: 75.7 us -> 54.3 us (0.72)
  blocking collectives: 22 us -> 0 us
  starting transfers between devices: 12.3 us -> 25 us
  Pallas kernels: 23.2 us -> 12.3 us
  other arithmetic: 2.18 us -> 0.4 us
  waiting for transfers between devices: 13.7 us -> 14.6 us
    all_to_all x1 -> x0, blocking collectives: 22 us -> none  [per_device_dense(): lax.all_to_all(outbox.reshape(devices, BLOCK, hidden_width), 'seq', split...]
    ppermute x8 -> x15, starting transfers between devices: 8.8 us -> 25 us  [swap(): return lax.ppermute(values, 'seq', [(i, i ^ bit) for i in range(devices)])]
    pallas_call x5, Pallas kernels: 23.2 us -> 12.3 us  [the longest x1 4.69 us: attend(): pl.pallas_call(functools.partial(attend_kernel, first, len(arrived)), gri...]
    all_to_all x1 -> x0, starting transfers between devices: 3.54 us -> none  [per_device_dense(): lax.all_to_all(kv_outbox.reshape(devices, -1, kv_outbox.shape[1]), 'seq',...]
    add x6, other arithmetic: 1.46 us -> 0.28 us  [fold(): total = kept + received.astype(jnp.float32)]
    ppermute x8 -> x15, waiting for transfers between devices: 13.7 us -> 14.6 us  [swap(): return lax.ppermute(values, 'seq', [(i, i ^ bit) for i in range(devices)])]
  transfers between devices with their start and end apart: 9 -> 15, of which waited for: 5 -> 8; matrix products, arithmetic and copies ran while one was open for 3% -> 1% of each run, Pallas kernels for 12% -> 18%
where the time goes in v3:
time: 54.3 us; the launch traced here: 54.1 us
  starting transfers between devices  25 us (46%)
  waiting for transfers between devices  14.6 us (27%)
  Pallas kernels  12.3 us (23%)
  local copies, waits for them, and re-layouts  0.87 us (2%)
  between operations  0.84 us (2%)
    ppermute x15, starting transfers between devices, swap(): return lax.ppermute(values, 'seq', [(i, i ^ bit) for i in range(devices)])  25 us
    ppermute x15, waiting for transfers between devices, swap(): return lax.ppermute(values, 'seq', [(i, i ^ bit) for i in range(devices)])  14.6 us
    pallas_call x1, Pallas kernels, attend(): pl.pallas_call(functools.partial(attend_kernel, first, len(arrived)), gri...  4.69 us
    pallas_call x1, Pallas kernels, load_down(): pl.pallas_call(functools.partial(load_kernel, devices, per_owner), in_spe...  3.77 us
    pallas_call x2, Pallas kernels, expert_part(): pl.pallas_call(functools.partial(expert_kernel, bits, part * width, len(a...  2.25 us
    pallas_call x1, Pallas kernels, pack_outboxes(): pl.pallas_call(functools.partial(outbox_kernel, devices // 2, rows), out_...  1.64 us
  transfers between devices with their start and end apart: 15, of which 8 were waited for; matrix products, arithmetic and copies ran while one was open for 1% of the time, Pallas kernels for 18%

profile of v3, /device:TPU:0, one launch (start us, length us, event | category | flops | bytes accessed | tf_op | source)
XLA Modules:
  0.0 54.1 jit_solution(14881316438361615748)
XLA Ops:
  0.6 1.6 %pack_outboxes.1 = (bf16[128,1664]{1,0:T(8,128)(2,1)S(1)}, bf16[128,1664]{1,0:T(8,128)(2,1)S(1)}) custom-call(s32[4,4,8]{2,1,0:T(4,128)} %routes_ref.1, f32[4,4,8]{2,1,0:T(4,128)} %weights_ref.1, bf16[128,1024]{1,0:T(8,128)(2,1)} %bitcast.5, s32[1,64]{1,0:T(1,128)} %bitcast.7, s32[1,64]{1,0:T(1,128)} %bitcast.9, bf16[576,128]{1,0:T(8,128)(2,1)} %bitcast.6), custom_call_target="tpu_custom_call" | custom-call | flops 104857600 | bytes 1703936 | tf_op jit(solution)/shard_map/pack_outboxes/pallas_call | solution.py:284
  2.3 0.5 collective-permute-start
  2.8 1.4 %collective-permute-done = bf16[128,1664]{1,0:T(8,128)(2,1)S(1)} collective-permute-done((bf16[128,1664]{1,0:T(8,128)(2,1)S(1)}, bf16[128,1664]{1,0:T(8,128)(2,1)S(1)}, u32[]{:S(2)}, u32[]{:S(2)}) %collective-permute-start) | collective-permute-done | bytes 426016 | tf_op jit(solution)/shard_map/ppermute | solution.py:471
  4.2 4.0 %collective-permute-start.1 = (bf16[32,1664]{1,0:T(8,128)(2,1)S(1)}, bf16[32,1664]{1,0:T(8,128)(2,1)S(1)}, u32[]{:S(2)}, u32[]{:S(2)}) collective-permute-start(bf16[32,1664]{1,0:T(8,128)(2,1)S(1)} %pad_maximum_fusion.1), channel_id=1, source_target_pairs={{0,8},{1,9},{2,10},{3,11},{4,12},{5,13},{6,14},{7,15},{8,0},{9,1},... | collective-permute-start | bytes 319496 | tf_op jit(solution)/shard_map/ppermute | solution.py:471
  8.3 1.6 %collective-permute-start.2 = (bf16[32,1664]{1,0:T(8,128)(2,1)S(1)}, bf16[32,1664]{1,0:T(8,128)(2,1)S(1)}, u32[]{:S(2)}, u32[]{:S(2)}) collective-permute-start(bf16[32,1664]{1,0:T(8,128)(2,1)S(1)} %pad_maximum_fusion.3), channel_id=1, source_target_pairs={{0,2},{1,3},{2,0},{3,1},{4,6},{5,7},{6,4},{7,5},{8,10},{9,11},{10,... | collective-permute-start | bytes 319496 | tf_op jit(solution)/shard_map/ppermute | solution.py:471
  9.9 1.6 %collective-permute-start.3 = (bf16[32,1664]{1,0:T(8,128)(2,1)S(1)}, bf16[32,1664]{1,0:T(8,128)(2,1)S(1)}, u32[]{:S(2)}, u32[]{:S(2)}) collective-permute-start(bf16[32,1664]{1,0:T(8,128)(2,1)S(1)} %pad_maximum_fusion.4), channel_id=1, source_target_pairs={{0,4},{1,5},{2,6},{3,7},{4,0},{5,1},{6,2},{7,3},{8,12},{9,13},{10,... | collective-permute-start | bytes 319496 | tf_op jit(solution)/shard_map/ppermute | solution.py:471
  11.5 0.5 collective-permute-start.4
  12.0 1.4 %collective-permute-start.5 = (bf16[32,1664]{1,0:T(8,128)(2,1)S(1)}, bf16[32,1664]{1,0:T(8,128)(2,1)S(1)}, u32[]{:S(2)}, u32[]{:S(2)}) collective-permute-start(bf16[32,1664]{1,0:T(8,128)(2,1)S(1)} %pad_maximum_fusion.6), channel_id=1, source_target_pairs={{0,10},{1,11},{2,8},{3,9},{4,14},{5,15},{6,12},{7,13},{8,2},{9,3},... | collective-permute-start | bytes 319496 | tf_op jit(solution)/shard_map/ppermute | solution.py:471
  13.4 0.5 %collective-permute-done.1.refs_4_ = bf16[32,1664]{1,0:T(8,128)(2,1)S(1)} collective-permute-done((bf16[32,1664]{1,0:T(8,128)(2,1)S(1)}, bf16[32,1664]{1,0:T(8,128)(2,1)S(1)}, u32[]{:S(2)}, u32[]{:S(2)}) %collective-permute-start.1) | collective-permute-done | bytes 106528 | tf_op jit(solution)/shard_map/ppermute | solution.py:471
  13.9 3.6 %collective-permute-start.6 = (bf16[32,1664]{1,0:T(8,128)(2,1)S(1)}, bf16[32,1664]{1,0:T(8,128)(2,1)S(1)}, u32[]{:S(2)}, u32[]{:S(2)}) collective-permute-start(bf16[32,1664]{1,0:T(8,128)(2,1)S(1)} %pad_maximum_fusion.7), channel_id=1, source_target_pairs={{0,12},{1,13},{2,14},{3,15},{4,8},{5,9},{6,10},{7,11},{8,4},{9,5},... | collective-permute-start | bytes 319496 | tf_op jit(solution)/shard_map/ppermute | solution.py:471
  17.5 0.0 collective-permute-done.2.refs_1_
  17.5 1.2 %collective-permute-start.7 = (bf16[32,1664]{1,0:T(8,128)(2,1)S(1)}, bf16[32,1664]{1,0:T(8,128)(2,1)S(1)}, u32[]{:S(2)}, u32[]{:S(2)}) collective-permute-start(bf16[32,1664]{1,0:T(8,128)(2,1)S(1)} %pad_maximum_fusion.8), channel_id=1, source_target_pairs={{0,14},{1,15},{2,12},{3,13},{4,10},{5,11},{6,8},{7,9},{8,6},{9,7},... | collective-permute-start | bytes 319496 | tf_op jit(solution)/shard_map/ppermute | solution.py:471
  18.8 3.8 %load_down.1 = (s32[1,256]{1,0:T(1,128)S(1)}, bf16[1,1024,3584]{2,1,0:T(8,128)(2,1)S(1)}) custom-call(s32[1,64]{1,0:T(1,128)} %bitcast.8, s32[1,64]{1,0:T(1,128)} %bitcast.10, bf16[1,1024,3584]{2,1,0:T(8,128)(2,1)} %down_ref.1), custom_call_target="tpu_custom_call" | custom-call | bytes 7340032 | tf_op jit(solution)/shard_map/load_down/pallas_call | solution.py:325
  22.5 0.0 collective-permute-done.3.refs_2_
  22.6 0.0 collective-permute-done.4.refs_3_
  22.6 3.9 %collective-permute-done.5.refs_5_ = bf16[32,1664]{1,0:T(8,128)(2,1)S(1)} collective-permute-done((bf16[32,1664]{1,0:T(8,128)(2,1)S(1)}, bf16[32,1664]{1,0:T(8,128)(2,1)S(1)}, u32[]{:S(2)}, u32[]{:S(2)}) %collective-permute-start.5) | collective-permute-done | bytes 106528 | tf_op jit(solution)/shard_map/ppermute | solution.py:471
  26.4 0.0 collective-permute-done.6.refs_6_
  26.4 0.0 collective-permute-done.7.refs_7_
  26.4 1.1 %expert_part.3 = (f32[128,1792]{1,0:T(8,128)S(1)}, bf16[128,1792]{1,0:T(8,128)(2,1)S(1)}) custom-call(bf16[1,1024,3584]{2,1,0:T(8,128)(2,1)S(1)} %get-tuple-element.16.down_ref, bf16[32,1664]{1,0:T(8,128)(2,1)S(1)} %pad_maximum_fusion.2.refs_0_, bf16[32,1664]{1,0:T(8,128)(2,1)S(1)} %collective-permute-done.2.refs_1_, ...), custom_call_target="tpu_custom_call" | custom-call | flops 939524096 | bytes 3670016 | tf_op jit(solution)/shard_map/expert_part/pallas_call | solution.py:448
  27.6 0.0 copy-start
  27.6 0.0 copy-start.1
  27.6 0.1 collective-permute-start.11
  27.7 1.1 %expert_part.2 = (f32[128,1792]{1,0:T(8,128)S(1)}, bf16[128,1792]{1,0:T(8,128)(2,1)S(1)}) custom-call(bf16[1,1024,3584]{2,1,0:T(8,128)(2,1)S(1)} %get-tuple-element.16.down_ref, bf16[32,1664]{1,0:T(8,128)(2,1)S(1)} %pad_maximum_fusion.2.refs_0_, bf16[32,1664]{1,0:T(8,128)(2,1)S(1)} %collective-permute-done.2.refs_1_, ...), custom_call_target="tpu_custom_call" | custom-call | flops 939524096 | bytes 3670016 | tf_op jit(solution)/shard_map/expert_part/pallas_call | solution.py:448
  28.8 0.6 %collective-permute-start.8 = (bf16[128,1792]{1,0:T(8,128)(2,1)S(1)}, bf16[128,1792]{1,0:T(8,128)(2,1)S(1)}, u32[]{:S(2)}, u32[]{:S(2)}) collective-permute-start(bf16[128,1792]{1,0:T(8,128)(2,1)S(1)} %get-tuple-element.18), channel_id=1, source_target_pairs={{0,1},{1,0},{2,3},{3,2},{4,5},{5,4},{6,7},{7,6},{8,9},{9,8},{10,11... | collective-permute-start | bytes 1376264 | tf_op jit(solution)/shard_map/ppermute | solution.py:471
  29.4 0.1 collective-permute-done.11
  29.5 0.1 convert_add_fusion
  29.6 4.1 %collective-permute-start.12 = (bf16[64,1792]{1,0:T(8,128)(2,1)S(1)}, bf16[64,1792]{1,0:T(8,128)(2,1)S(1)}, u32[]{:S(2)}, u32[]{:S(2)}) collective-permute-start(bf16[64,1792]{1,0:T(8,128)(2,1)S(1)} %slice.148), channel_id=1, source_target_pairs={{0,4},{1,5},{2,6},{3,7},{4,0},{5,1},{6,2},{7,3},{8,12},{9,13},{10,... | collective-permute-start | bytes 688136 | tf_op jit(solution)/shard_map/ppermute | solution.py:471
  33.7 0.0 collective-permute-done.8
  33.7 0.1 convert_add_fusion.1
  33.8 0.9 %collective-permute-start.9 = (bf16[64,1792]{1,0:T(8,128)(2,1)S(1)}, bf16[64,1792]{1,0:T(8,128)(2,1)S(1)}, u32[]{:S(2)}, u32[]{:S(2)}) collective-permute-start(bf16[64,1792]{1,0:T(8,128)(2,1)S(1)} %slice.149), channel_id=1, source_target_pairs={{0,2},{1,3},{2,0},{3,1},{4,6},{5,7},{6,4},{7,5},{8,10},{9,11},{10,... | collective-permute-start | bytes 688136 | tf_op jit(solution)/shard_map/ppermute | solution.py:471
  34.7 4.9 %collective-permute-done.12 = bf16[64,1792]{1,0:T(8,128)(2,1)S(1)} collective-permute-done((bf16[64,1792]{1,0:T(8,128)(2,1)S(1)}, bf16[64,1792]{1,0:T(8,128)(2,1)S(1)}, u32[]{:S(2)}, u32[]{:S(2)}) %collective-permute-start.12) | collective-permute-done | bytes 229408 | tf_op jit(solution)/shard_map/ppermute | solution.py:471
  39.7 0.9 %collective-permute-start.13 = (bf16[32,1792]{1,0:T(8,128)(2,1)S(1)}, bf16[32,1792]{1,0:T(8,128)(2,1)S(1)}, u32[]{:S(2)}, u32[]{:S(2)}) collective-permute-start(bf16[32,1792]{1,0:T(8,128)(2,1)S(1)} %slice.150), channel_id=1, source_target_pairs={{0,2},{1,3},{2,0},{3,1},{4,6},{5,7},{6,4},{7,5},{8,10},{9,11},{10,... | collective-permute-start | bytes 344072 | tf_op jit(solution)/shard_map/ppermute | solution.py:471
  40.6 0.7 %collective-permute-done.9 = bf16[64,1792]{1,0:T(8,128)(2,1)S(1)} collective-permute-done((bf16[64,1792]{1,0:T(8,128)(2,1)S(1)}, bf16[64,1792]{1,0:T(8,128)(2,1)S(1)}, u32[]{:S(2)}, u32[]{:S(2)}) %collective-permute-start.9) | collective-permute-done | bytes 229408 | tf_op jit(solution)/shard_map/ppermute | solution.py:471
  41.3 1.7 %collective-permute-start.10 = (bf16[32,1792]{1,0:T(8,128)(2,1)S(1)}, bf16[32,1792]{1,0:T(8,128)(2,1)S(1)}, u32[]{:S(2)}, u32[]{:S(2)}) collective-permute-start(bf16[32,1792]{1,0:T(8,128)(2,1)S(1)} %slice.151), channel_id=1, source_target_pairs={{0,4},{1,5},{2,6},{3,7},{4,0},{5,1},{6,2},{7,3},{8,12},{9,13},{10,... | collective-permute-start | bytes 344072 | tf_op jit(solution)/shard_map/ppermute | solution.py:471
  43.1 1.5 %collective-permute-done.13 = bf16[32,1792]{1,0:T(8,128)(2,1)S(1)} collective-permute-done((bf16[32,1792]{1,0:T(8,128)(2,1)S(1)}, bf16[32,1792]{1,0:T(8,128)(2,1)S(1)}, u32[]{:S(2)}, u32[]{:S(2)}) %collective-permute-start.13) | collective-permute-done | bytes 114720 | tf_op jit(solution)/shard_map/ppermute | solution.py:471
  44.6 1.6 %collective-permute-done.10 = bf16[32,1792]{1,0:T(8,128)(2,1)S(1)} collective-permute-done((bf16[32,1792]{1,0:T(8,128)(2,1)S(1)}, bf16[32,1792]{1,0:T(8,128)(2,1)S(1)}, u32[]{:S(2)}, u32[]{:S(2)}) %collective-permute-start.10) | collective-permute-done | bytes 114720 | tf_op jit(solution)/shard_map/ppermute | solution.py:471
  46.3 2.4 %collective-permute-start.14 = (bf16[16,3584]{1,0:T(8,128)(2,1)S(1)}, bf16[16,3584]{1,0:T(8,128)(2,1)S(1)}, u32[]{:S(2)}, u32[]{:S(2)}) collective-permute-start(bf16[16,3584]{1,0:T(8,128)(2,1)S(1)} %pad_maximum_fusion), channel_id=1, source_target_pairs={{0,8},{1,9},{2,10},{3,11},{4,12},{5,13},{6,14},{7,15},{8,0},{9,1},... | collective-permute-start | bytes 344072 | tf_op jit(solution)/shard_map/ppermute | solution.py:471
  48.6 0.0 copy-done
  48.6 0.0 copy-done.1
  48.6 4.7 %attend.1 = bf16[4,4,64,512]{3,2,1,0:T(8,128)(2,1)} custom-call(bf16[4,4,64,576]{3,2,1,0:T(8,128)(2,1)S(1)} %copy-done, bf16[4,4,576]{2,1,0:T(4,128)(2,1)S(1)} %copy-done.1, s32[1,256]{1,0:T(1,128)S(1)} %get-tuple-element.21.tags_ref, bf16[32,1664]{1,0:T(8,128)(2,1)S(1)} %pad_maximum_fusion.2.refs_0_, bf16[32,1664]{1,0:T(8,128)(2,1)S(1)} %collective-permute-done.2.refs_1_, ...), custom_call_target="tpu_custom_call" | custom-call | flops 570425344 | bytes 2228224 | tf_op jit(solution)/shard_map/attend/pallas_call | solution.py:401
  53.4 0.0 collective-permute-done.14
  53.4 0.7 %reshape.24 = bf16[4,4,3584]{2,1,0:T(4,128)(2,1)} reshape(bf16[16,3584]{1,0:T(8,128)(2,1)S(1)} %fusion) | data formatting | bytes 229376 | tf_op jit(solution)/shard_map/reshape | solution.py:526
  (24 shorter events, 0.4 us)
Async XLA Ops:
  2.3 1.9 %collective-permute-start = (bf16[128,1664]{1,0:T(8,128)(2,1)S(1)}, bf16[128,1664]{1,0:T(8,128)(2,1)S(1)}, u32[]{:S(2)}, u32[]{:S(2)}) collective-permute-start(bf16[128,1664]{1,0:T(8,128)(2,1)S(1)} %get-tuple-element.14), channel_id=1, source_target_pairs={{0,1},{1,0},{2,3},{3,2},{4,5},{5,4},{6,7},{7,6},{8,9},{9,8},{10,11... | collective-permute-start | bytes 1277960 | tf_op jit(solution)/shard_map/ppermute | solution.py:471
  4.2 9.7 %collective-permute-start.1 = (bf16[32,1664]{1,0:T(8,128)(2,1)S(1)}, bf16[32,1664]{1,0:T(8,128)(2,1)S(1)}, u32[]{:S(2)}, u32[]{:S(2)}) collective-permute-start(bf16[32,1664]{1,0:T(8,128)(2,1)S(1)} %pad_maximum_fusion.1), channel_id=1, source_target_pairs={{0,8},{1,9},{2,10},{3,11},{4,12},{5,13},{6,14},{7,15},{8,0},{9,1},... | collective-permute-start | bytes 319496 | tf_op jit(solution)/shard_map/ppermute | solution.py:471
  8.3 9.3 %collective-permute-start.2 = (bf16[32,1664]{1,0:T(8,128)(2,1)S(1)}, bf16[32,1664]{1,0:T(8,128)(2,1)S(1)}, u32[]{:S(2)}, u32[]{:S(2)}) collective-permute-start(bf16[32,1664]{1,0:T(8,128)(2,1)S(1)} %pad_maximum_fusion.3), channel_id=1, source_target_pairs={{0,2},{1,3},{2,0},{3,1},{4,6},{5,7},{6,4},{7,5},{8,10},{9,11},{10,... | collective-permute-start | bytes 319496 | tf_op jit(solution)/shard_map/ppermute | solution.py:471
  9.9 12.7 %collective-permute-start.3 = (bf16[32,1664]{1,0:T(8,128)(2,1)S(1)}, bf16[32,1664]{1,0:T(8,128)(2,1)S(1)}, u32[]{:S(2)}, u32[]{:S(2)}) collective-permute-start(bf16[32,1664]{1,0:T(8,128)(2,1)S(1)} %pad_maximum_fusion.4), channel_id=1, source_target_pairs={{0,4},{1,5},{2,6},{3,7},{4,0},{5,1},{6,2},{7,3},{8,12},{9,13},{10,... | collective-permute-start | bytes 319496 | tf_op jit(solution)/shard_map/ppermute | solution.py:471
  11.5 11.0 %collective-permute-start.4 = (bf16[32,1664]{1,0:T(8,128)(2,1)S(1)}, bf16[32,1664]{1,0:T(8,128)(2,1)S(1)}, u32[]{:S(2)}, u32[]{:S(2)}) collective-permute-start(bf16[32,1664]{1,0:T(8,128)(2,1)S(1)} %pad_maximum_fusion.5), channel_id=1, source_target_pairs={{0,6},{1,7},{2,4},{3,5},{4,2},{5,3},{6,0},{7,1},{8,14},{9,15},{10,... | collective-permute-start | bytes 319496 | tf_op jit(solution)/shard_map/ppermute | solution.py:471
  12.0 14.4 %collective-permute-start.5 = (bf16[32,1664]{1,0:T(8,128)(2,1)S(1)}, bf16[32,1664]{1,0:T(8,128)(2,1)S(1)}, u32[]{:S(2)}, u32[]{:S(2)}) collective-permute-start(bf16[32,1664]{1,0:T(8,128)(2,1)S(1)} %pad_maximum_fusion.6), channel_id=1, source_target_pairs={{0,10},{1,11},{2,8},{3,9},{4,14},{5,15},{6,12},{7,13},{8,2},{9,3},... | collective-permute-start | bytes 319496 | tf_op jit(solution)/shard_map/ppermute | solution.py:471
  13.9 12.5 %collective-permute-start.6 = (bf16[32,1664]{1,0:T(8,128)(2,1)S(1)}, bf16[32,1664]{1,0:T(8,128)(2,1)S(1)}, u32[]{:S(2)}, u32[]{:S(2)}) collective-permute-start(bf16[32,1664]{1,0:T(8,128)(2,1)S(1)} %pad_maximum_fusion.7), channel_id=1, source_target_pairs={{0,12},{1,13},{2,14},{3,15},{4,8},{5,9},{6,10},{7,11},{8,4},{9,5},... | collective-permute-start | bytes 319496 | tf_op jit(solution)/shard_map/ppermute | solution.py:471
  17.5 8.9 %collective-permute-start.7 = (bf16[32,1664]{1,0:T(8,128)(2,1)S(1)}, bf16[32,1664]{1,0:T(8,128)(2,1)S(1)}, u32[]{:S(2)}, u32[]{:S(2)}) collective-permute-start(bf16[32,1664]{1,0:T(8,128)(2,1)S(1)} %pad_maximum_fusion.8), channel_id=1, source_target_pairs={{0,14},{1,15},{2,12},{3,13},{4,10},{5,11},{6,8},{7,9},{8,6},{9,7},... | collective-permute-start | bytes 319496 | tf_op jit(solution)/shard_map/ppermute | solution.py:471
  27.6 21.1 %copy-start = (bf16[4,4,64,576]{3,2,1,0:T(8,128)(2,1)S(1)}, bf16[4,4,64,576]{3,2,1,0:T(8,128)(2,1)}, u32[]{:S(2)}) copy-start(bf16[4,4,64,576]{3,2,1,0:T(8,128)(2,1)} %queries_ref.1) | copy-start | bytes 3538948
  27.6 21.1 %copy-start.1 = (bf16[4,4,576]{2,1,0:T(4,128)(2,1)S(1)}, bf16[4,4,576]{2,1,0:T(4,128)(2,1)}, u32[]{:S(2)}) copy-start(bf16[4,4,576]{2,1,0:T(4,128)(2,1)} %fresh_ref.1) | copy-start | bytes 55300
  27.6 1.9 %collective-permute-start.11 = (bf16[128,1792]{1,0:T(8,128)(2,1)S(1)}, bf16[128,1792]{1,0:T(8,128)(2,1)S(1)}, u32[]{:S(2)}, u32[]{:S(2)}) collective-permute-start(bf16[128,1792]{1,0:T(8,128)(2,1)S(1)} %get-tuple-element.20), channel_id=1, source_target_pairs={{0,1},{1,0},{2,3},{3,2},{4,5},{5,4},{6,7},{7,6},{8,9},{9,8},{10,11... | collective-permute-start | bytes 1376264 | tf_op jit(solution)/shard_map/ppermute | solution.py:471
  28.8 4.9 %collective-permute-start.8 = (bf16[128,1792]{1,0:T(8,128)(2,1)S(1)}, bf16[128,1792]{1,0:T(8,128)(2,1)S(1)}, u32[]{:S(2)}, u32[]{:S(2)}) collective-permute-start(bf16[128,1792]{1,0:T(8,128)(2,1)S(1)} %get-tuple-element.18), channel_id=1, source_target_pairs={{0,1},{1,0},{2,3},{3,2},{4,5},{5,4},{6,7},{7,6},{8,9},{9,8},{10,11... | collective-permute-start | bytes 1376264 | tf_op jit(solution)/shard_map/ppermute | solution.py:471
  29.6 10.0 %collective-permute-start.12 = (bf16[64,1792]{1,0:T(8,128)(2,1)S(1)}, bf16[64,1792]{1,0:T(8,128)(2,1)S(1)}, u32[]{:S(2)}, u32[]{:S(2)}) collective-permute-start(bf16[64,1792]{1,0:T(8,128)(2,1)S(1)} %slice.148), channel_id=1, source_target_pairs={{0,4},{1,5},{2,6},{3,7},{4,0},{5,1},{6,2},{7,3},{8,12},{9,13},{10,... | collective-permute-start | bytes 688136 | tf_op jit(solution)/shard_map/ppermute | solution.py:471
  33.8 7.4 %collective-permute-start.9 = (bf16[64,1792]{1,0:T(8,128)(2,1)S(1)}, bf16[64,1792]{1,0:T(8,128)(2,1)S(1)}, u32[]{:S(2)}, u32[]{:S(2)}) collective-permute-start(bf16[64,1792]{1,0:T(8,128)(2,1)S(1)} %slice.149), channel_id=1, source_target_pairs={{0,2},{1,3},{2,0},{3,1},{4,6},{5,7},{6,4},{7,5},{8,10},{9,11},{10,... | collective-permute-start | bytes 688136 | tf_op jit(solution)/shard_map/ppermute | solution.py:471
  39.7 4.9 %collective-permute-start.13 = (bf16[32,1792]{1,0:T(8,128)(2,1)S(1)}, bf16[32,1792]{1,0:T(8,128)(2,1)S(1)}, u32[]{:S(2)}, u32[]{:S(2)}) collective-permute-start(bf16[32,1792]{1,0:T(8,128)(2,1)S(1)} %slice.150), channel_id=1, source_target_pairs={{0,2},{1,3},{2,0},{3,1},{4,6},{5,7},{6,4},{7,5},{8,10},{9,11},{10,... | collective-permute-start | bytes 344072 | tf_op jit(solution)/shard_map/ppermute | solution.py:471
  41.3 4.9 %collective-permute-start.10 = (bf16[32,1792]{1,0:T(8,128)(2,1)S(1)}, bf16[32,1792]{1,0:T(8,128)(2,1)S(1)}, u32[]{:S(2)}, u32[]{:S(2)}) collective-permute-start(bf16[32,1792]{1,0:T(8,128)(2,1)S(1)} %slice.151), channel_id=1, source_target_pairs={{0,4},{1,5},{2,6},{3,7},{4,0},{5,1},{6,2},{7,3},{8,12},{9,13},{10,... | collective-permute-start | bytes 344072 | tf_op jit(solution)/shard_map/ppermute | solution.py:471
  46.3 7.1 %collective-permute-start.14 = (bf16[16,3584]{1,0:T(8,128)(2,1)S(1)}, bf16[16,3584]{1,0:T(8,128)(2,1)S(1)}, u32[]{:S(2)}, u32[]{:S(2)}) collective-permute-start(bf16[16,3584]{1,0:T(8,128)(2,1)S(1)} %pad_maximum_fusion), channel_id=1, source_target_pairs={{0,8},{1,9},{2,10},{3,11},{4,12},{5,13},{6,14},{7,15},{8,0},{9,1},... | collective-permute-start | bytes 344072 | tf_op jit(solution)/shard_map/ppermute | solution.py:471

commit v4 on v3

--- a/solution.py
+++ b/solution.py
@@ -152,6 +152,8 @@
 
 
 BLOCK = 16
+CHIP_ORDER = (0, 4, 2, 6, 1, 5, 3, 7)
+EARLY = 5
 SCOPED_BYTES = 16 * 2**20
 
 
@@ -206,14 +208,12 @@
     lengths_ref,
     assignment_ref,
     kv_ref,
-    near_ref,
-    far_ref,
+    *out_refs,
 ):
     me = lax.axis_index("seq")
     devices = 2 * chips
-    half = near_ref.shape[0]
-    slots = 2 * half
-    room = slots // devices
+    room = out_refs[0].shape[0] // 2
+    slots = room * devices
     rows, steps, top = routes_ref.shape
     tokens = rows * steps
     lanes = tokens * top
@@ -225,14 +225,14 @@
     slot = lax.broadcasted_iota(jnp.int32, (slots, lanes), 0)
     lane = lax.broadcasted_iota(jnp.int32, (slots, lanes), 1)
     block = slot // room
-    target = me ^ (2 * (block % chips) + block // chips)
+    target = me ^ block
     pick = (lane // top == slot % room) & (route_row == target)
     scale = jnp.sum(jnp.where(pick, weight_row, 0.0), axis=1, keepdims=True)
     chosen = jnp.where(pick, 1.0, 0.0).astype(jnp.bfloat16)
     moved = jnp.dot(chosen, hidden_ref[...], preferred_element_type=jnp.float32)
     moved = (moved * scale).astype(jnp.bfloat16)
-    near_ref[:, :hidden_width] = moved[:half]
-    far_ref[:, :hidden_width] = moved[half:]
+    for chip in range(chips):
+        out_refs[chip][:, :hidden_width] = moved[2 * chip * room : 2 * (chip + 1) * room]
 
     requests = lengths_ref.shape[1]
     kv_width, here = kv_ref.shape
@@ -246,7 +246,7 @@
     slot = lax.broadcasted_iota(jnp.int32, (slots, requests), 0)
     decode = lax.broadcasted_iota(jnp.int32, (slots, requests), 1)
     block = slot // room
-    target = me ^ (2 * (block % chips) + block // chips)
+    target = me ^ block
     rank = slot % room - offset
     held = (target == decode // per_owner) & (rank >= 0) & (rank < count)
     source = jnp.sum(jnp.where(held, low + rank + 1, 0), axis=1, keepdims=True) - 1
@@ -258,11 +258,10 @@
         preferred_element_type=jnp.float32,
     ).astype(jnp.bfloat16)
     last = hidden_width + kv_width
-    empty = jnp.zeros((half, near_ref.shape[1] - last), jnp.bfloat16)
-    near_ref[:, hidden_width:last] = moved[:half]
-    far_ref[:, hidden_width:last] = moved[half:]
-    near_ref[:, last:] = empty
-    far_ref[:, last:] = empty
+    empty = jnp.zeros((2 * room, out_refs[0].shape[1] - last), jnp.bfloat16)
+    for chip in range(chips):
+        out_refs[chip][:, hidden_width:last] = moved[2 * chip * room : 2 * (chip + 1) * room]
+        out_refs[chip][:, last:] = empty
 
 
 def pack_outboxes(
@@ -283,7 +282,7 @@
     )
     return pl.pallas_call(
         functools.partial(outbox_kernel, devices // 2, rows),
-        out_shape=(jax.ShapeDtypeStruct((slots // 2, width), jnp.bfloat16),) * 2,
+        out_shape=(jax.ShapeDtypeStruct((2 * tokens, width), jnp.bfloat16),) * (devices // 2),
         compiler_params=pltpu.CompilerParams(vmem_limit_bytes=SCOPED_BYTES),
         cost_estimate=pl.CostEstimate(
             flops=2 * slots * (tokens * top * hidden_width + here * kv_width),
@@ -343,15 +342,28 @@
     )
 
 
+def blocks_of(chip, arrived_refs, crossed_refs):
+    place = CHIP_ORDER.index(chip)
+    late = place >= EARLY
+    start = (place - EARLY * late) * BLOCK
+    return (
+        (arrived_refs[place], slice(0, BLOCK)),
+        (crossed_refs[late], slice(start, start + BLOCK)),
+    )
+
+
 def attend_kernel(first, pieces, queries_ref, fresh_ref, tags_ref, *refs):
-    arrived_refs, out_ref, cache_ref = refs[:pieces], refs[pieces], refs[pieces + 1]
+    arrived_refs, crossed_refs = refs[:pieces], refs[pieces:-2]
+    out_ref, cache_ref = refs[-2:]
     mine = pl.program_id(0)
-    rows, width = arrived_refs[0].shape[0], cache_ref.shape[1]
+    latent_columns = slice(first, first + cache_ref.shape[1])
 
     @pl.when(mine == 0)
     def _():
-        for i, arrived_ref in enumerate(arrived_refs):
-            cache_ref[i * rows : (i + 1) * rows, :] = arrived_ref[:, first : first + width]
+        for chip in range(pieces):
+            for block, rows in enumerate(blocks_of(chip, arrived_refs, crossed_refs)):
+                start = (2 * chip + block) * BLOCK
+                cache_ref[start : start + BLOCK, :] = rows[0][rows[1], latent_columns]
 
     steps, _, heads, width = queries_ref.shape
     latent = out_ref.shape[3]
@@ -394,7 +406,7 @@
     out_ref[...] = context.reshape(steps, 1, heads, latent)
 
 
-def attend(queries, new_kv, arrived, first, tags):
+def attend(queries, new_kv, arrived, crossed, first, tags):
     steps, per_owner, heads, width = queries.shape
     slots = tags.shape[1]
     latent = width - ROPE
@@ -406,7 +418,7 @@
             pl.BlockSpec((steps, per_owner, width), lambda q: (0, 0, 0)),
             pl.BlockSpec((1, slots), lambda q: (0, 0)),
         ]
-        + [pl.BlockSpec(piece.shape, lambda q: (0, 0)) for piece in arrived],
+        + [pl.BlockSpec(piece.shape, lambda q: (0, 0)) for piece in arrived + crossed],
         out_specs=pl.BlockSpec((steps, 1, heads, latent), lambda q: (0, q, 0, 0)),
         out_shape=jax.ShapeDtypeStruct((steps, per_owner, heads, latent), jnp.bfloat16),
         scratch_shapes=[pltpu.VMEM((slots, width), jnp.bfloat16)],
@@ -417,51 +429,56 @@
             transcendentals=steps * per_owner * heads * slots,
         ),
         name="attend",
-    )(queries, new_kv, tags, *arrived)
-
-
-def expert_kernel(bits, first, pieces, down_ref, *refs):
-    arrived_refs, (keep_ref, send_ref, sorted_ref) = refs[:pieces], refs[pieces:]
-    half, width = keep_ref.shape
+    )(queries, new_kv, tags, *arrived, *crossed)
+
+
+def kept_kernel(orders, pieces, down_ref, *refs):
+    arrived_refs, out_refs, sorted_ref = refs[:pieces], refs[pieces:-1], refs[-1]
+    width = out_refs[0].shape[1]
     hidden_width = sorted_ref.shape[1]
-    per_piece = arrived_refs[0].shape[0] // BLOCK
-    for place in range(1 << len(bits)):
-        piece, block = divmod(apart_of(place, bits), per_piece)
-        sorted_ref[place * BLOCK : (place + 1) * BLOCK, :] = arrived_refs[piece][
-            block * BLOCK : (block + 1) * BLOCK, :hidden_width
-        ]
+    for part, (bits, out_ref) in enumerate(zip(orders, out_refs)):
+        for place in range(pieces):
+            ref, rows = blocks_of(apart_of(place, bits), arrived_refs, (None, None))[0]
+            sorted_ref[place * BLOCK : (place + 1) * BLOCK, :] = ref[rows, :hidden_width]
+        out_ref[...] = jnp.dot(
+            sorted_ref[...],
+            down_ref[0, :, part * width : (part + 1) * width],
+            preferred_element_type=jnp.float32,
+        )
+
+
+def sent_kernel(bits, first, pieces, down_ref, early_ref, late_ref, out_ref, sorted_ref):
+    width = out_ref.shape[1]
+    hidden_width = sorted_ref.shape[1]
+    for place in range(pieces):
+        ref, rows = blocks_of(apart_of(place, bits), (None,) * pieces, (early_ref, late_ref))[1]
+        sorted_ref[place * BLOCK : (place + 1) * BLOCK, :] = ref[rows, :hidden_width]
     result = jnp.dot(
         sorted_ref[...],
         down_ref[0, :, first : first + width],
         preferred_element_type=jnp.float32,
     )
-    keep_ref[...] = result[:half]
-    send_ref[...] = result[half:].astype(jnp.bfloat16)
-
-
-def expert_part(arrived, expert_down, bits, part, parts):
-    slots = BLOCK << len(bits)
+    out_ref[...] = result.astype(jnp.bfloat16)
+
+
+def expert_call(kernel, expert_down, arrays, pieces, outs, name):
     _, hidden_width, model_width = expert_down.shape
-    width = model_width // parts
-    half = slots // 2
+    slots = BLOCK * pieces
     vmem = pl.BlockSpec(memory_space=pltpu.VMEM)
     return pl.pallas_call(
-        functools.partial(expert_kernel, bits, part * width, len(arrived)),
-        in_specs=[vmem] * (1 + len(arrived)),
-        out_specs=[vmem] * 2,
-        out_shape=(
-            jax.ShapeDtypeStruct((half, width), jnp.float32),
-            jax.ShapeDtypeStruct((half, width), jnp.bfloat16),
-        ),
+        kernel,
+        in_specs=[vmem] * (1 + len(arrays)),
+        out_specs=[vmem] * len(outs),
+        out_shape=outs,
         scratch_shapes=[pltpu.VMEM((slots, hidden_width), jnp.bfloat16)],
         compiler_params=pltpu.CompilerParams(vmem_limit_bytes=SCOPED_BYTES),
         cost_estimate=pl.CostEstimate(
-            flops=2 * slots * hidden_width * width,
-            bytes_accessed=2 * hidden_width * width,
+            flops=2 * slots * hidden_width * sum(out.shape[1] for out in outs),
+            bytes_accessed=2 * hidden_width * sum(out.shape[1] for out in outs),
             transcendentals=0,
         ),
-        name="expert_part",
-    )(expert_down, *arrived)
+        name=name,
+    )(expert_down, *arrays)
 
 
 after = lax.optimization_barrier
@@ -492,35 +509,56 @@
     steps, per_owner = queries.shape[:2]
     rows, _, top, hidden_width = expert_hidden.shape
     model_width = expert_down.shape[2]
-    near, far = pack_outboxes(
+    outboxes = pack_outboxes(
         routes, route_weights, expert_hidden, lengths, assignment, prefill_kv, devices
     )
-    crossed = swap(far, 1, devices)
     chips = devices // 2
-    arrived = [None] * chips
-    for apart in (0, 4, 2, 6, 1, 5, 3, 7):
-        block = slice(apart * BLOCK, (apart + 1) * BLOCK)
-        piece = jnp.concatenate([near[block], crossed[block]], axis=0)
-        arrived[apart] = swap(piece, 2 * apart, devices) if apart else piece
-    late_lengths, _ = after((lengths, arrived[4]))
+    arrived = [
+        swap(outboxes[apart], 2 * apart, devices) if apart else outboxes[apart]
+        for apart in CHIP_ORDER
+    ]
+    late_lengths, _ = after((lengths, arrived[1]))
     tags, down = load_down(
         late_lengths, assignment, expert_down, devices, per_owner, devices * BLOCK
     )
-    context = attend(queries, new_kv, arrived, hidden_width, tags)
-
-    orders = ((1, 2, 4, 8), (1, 4, 2, 8))
+    late, _ = after((arrived[EARLY:], tags))
+    crossed = [
+        swap(jnp.concatenate([piece[BLOCK:] for piece in group], axis=0), 1, devices)
+        for group in (arrived[:EARLY], late)
+    ]
+    context = attend(queries, new_kv, arrived, crossed, hidden_width, tags)
+
+    orders = ((1, 2, 4), (2, 1, 4))
+    width = model_width // len(orders)
+    half = devices * BLOCK // 2
+    kept = expert_call(
+        functools.partial(kept_kernel, orders, chips),
+        down,
+        arrived,
+        chips,
+        (jax.ShapeDtypeStruct((half, width), jnp.float32),) * len(orders),
+        "expert_kept",
+    )
+    crossed, kept = after((crossed, kept))
     flows = []
     for part, bits in enumerate(orders):
-        kept, sent = expert_part(arrived, down, bits, part, len(orders))
-        flows.append((kept, swap(sent, bits[0], devices)))
+        (sent,) = expert_call(
+            functools.partial(sent_kernel, bits, part * width, chips),
+            down,
+            crossed,
+            chips,
+            (jax.ShapeDtypeStruct((half, width), jnp.bfloat16),),
+            "expert_sent",
+        )
+        flows.append((kept[part], swap(sent, 1, devices)))
     flows = [fold(kept, received) for kept, received in flows]
-    received = [swap(sent, bits[1], devices) for (_, sent), bits in zip(flows, orders)]
+    received = [swap(sent, 2 * bits[0], devices) for (_, sent), bits in zip(flows, orders)]
     flows = [fold(kept, got) for (kept, _), got in zip(flows, received)]
-    received = [swap(sent, bits[2], devices) for (_, sent), bits in zip(flows, orders)]
+    received = [swap(sent, 2 * bits[1], devices) for (_, sent), bits in zip(flows, orders)]
     flows = [fold(kept, got) for (kept, _), got in zip(flows, received)]
     kept = jnp.concatenate([kept for kept, _ in flows], axis=1)
     sent = jnp.concatenate([sent for _, sent in flows], axis=1)
-    received = swap(sent, orders[0][-1], devices)
+    received = swap(sent, 2 * orders[0][-1], devices)
     received, context = lax.optimization_barrier((received, context))
     moe_out = (kept + received.astype(jnp.float32)).astype(jnp.bfloat16)
     return context, moe_out.reshape(rows, steps, model_width)

time: 54.3 us -> 52.6 us (0.969)
  waiting for transfers between devices: 14.6 us -> 13.7 us
  starting transfers between devices: 25 us -> 24.2 us
    ppermute x15 -> x16, waiting for transfers between devices: 14.6 us -> 13.7 us  [swap(): return lax.ppermute(values, 'seq', [(i, i ^ bit) for i in range(devices)])]
    ppermute x15 -> x16, starting transfers between devices: 25 us -> 24.2 us  [swap(): return lax.ppermute(values, 'seq', [(i, i ^ bit) for i in range(devices)])]
    pallas_call x2 -> x3, Pallas kernels: 2.25 us -> 2.43 us  [expert_call(): pl.pallas_call(kernel, in_specs=[vmem] * (1 + len(arrays)), out_specs=[vm...]
  transfers between devices with their start and end apart: 15 -> 16, of which waited for: 8 -> 8; matrix products, arithmetic and copies ran while one was open for 1% -> 1% of each run, Pallas kernels for 18% -> 20%
where the time goes in v4:
time: 52.6 us; the launch traced here: 52.4 us
  starting transfers between devices  24.2 us (46%)
  waiting for transfers between devices  13.7 us (26%)
  Pallas kernels  12.5 us (24%)
  local copies, waits for them, and re-layouts  0.87 us (2%)
  between operations  0.85 us (2%)
    ppermute x16, starting transfers between devices, swap(): return lax.ppermute(values, 'seq', [(i, i ^ bit) for i in range(devices)])  24.2 us
    ppermute x16, waiting for transfers between devices, swap(): return lax.ppermute(values, 'seq', [(i, i ^ bit) for i in range(devices)])  13.7 us
    pallas_call x1, Pallas kernels, attend(): pl.pallas_call(functools.partial(attend_kernel, first, len(arrived)), gri...  4.7 us
    pallas_call x1, Pallas kernels, load_down(): pl.pallas_call(functools.partial(load_kernel, devices, per_owner), in_spe...  3.77 us
    pallas_call x3, Pallas kernels, expert_call(): pl.pallas_call(kernel, in_specs=[vmem] * (1 + len(arrays)), out_specs=[vm...  2.43 us
    pallas_call x1, Pallas kernels, pack_outboxes(): pl.pallas_call(functools.partial(outbox_kernel, devices // 2, rows), out_...  1.64 us
  transfers between devices with their start and end apart: 16, of which 8 were waited for; matrix products, arithmetic and copies ran while one was open for 1% of the time, Pallas kernels for 20%

profile of v4, /device:TPU:0, one launch (start us, length us, event | category | flops | bytes accessed | tf_op | source)
XLA Modules:
  0.0 52.4 jit_solution(11504045908193623392)
XLA Ops:
  0.6 1.6 %pack_outboxes.1 = (bf16[32,1664]{1,0:T(8,128)(2,1)S(1)}, bf16[32,1664]{1,0:T(8,128)(2,1)S(1)}, bf16[32,1664]{1,0:T(8,128)(2,1)S(1)}, bf16[32,1664]{1,0:T(8,128)...) custom-call(s32[4,4,8]{2,1,0:T(4,128)} %routes_ref.1, ...), custom_call_target="tpu_custom_call" | custom-call | flops 104857600 | bytes 1703936 | tf_op jit(solution)/shard_map/pack_outboxes/pallas_call | solution.py:283
  2.3 4.1 %collective-permute-start = (bf16[32,1664]{1,0:T(8,128)(2,1)S(1)}, bf16[32,1664]{1,0:T(8,128)(2,1)S(1)}, u32[]{:S(2)}, u32[]{:S(2)}) collective-permute-start(bf16[32,1664]{1,0:T(8,128)(2,1)S(1)} %get-tuple-element.25), channel_id=1, source_target_pairs={{0,8},{1,9},{2,10},{3,11},{4,12},{5,13},{6,14},{7,15},{8,0},{9,1},... | collective-permute-start | bytes 319496 | tf_op jit(solution)/shard_map/ppermute | solution.py:488
  6.4 1.6 %collective-permute-start.1 = (bf16[32,1664]{1,0:T(8,128)(2,1)S(1)}, bf16[32,1664]{1,0:T(8,128)(2,1)S(1)}, u32[]{:S(2)}, u32[]{:S(2)}) collective-permute-start(bf16[32,1664]{1,0:T(8,128)(2,1)S(1)} %get-tuple-element.26), channel_id=1, source_target_pairs={{0,4},{1,5},{2,6},{3,7},{4,0},{5,1},{6,2},{7,3},{8,12},{9,13},{10,... | collective-permute-start | bytes 319496 | tf_op jit(solution)/shard_map/ppermute | solution.py:488
  8.0 0.0 collective-permute-start.2
  8.0 1.7 %collective-permute-start.3 = (bf16[32,1664]{1,0:T(8,128)(2,1)S(1)}, bf16[32,1664]{1,0:T(8,128)(2,1)S(1)}, u32[]{:S(2)}, u32[]{:S(2)}) collective-permute-start(bf16[32,1664]{1,0:T(8,128)(2,1)S(1)} %get-tuple-element.28), channel_id=1, source_target_pairs={{0,2},{1,3},{2,0},{3,1},{4,6},{5,7},{6,4},{7,5},{8,10},{9,11},{10,... | collective-permute-start | bytes 319496 | tf_op jit(solution)/shard_map/ppermute | solution.py:488
  9.7 1.6 %collective-permute-start.5 = (bf16[32,1664]{1,0:T(8,128)(2,1)S(1)}, bf16[32,1664]{1,0:T(8,128)(2,1)S(1)}, u32[]{:S(2)}, u32[]{:S(2)}) collective-permute-start(bf16[32,1664]{1,0:T(8,128)(2,1)S(1)} %get-tuple-element.29), channel_id=1, source_target_pairs={{0,10},{1,11},{2,8},{3,9},{4,14},{5,15},{6,12},{7,13},{8,2},{9,3},... | collective-permute-start | bytes 319496 | tf_op jit(solution)/shard_map/ppermute | solution.py:488
  11.3 2.0 %collective-permute-done.refs_1_ = bf16[32,1664]{1,0:T(8,128)(2,1)S(1)} collective-permute-done((bf16[32,1664]{1,0:T(8,128)(2,1)S(1)}, bf16[32,1664]{1,0:T(8,128)(2,1)S(1)}, u32[]{:S(2)}, u32[]{:S(2)}) %collective-permute-start) | collective-permute-done | bytes 106528 | tf_op jit(solution)/shard_map/ppermute | solution.py:488
  13.3 1.5 %collective-permute-start.6 = (bf16[32,1664]{1,0:T(8,128)(2,1)S(1)}, bf16[32,1664]{1,0:T(8,128)(2,1)S(1)}, u32[]{:S(2)}, u32[]{:S(2)}) collective-permute-start(bf16[32,1664]{1,0:T(8,128)(2,1)S(1)} %get-tuple-element.30), channel_id=1, source_target_pairs={{0,6},{1,7},{2,4},{3,5},{4,2},{5,3},{6,0},{7,1},{8,14},{9,15},{10,... | collective-permute-start | bytes 319496 | tf_op jit(solution)/shard_map/ppermute | solution.py:488
  14.9 0.0 collective-permute-done.1.refs_2_
  14.9 5.1 %collective-permute-start.7 = (bf16[32,1664]{1,0:T(8,128)(2,1)S(1)}, bf16[32,1664]{1,0:T(8,128)(2,1)S(1)}, u32[]{:S(2)}, u32[]{:S(2)}) collective-permute-start(bf16[32,1664]{1,0:T(8,128)(2,1)S(1)} %get-tuple-element.31), channel_id=1, source_target_pairs={{0,14},{1,15},{2,12},{3,13},{4,10},{5,11},{6,8},{7,9},{8,6},{9,7},... | collective-permute-start | bytes 319496 | tf_op jit(solution)/shard_map/ppermute | solution.py:488
  20.0 0.0 collective-permute-done.2.refs_3_
  20.0 0.0 collective-permute-done.3.refs_4_
  20.0 0.1 collective-permute-start.4
  20.1 3.8 %load_down.1 = (s32[1,256]{1,0:T(1,128)S(1)}, bf16[1,1024,3584]{2,1,0:T(8,128)(2,1)S(1)}) custom-call(s32[1,64]{1,0:T(1,128)} %bitcast.8, s32[1,64]{1,0:T(1,128)} %bitcast.10, bf16[1,1024,3584]{2,1,0:T(8,128)(2,1)} %down_ref.1), custom_call_target="tpu_custom_call" | custom-call | bytes 7340032 | tf_op jit(solution)/shard_map/load_down/pallas_call | solution.py:324
  23.9 1.2 %collective-permute-done.5.refs_5_ = bf16[32,1664]{1,0:T(8,128)(2,1)S(1)} collective-permute-done((bf16[32,1664]{1,0:T(8,128)(2,1)S(1)}, bf16[32,1664]{1,0:T(8,128)(2,1)S(1)}, u32[]{:S(2)}, u32[]{:S(2)}) %collective-permute-start.5) | collective-permute-done | bytes 106528 | tf_op jit(solution)/shard_map/ppermute | solution.py:488
  25.1 0.0 collective-permute-done.6.refs_6_
  25.1 0.0 collective-permute-done.7.refs_7_
  25.2 0.1 collective-permute-start.8
  25.2 1.1 %expert_kept.1 = (f32[128,1792]{1,0:T(8,128)S(1)}, f32[128,1792]{1,0:T(8,128)S(1)}) custom-call(bf16[1,1024,3584]{2,1,0:T(8,128)(2,1)S(1)} %get-tuple-element.37.down_ref, bf16[32,1664]{1,0:T(8,128)(2,1)S(1)} %get-tuple-element.24.refs_0_, bf16[32,1664]{1,0:T(8,128)(2,1)S(1)} %collective-permute-done.refs_1_, ...), custom_call_target="tpu_custom_call" | custom-call | flops 939524096 | bytes 7340032 | tf_op jit(solution)/shard_map/expert_kept/pallas_call | solution.py:468
  26.4 0.2 collective-permute-done.8.late_ref.refs_9_
  26.6 0.0 collective-permute-done.4.early_ref.refs_8_
  26.6 0.6 %expert_sent.2 = bf16[128,1792]{1,0:T(8,128)(2,1)S(1)} custom-call(bf16[1,1024,3584]{2,1,0:T(8,128)(2,1)S(1)} %get-tuple-element.37.down_ref, bf16[80,1664]{1,0:T(8,128)(2,1)S(1)} %collective-permute-done.4.early_ref.refs_8_, bf16[48,1664]{1,0:T(8,128)(2,1)S(1)} %collective-permute-done.8.late_ref.refs_9_), custom_call_target="tpu_custom_call" | custom-call | flops 469762048 | bytes 3670016 | tf_op jit(solution)/shard_map/expert_sent/pallas_call | solution.py:468
  27.3 0.0 copy-start
  27.3 0.0 copy-start.1
  27.3 0.3 collective-permute-start.9
  27.7 0.6 %expert_sent.3 = bf16[128,1792]{1,0:T(8,128)(2,1)S(1)} custom-call(bf16[1,1024,3584]{2,1,0:T(8,128)(2,1)S(1)} %get-tuple-element.37.down_ref, bf16[80,1664]{1,0:T(8,128)(2,1)S(1)} %collective-permute-done.4.early_ref.refs_8_, bf16[48,1664]{1,0:T(8,128)(2,1)S(1)} %collective-permute-done.8.late_ref.refs_9_), custom_call_target="tpu_custom_call" | custom-call | flops 469762048 | bytes 3670016 | tf_op jit(solution)/shard_map/expert_sent/pallas_call | solution.py:468
  28.3 0.3 collective-permute-start.12
  28.6 0.6 %collective-permute-done.9 = bf16[128,1792]{1,0:T(8,128)(2,1)S(1)} collective-permute-done((bf16[128,1792]{1,0:T(8,128)(2,1)S(1)}, bf16[128,1792]{1,0:T(8,128)(2,1)S(1)}, u32[]{:S(2)}, u32[]{:S(2)}) %collective-permute-start.9) | collective-permute-done | bytes 458784 | tf_op jit(solution)/shard_map/ppermute | solution.py:488
  29.2 0.1 convert_add_fusion.1
  29.3 0.3 collective-permute-start.10
  29.6 0.6 %collective-permute-done.12 = bf16[128,1792]{1,0:T(8,128)(2,1)S(1)} collective-permute-done((bf16[128,1792]{1,0:T(8,128)(2,1)S(1)}, bf16[128,1792]{1,0:T(8,128)(2,1)S(1)}, u32[]{:S(2)}, u32[]{:S(2)}) %collective-permute-start.12) | collective-permute-done | bytes 458784 | tf_op jit(solution)/shard_map/ppermute | solution.py:488
  30.2 0.1 convert_add_fusion
  30.3 1.8 %collective-permute-start.13 = (bf16[64,1792]{1,0:T(8,128)(2,1)S(1)}, bf16[64,1792]{1,0:T(8,128)(2,1)S(1)}, u32[]{:S(2)}, u32[]{:S(2)}) collective-permute-start(bf16[64,1792]{1,0:T(8,128)(2,1)S(1)} %slice.117), channel_id=1, source_target_pairs={{0,4},{1,5},{2,6},{3,7},{4,0},{5,1},{6,2},{7,3},{8,12},{9,13},{10,... | collective-permute-start | bytes 688136 | tf_op jit(solution)/shard_map/ppermute | solution.py:488
  32.1 5.0 %collective-permute-done.10 = bf16[64,1792]{1,0:T(8,128)(2,1)S(1)} collective-permute-done((bf16[64,1792]{1,0:T(8,128)(2,1)S(1)}, bf16[64,1792]{1,0:T(8,128)(2,1)S(1)}, u32[]{:S(2)}, u32[]{:S(2)}) %collective-permute-start.10) | collective-permute-done | bytes 229408 | tf_op jit(solution)/shard_map/ppermute | solution.py:488
  37.2 1.8 %collective-permute-start.11 = (bf16[32,1792]{1,0:T(8,128)(2,1)S(1)}, bf16[32,1792]{1,0:T(8,128)(2,1)S(1)}, u32[]{:S(2)}, u32[]{:S(2)}) collective-permute-start(bf16[32,1792]{1,0:T(8,128)(2,1)S(1)} %slice.120), channel_id=1, source_target_pairs={{0,4},{1,5},{2,6},{3,7},{4,0},{5,1},{6,2},{7,3},{8,12},{9,13},{10,... | collective-permute-start | bytes 344072 | tf_op jit(solution)/shard_map/ppermute | solution.py:488
  39.1 0.0 collective-permute-done.13
  39.1 0.1 slice_add_fusion
  39.2 0.7 %collective-permute-start.14 = (bf16[32,1792]{1,0:T(8,128)(2,1)S(1)}, bf16[32,1792]{1,0:T(8,128)(2,1)S(1)}, u32[]{:S(2)}, u32[]{:S(2)}) collective-permute-start(bf16[32,1792]{1,0:T(8,128)(2,1)S(1)} %slice.119), channel_id=1, source_target_pairs={{0,2},{1,3},{2,0},{3,1},{4,6},{5,7},{6,4},{7,5},{8,10},{9,11},{10,... | collective-permute-start | bytes 344072 | tf_op jit(solution)/shard_map/ppermute | solution.py:488
  39.9 2.2 %collective-permute-done.11 = bf16[32,1792]{1,0:T(8,128)(2,1)S(1)} collective-permute-done((bf16[32,1792]{1,0:T(8,128)(2,1)S(1)}, bf16[32,1792]{1,0:T(8,128)(2,1)S(1)}, u32[]{:S(2)}, u32[]{:S(2)}) %collective-permute-start.11) | collective-permute-done | bytes 114720 | tf_op jit(solution)/shard_map/ppermute | solution.py:488
  42.1 1.9 %collective-permute-done.14 = bf16[32,1792]{1,0:T(8,128)(2,1)S(1)} collective-permute-done((bf16[32,1792]{1,0:T(8,128)(2,1)S(1)}, bf16[32,1792]{1,0:T(8,128)(2,1)S(1)}, u32[]{:S(2)}, u32[]{:S(2)}) %collective-permute-start.14) | collective-permute-done | bytes 114720 | tf_op jit(solution)/shard_map/ppermute | solution.py:488
  44.1 2.9 %collective-permute-start.15 = (bf16[16,3584]{1,0:T(8,128)(2,1)S(1)}, bf16[16,3584]{1,0:T(8,128)(2,1)S(1)}, u32[]{:S(2)}, u32[]{:S(2)}) collective-permute-start(bf16[16,3584]{1,0:T(8,128)(2,1)S(1)} %pad_maximum_fusion.1), channel_id=1, source_target_pairs={{0,8},{1,9},{2,10},{3,11},{4,12},{5,13},{6,14},{7,15},{8,0},{9,1},... | collective-permute-start | bytes 344072 | tf_op jit(solution)/shard_map/ppermute | solution.py:488
  47.0 0.0 copy-done
  47.0 0.0 copy-done.1
  47.0 4.7 %attend.1 = bf16[4,4,64,512]{3,2,1,0:T(8,128)(2,1)} custom-call(bf16[4,4,64,576]{3,2,1,0:T(8,128)(2,1)S(1)} %copy-done, bf16[4,4,576]{2,1,0:T(4,128)(2,1)S(1)} %copy-done.1, s32[1,256]{1,0:T(1,128)S(1)} %get-tuple-element.33.tags_ref, bf16[32,1664]{1,0:T(8,128)(2,1)S(1)} %get-tuple-element.24.refs_0_, bf16[32,1664]{1,0:T(8,128)(2,1)S(1)} %collective-permute-done.refs_1_, ...), custom_call_target="tpu_custom_call" | custom-call | flops 570425344 | bytes 2228224 | tf_op jit(solution)/shard_map/attend/pallas_call | solution.py:413
  51.7 0.0 collective-permute-done.15
  51.8 0.7 %reshape.24 = bf16[4,4,3584]{2,1,0:T(4,128)(2,1)} reshape(bf16[16,3584]{1,0:T(8,128)(2,1)S(1)} %fusion) | data formatting | bytes 229376 | tf_op jit(solution)/shard_map/reshape | solution.py:564
  (22 shorter events, 0.3 us)
Async XLA Ops:
  2.3 11.0 %collective-permute-start = (bf16[32,1664]{1,0:T(8,128)(2,1)S(1)}, bf16[32,1664]{1,0:T(8,128)(2,1)S(1)}, u32[]{:S(2)}, u32[]{:S(2)}) collective-permute-start(bf16[32,1664]{1,0:T(8,128)(2,1)S(1)} %get-tuple-element.25), channel_id=1, source_target_pairs={{0,8},{1,9},{2,10},{3,11},{4,12},{5,13},{6,14},{7,15},{8,0},{9,1},... | collective-permute-start | bytes 319496 | tf_op jit(solution)/shard_map/ppermute | solution.py:488
  6.4 8.5 %collective-permute-start.1 = (bf16[32,1664]{1,0:T(8,128)(2,1)S(1)}, bf16[32,1664]{1,0:T(8,128)(2,1)S(1)}, u32[]{:S(2)}, u32[]{:S(2)}) collective-permute-start(bf16[32,1664]{1,0:T(8,128)(2,1)S(1)} %get-tuple-element.26), channel_id=1, source_target_pairs={{0,4},{1,5},{2,6},{3,7},{4,0},{5,1},{6,2},{7,3},{8,12},{9,13},{10,... | collective-permute-start | bytes 319496 | tf_op jit(solution)/shard_map/ppermute | solution.py:488
  8.0 12.0 %collective-permute-start.2 = (bf16[32,1664]{1,0:T(8,128)(2,1)S(1)}, bf16[32,1664]{1,0:T(8,128)(2,1)S(1)}, u32[]{:S(2)}, u32[]{:S(2)}) collective-permute-start(bf16[32,1664]{1,0:T(8,128)(2,1)S(1)} %get-tuple-element.27), channel_id=1, source_target_pairs={{0,12},{1,13},{2,14},{3,15},{4,8},{5,9},{6,10},{7,11},{8,4},{9,5},... | collective-permute-start | bytes 319496 | tf_op jit(solution)/shard_map/ppermute | solution.py:488
  8.0 12.1 %collective-permute-start.3 = (bf16[32,1664]{1,0:T(8,128)(2,1)S(1)}, bf16[32,1664]{1,0:T(8,128)(2,1)S(1)}, u32[]{:S(2)}, u32[]{:S(2)}) collective-permute-start(bf16[32,1664]{1,0:T(8,128)(2,1)S(1)} %get-tuple-element.28), channel_id=1, source_target_pairs={{0,2},{1,3},{2,0},{3,1},{4,6},{5,7},{6,4},{7,5},{8,10},{9,11},{10,... | collective-permute-start | bytes 319496 | tf_op jit(solution)/shard_map/ppermute | solution.py:488
  9.7 15.4 %collective-permute-start.5 = (bf16[32,1664]{1,0:T(8,128)(2,1)S(1)}, bf16[32,1664]{1,0:T(8,128)(2,1)S(1)}, u32[]{:S(2)}, u32[]{:S(2)}) collective-permute-start(bf16[32,1664]{1,0:T(8,128)(2,1)S(1)} %get-tuple-element.29), channel_id=1, source_target_pairs={{0,10},{1,11},{2,8},{3,9},{4,14},{5,15},{6,12},{7,13},{8,2},{9,3},... | collective-permute-start | bytes 319496 | tf_op jit(solution)/shard_map/ppermute | solution.py:488
  13.3 11.8 %collective-permute-start.6 = (bf16[32,1664]{1,0:T(8,128)(2,1)S(1)}, bf16[32,1664]{1,0:T(8,128)(2,1)S(1)}, u32[]{:S(2)}, u32[]{:S(2)}) collective-permute-start(bf16[32,1664]{1,0:T(8,128)(2,1)S(1)} %get-tuple-element.30), channel_id=1, source_target_pairs={{0,6},{1,7},{2,4},{3,5},{4,2},{5,3},{6,0},{7,1},{8,14},{9,15},{10,... | collective-permute-start | bytes 319496 | tf_op jit(solution)/shard_map/ppermute | solution.py:488
  14.9 10.2 %collective-permute-start.7 = (bf16[32,1664]{1,0:T(8,128)(2,1)S(1)}, bf16[32,1664]{1,0:T(8,128)(2,1)S(1)}, u32[]{:S(2)}, u32[]{:S(2)}) collective-permute-start(bf16[32,1664]{1,0:T(8,128)(2,1)S(1)} %get-tuple-element.31), channel_id=1, source_target_pairs={{0,14},{1,15},{2,12},{3,13},{4,10},{5,11},{6,8},{7,9},{8,6},{9,7},... | collective-permute-start | bytes 319496 | tf_op jit(solution)/shard_map/ppermute | solution.py:488
  20.0 6.6 %collective-permute-start.4 = (bf16[80,1664]{1,0:T(8,128)(2,1)S(1)}, bf16[80,1664]{1,0:T(8,128)(2,1)S(1)}, u32[]{:S(2)}, u32[]{:S(2)}) collective-permute-start(bf16[80,1664]{1,0:T(8,128)(2,1)S(1)} %slice_dynamic-update-slice_fusion), channel_id=1, source_target_pairs={{0,1},{1,0},{2,3},{3,2},{4,5},{5,4},{6,7},{7,6},{8,9},{9,8},{10,11... | collective-permute-start | bytes 798728 | tf_op jit(solution)/shard_map/ppermute | solution.py:488
  25.2 1.5 %collective-permute-start.8 = (bf16[48,1664]{1,0:T(8,128)(2,1)S(1)}, bf16[48,1664]{1,0:T(8,128)(2,1)S(1)}, u32[]{:S(2)}, u32[]{:S(2)}) collective-permute-start(bf16[48,1664]{1,0:T(8,128)(2,1)S(1)} %pad_maximum_fusion), channel_id=1, source_target_pairs={{0,1},{1,0},{2,3},{3,2},{4,5},{5,4},{6,7},{7,6},{8,9},{9,8},{10,11... | collective-permute-start | bytes 479240 | tf_op jit(solution)/shard_map/ppermute | solution.py:488
  27.3 19.7 %copy-start = (bf16[4,4,64,576]{3,2,1,0:T(8,128)(2,1)S(1)}, bf16[4,4,64,576]{3,2,1,0:T(8,128)(2,1)}, u32[]{:S(2)}) copy-start(bf16[4,4,64,576]{3,2,1,0:T(8,128)(2,1)} %queries_ref.1) | copy-start | bytes 3538948
  27.3 19.7 %copy-start.1 = (bf16[4,4,576]{2,1,0:T(4,128)(2,1)S(1)}, bf16[4,4,576]{2,1,0:T(4,128)(2,1)}, u32[]{:S(2)}) copy-start(bf16[4,4,576]{2,1,0:T(4,128)(2,1)} %fresh_ref.1) | copy-start | bytes 55300
  27.3 1.9 %collective-permute-start.9 = (bf16[128,1792]{1,0:T(8,128)(2,1)S(1)}, bf16[128,1792]{1,0:T(8,128)(2,1)S(1)}, u32[]{:S(2)}, u32[]{:S(2)}) collective-permute-start(bf16[128,1792]{1,0:T(8,128)(2,1)S(1)} %expert_sent.2), channel_id=1, source_target_pairs={{0,1},{1,0},{2,3},{3,2},{4,5},{5,4},{6,7},{7,6},{8,9},{9,8},{10,11... | collective-permute-start | bytes 1376264 | tf_op jit(solution)/shard_map/ppermute | solution.py:488
  28.3 1.9 %collective-permute-start.12 = (bf16[128,1792]{1,0:T(8,128)(2,1)S(1)}, bf16[128,1792]{1,0:T(8,128)(2,1)S(1)}, u32[]{:S(2)}, u32[]{:S(2)}) collective-permute-start(bf16[128,1792]{1,0:T(8,128)(2,1)S(1)} %expert_sent.3), channel_id=1, source_target_pairs={{0,1},{1,0},{2,3},{3,2},{4,5},{5,4},{6,7},{7,6},{8,9},{9,8},{10,11... | collective-permute-start | bytes 1376264 | tf_op jit(solution)/shard_map/ppermute | solution.py:488
  29.3 7.9 %collective-permute-start.10 = (bf16[64,1792]{1,0:T(8,128)(2,1)S(1)}, bf16[64,1792]{1,0:T(8,128)(2,1)S(1)}, u32[]{:S(2)}, u32[]{:S(2)}) collective-permute-start(bf16[64,1792]{1,0:T(8,128)(2,1)S(1)} %slice.118), channel_id=1, source_target_pairs={{0,2},{1,3},{2,0},{3,1},{4,6},{5,7},{6,4},{7,5},{8,10},{9,11},{10,... | collective-permute-start | bytes 688136 | tf_op jit(solution)/shard_map/ppermute | solution.py:488
  30.3 8.8 %collective-permute-start.13 = (bf16[64,1792]{1,0:T(8,128)(2,1)S(1)}, bf16[64,1792]{1,0:T(8,128)(2,1)S(1)}, u32[]{:S(2)}, u32[]{:S(2)}) collective-permute-start(bf16[64,1792]{1,0:T(8,128)(2,1)S(1)} %slice.117), channel_id=1, source_target_pairs={{0,4},{1,5},{2,6},{3,7},{4,0},{5,1},{6,2},{7,3},{8,12},{9,13},{10,... | collective-permute-start | bytes 688136 | tf_op jit(solution)/shard_map/ppermute | solution.py:488
  37.2 4.9 %collective-permute-start.11 = (bf16[32,1792]{1,0:T(8,128)(2,1)S(1)}, bf16[32,1792]{1,0:T(8,128)(2,1)S(1)}, u32[]{:S(2)}, u32[]{:S(2)}) collective-permute-start(bf16[32,1792]{1,0:T(8,128)(2,1)S(1)} %slice.120), channel_id=1, source_target_pairs={{0,4},{1,5},{2,6},{3,7},{4,0},{5,1},{6,2},{7,3},{8,12},{9,13},{10,... | collective-permute-start | bytes 344072 | tf_op jit(solution)/shard_map/ppermute | solution.py:488
  39.2 4.9 %collective-permute-start.14 = (bf16[32,1792]{1,0:T(8,128)(2,1)S(1)}, bf16[32,1792]{1,0:T(8,128)(2,1)S(1)}, u32[]{:S(2)}, u32[]{:S(2)}) collective-permute-start(bf16[32,1792]{1,0:T(8,128)(2,1)S(1)} %slice.119), channel_id=1, source_target_pairs={{0,2},{1,3},{2,0},{3,1},{4,6},{5,7},{6,4},{7,5},{8,10},{9,11},{10,... | collective-permute-start | bytes 344072 | tf_op jit(solution)/shard_map/ppermute | solution.py:488
  44.1 7.6 %collective-permute-start.15 = (bf16[16,3584]{1,0:T(8,128)(2,1)S(1)}, bf16[16,3584]{1,0:T(8,128)(2,1)S(1)}, u32[]{:S(2)}, u32[]{:S(2)}) collective-permute-start(bf16[16,3584]{1,0:T(8,128)(2,1)S(1)} %pad_maximum_fusion.1), channel_id=1, source_target_pairs={{0,8},{1,9},{2,10},{3,11},{4,12},{5,13},{6,14},{7,15},{8,0},{9,1},... | collective-permute-start | bytes 344072 | tf_op jit(solution)/shard_map/ppermute | solution.py:488

commit v5 on v4

--- a/solution.py
+++ b/solution.py
@@ -152,6 +152,7 @@
 
 
 BLOCK = 16
+LANES = 128
 CHIP_ORDER = (0, 4, 2, 6, 1, 5, 3, 7)
 EARLY = 5
 SCOPED_BYTES = 16 * 2**20
@@ -212,7 +213,7 @@
 ):
     me = lax.axis_index("seq")
     devices = 2 * chips
-    room = out_refs[0].shape[0] // 2
+    room = BLOCK
     slots = room * devices
     rows, steps, top = routes_ref.shape
     tokens = rows * steps
@@ -231,11 +232,17 @@
     chosen = jnp.where(pick, 1.0, 0.0).astype(jnp.bfloat16)
     moved = jnp.dot(chosen, hidden_ref[...], preferred_element_type=jnp.float32)
     moved = (moved * scale).astype(jnp.bfloat16)
-    for chip in range(chips):
-        out_refs[chip][:, :hidden_width] = moved[2 * chip * room : 2 * (chip + 1) * room]
+    kv_width, here = kv_ref.shape
+    tiles = (hidden_width + kv_width) // LANES
+    for chip, out_ref in enumerate(out_refs):
+        for block in range(2):
+            start = (2 * chip + block) * room
+            for tile in range(hidden_width // LANES):
+                out_ref[(block * tiles + tile) * room : (block * tiles + tile + 1) * room, :] = (
+                    moved[start : start + room, tile * LANES : (tile + 1) * LANES]
+                )
 
     requests = lengths_ref.shape[1]
-    kv_width, here = kv_ref.shape
     before, after_last = request_spans(lengths_ref, assignment_ref)
     low = ceil_rows(before, me, devices)
     count = ceil_rows(after_last, me, devices) - low
@@ -257,11 +264,18 @@
         (((1,), (1,)), ((), ())),
         preferred_element_type=jnp.float32,
     ).astype(jnp.bfloat16)
-    last = hidden_width + kv_width
-    empty = jnp.zeros((2 * room, out_refs[0].shape[1] - last), jnp.bfloat16)
-    for chip in range(chips):
-        out_refs[chip][:, hidden_width:last] = moved[2 * chip * room : 2 * (chip + 1) * room]
-        out_refs[chip][:, last:] = empty
+    whole = kv_width // LANES
+    for chip, out_ref in enumerate(out_refs):
+        ends = []
+        for block in range(2):
+            start = (2 * chip + block) * room
+            for tile in range(whole):
+                place = (block + 1) * tiles - whole + tile
+                out_ref[place * room : (place + 1) * room, :] = moved[
+                    start : start + room, tile * LANES : (tile + 1) * LANES
+                ]
+            ends.append(moved[start : start + room, whole * LANES :])
+        out_ref[2 * tiles * room :, :] = jnp.concatenate(ends, axis=1)
 
 
 def pack_outboxes(
@@ -271,7 +285,7 @@
     here, kv_width = prefill_kv.shape
     tokens = rows * steps
     slots = tokens * devices
-    width = pl.cdiv(hidden_width + kv_width, 128) * 128
+    tiles = (hidden_width + kv_width) // LANES
     operands = (
         routes,
         route_weights,
@@ -282,11 +296,12 @@
     )
     return pl.pallas_call(
         functools.partial(outbox_kernel, devices // 2, rows),
-        out_shape=(jax.ShapeDtypeStruct((2 * tokens, width), jnp.bfloat16),) * (devices // 2),
+        out_shape=(jax.ShapeDtypeStruct(((2 * tiles + 1) * tokens, LANES), jnp.bfloat16),)
+        * (devices // 2),
         compiler_params=pltpu.CompilerParams(vmem_limit_bytes=SCOPED_BYTES),
         cost_estimate=pl.CostEstimate(
             flops=2 * slots * (tokens * top * hidden_width + here * kv_width),
-            bytes_accessed=4 * slots * width,
+            bytes_accessed=4 * slots * (hidden_width + kv_width),
             transcendentals=0,
         ),
         name="pack_outboxes",
@@ -342,28 +357,42 @@
     )
 
 
-def blocks_of(chip, arrived_refs, crossed_refs):
+def blocks_of(chip, arrived_refs, crossed_refs, tiles):
     place = CHIP_ORDER.index(chip)
     late = place >= EARLY
-    start = (place - EARLY * late) * BLOCK
-    return (
-        (arrived_refs[place], slice(0, BLOCK)),
-        (crossed_refs[late], slice(start, start + BLOCK)),
-    )
+    start = (place - EARLY * late) * (tiles + 1) * BLOCK
+    return (arrived_refs[place], 0, tiles * BLOCK), (crossed_refs[late], start, 0)
+
+
+def copy_tiles(ref, start, first, count, to_ref, place):
+    for tile in range(count):
+        at = start + (first + tile) * BLOCK
+        to_ref[place * BLOCK : (place + 1) * BLOCK, tile * LANES : (tile + 1) * LANES] = ref[
+            at : at + BLOCK, :
+        ]
 
 
 def attend_kernel(first, pieces, queries_ref, fresh_ref, tags_ref, *refs):
     arrived_refs, crossed_refs = refs[:pieces], refs[pieces:-2]
     out_ref, cache_ref = refs[-2:]
     mine = pl.program_id(0)
-    latent_columns = slice(first, first + cache_ref.shape[1])
+    kv_width = cache_ref.shape[1]
+    whole = kv_width // LANES
+    tiles = first // LANES + whole
 
     @pl.when(mine == 0)
     def _():
         for chip in range(pieces):
-            for block, rows in enumerate(blocks_of(chip, arrived_refs, crossed_refs)):
-                start = (2 * chip + block) * BLOCK
-                cache_ref[start : start + BLOCK, :] = rows[0][rows[1], latent_columns]
+            for block, (ref, start, gap) in enumerate(
+                blocks_of(chip, arrived_refs, crossed_refs, tiles)
+            ):
+                place = 2 * chip + block
+                copy_tiles(ref, start, tiles - whole, whole, cache_ref, place)
+                end = start + tiles * BLOCK + gap
+                side = block * (kv_width - whole * LANES)
+                cache_ref[place * BLOCK : (place + 1) * BLOCK, whole * LANES :] = ref[
+                    end : end + BLOCK, side : side + kv_width - whole * LANES
+                ]
 
     steps, _, heads, width = queries_ref.shape
     latent = out_ref.shape[3]
@@ -432,14 +461,14 @@
     )(queries, new_kv, tags, *arrived, *crossed)
 
 
-def kept_kernel(orders, pieces, down_ref, *refs):
+def kept_kernel(orders, pieces, tiles, down_ref, *refs):
     arrived_refs, out_refs, sorted_ref = refs[:pieces], refs[pieces:-1], refs[-1]
     width = out_refs[0].shape[1]
     hidden_width = sorted_ref.shape[1]
     for part, (bits, out_ref) in enumerate(zip(orders, out_refs)):
         for place in range(pieces):
-            ref, rows = blocks_of(apart_of(place, bits), arrived_refs, (None, None))[0]
-            sorted_ref[place * BLOCK : (place + 1) * BLOCK, :] = ref[rows, :hidden_width]
+            ref, start, _ = blocks_of(apart_of(place, bits), arrived_refs, (None,) * 2, tiles)[0]
+            copy_tiles(ref, start, 0, hidden_width // LANES, sorted_ref, place)
         out_ref[...] = jnp.dot(
             sorted_ref[...],
             down_ref[0, :, part * width : (part + 1) * width],
@@ -447,12 +476,16 @@
         )
 
 
-def sent_kernel(bits, first, pieces, down_ref, early_ref, late_ref, out_ref, sorted_ref):
+def sent_kernel(
+    bits, first, pieces, tiles, down_ref, early_ref, late_ref, out_ref, sorted_ref
+):
     width = out_ref.shape[1]
     hidden_width = sorted_ref.shape[1]
     for place in range(pieces):
-        ref, rows = blocks_of(apart_of(place, bits), (None,) * pieces, (early_ref, late_ref))[1]
-        sorted_ref[place * BLOCK : (place + 1) * BLOCK, :] = ref[rows, :hidden_width]
+        ref, start, _ = blocks_of(
+            apart_of(place, bits), (None,) * pieces, (early_ref, late_ref), tiles
+        )[1]
+        copy_tiles(ref, start, 0, hidden_width // LANES, sorted_ref, place)
     result = jnp.dot(
         sorted_ref[...],
         down_ref[0, :, first : first + width],
@@ -513,6 +546,7 @@
         routes, route_weights, expert_hidden, lengths, assignment, prefill_kv, devices
     )
     chips = devices // 2
+    tiles = (hidden_width + prefill_kv.shape[1]) // LANES
     arrived = [
         swap(outboxes[apart], 2 * apart, devices) if apart else outboxes[apart]
         for apart in CHIP_ORDER
@@ -523,16 +557,15 @@
     )
     late, _ = after((arrived[EARLY:], tags))
     crossed = [
-        swap(jnp.concatenate([piece[BLOCK:] for piece in group], axis=0), 1, devices)
+        swap(jnp.concatenate([rows[tiles * BLOCK :] for rows in group], axis=0), 1, devices)
         for group in (arrived[:EARLY], late)
     ]
-    context = attend(queries, new_kv, arrived, crossed, hidden_width, tags)
 
     orders = ((1, 2, 4), (2, 1, 4))
     width = model_width // len(orders)
     half = devices * BLOCK // 2
     kept = expert_call(
-        functools.partial(kept_kernel, orders, chips),
+        functools.partial(kept_kernel, orders, chips, tiles),
         down,
         arrived,
         chips,
@@ -543,7 +576,7 @@
     flows = []
     for part, bits in enumerate(orders):
         (sent,) = expert_call(
-            functools.partial(sent_kernel, bits, part * width, chips),
+            functools.partial(sent_kernel, bits, part * width, chips, tiles),
             down,
             crossed,
             chips,
@@ -553,13 +586,15 @@
         flows.append((kept[part], swap(sent, 1, devices)))
     flows = [fold(kept, received) for kept, received in flows]
     received = [swap(sent, 2 * bits[0], devices) for (_, sent), bits in zip(flows, orders)]
+    late_tags, _ = after((tags, [sent for _, sent in flows]))
+    context = attend(queries, new_kv, arrived, crossed, hidden_width, late_tags)
+    received[1], _ = after((received[1], context))
     flows = [fold(kept, got) for (kept, _), got in zip(flows, received)]
     received = [swap(sent, 2 * bits[1], devices) for (_, sent), bits in zip(flows, orders)]
     flows = [fold(kept, got) for (kept, _), got in zip(flows, received)]
     kept = jnp.concatenate([kept for kept, _ in flows], axis=1)
     sent = jnp.concatenate([sent for _, sent in flows], axis=1)
     received = swap(sent, 2 * orders[0][-1], devices)
-    received, context = lax.optimization_barrier((received, context))
     moe_out = (kept + received.astype(jnp.float32)).astype(jnp.bfloat16)
     return context, moe_out.reshape(rows, steps, model_width)
 
@@ -571,7 +606,8 @@
     tokens = rows * steps
     experts = expert_down.shape[0] * devices
     bound = max(2, 2 * tokens * top // experts)
-    if devices == 16 and experts == devices and tokens == BLOCK and bound == tokens:
+    whole = expert_hidden.shape[3] % LANES == 0 and 2 * arrays[0].shape[1] % LANES == 0
+    if whole and devices == 16 and experts == devices and tokens == BLOCK == bound:
         return per_device_dense(*arrays)
     return per_device_general(*arrays)
 

time: 52.6 us -> 51.6 us (0.981)
  waiting for transfers between devices: 13.7 us -> 12.1 us
    ppermute x16, waiting for transfers between devices: 13.7 us -> 12.1 us  [swap(): return lax.ppermute(values, 'seq', [(i, i ^ bit) for i in range(devices)])]
  transfers between devices with their start and end apart: 16 -> 16, of which waited for: 8 -> 9; matrix products, arithmetic and copies ran while one was open for 1% -> 1% of each run, Pallas kernels for 20% -> 20%
where the time goes in v5:
time: 51.6 us; the launch traced here: 51.4 us
  starting transfers between devices  24.5 us (47%)
  Pallas kernels  12.7 us (25%)
  waiting for transfers between devices  12.1 us (23%)
  local copies, waits for them, and re-layouts  0.87 us (2%)
  between operations  0.87 us (2%)
    ppermute x16, starting transfers between devices, swap(): return lax.ppermute(values, 'seq', [(i, i ^ bit) for i in range(devices)])  24.5 us
    ppermute x16, waiting for transfers between devices, swap(): return lax.ppermute(values, 'seq', [(i, i ^ bit) for i in range(devices)])  12.1 us
    pallas_call x1, Pallas kernels, attend(): pl.pallas_call(functools.partial(attend_kernel, first, len(arrived)), gri...  4.77 us
    pallas_call x1, Pallas kernels, load_down(): pl.pallas_call(functools.partial(load_kernel, devices, per_owner), in_spe...  3.77 us
    pallas_call x3, Pallas kernels, expert_call(): pl.pallas_call(kernel, in_specs=[vmem] * (1 + len(arrays)), out_specs=[vm...  2.48 us
    pallas_call x1, Pallas kernels, pack_outboxes(): pl.pallas_call(functools.partial(outbox_kernel, devices // 2, rows), out_...  1.71 us
  transfers between devices with their start and end apart: 16, of which 9 were waited for; matrix products, arithmetic and copies ran while one was open for 1% of the time, Pallas kernels for 20%

profile of v5, /device:TPU:0, one launch (start us, length us, event | category | flops | bytes accessed | tf_op | source)
XLA Modules:
  0.0 51.4 jit_solution(10022701717078216936)
XLA Ops:
  0.6 1.7 %pack_outboxes.1 = (bf16[400,128]{1,0:T(8,128)(2,1)S(1)}, bf16[400,128]{1,0:T(8,128)(2,1)S(1)}, bf16[400,128]{1,0:T(8,128)(2,1)S(1)}, bf16[400,128]{1,0:T(8,128)...) custom-call(s32[4,4,8]{2,1,0:T(4,128)} %routes_ref.1, ...), custom_call_target="tpu_custom_call" | custom-call | flops 104857600 | bytes 1638400 | tf_op jit(solution)/shard_map/pack_outboxes/pallas_call | solution.py:297
  2.3 4.1 %collective-permute-start = (bf16[400,128]{1,0:T(8,128)(2,1)S(1)}, bf16[400,128]{1,0:T(8,128)(2,1)S(1)}, u32[]{:S(2)}, u32[]{:S(2)}) collective-permute-start(bf16[400,128]{1,0:T(8,128)(2,1)S(1)} %get-tuple-element.24), channel_id=1, source_target_pairs={{0,8},{1,9},{2,10},{3,11},{4,12},{5,13},{6,14},{7,15},{8,0},{9,1},... | collective-permute-start | bytes 307208 | tf_op jit(solution)/shard_map/ppermute | solution.py:521
  6.4 1.6 %collective-permute-start.1 = (bf16[400,128]{1,0:T(8,128)(2,1)S(1)}, bf16[400,128]{1,0:T(8,128)(2,1)S(1)}, u32[]{:S(2)}, u32[]{:S(2)}) collective-permute-start(bf16[400,128]{1,0:T(8,128)(2,1)S(1)} %get-tuple-element.28), channel_id=1, source_target_pairs={{0,4},{1,5},{2,6},{3,7},{4,0},{5,1},{6,2},{7,3},{8,12},{9,13},{10,... | collective-permute-start | bytes 307208 | tf_op jit(solution)/shard_map/ppermute | solution.py:521
  8.0 0.0 collective-permute-start.2
  8.0 1.7 %collective-permute-start.3 = (bf16[400,128]{1,0:T(8,128)(2,1)S(1)}, bf16[400,128]{1,0:T(8,128)(2,1)S(1)}, u32[]{:S(2)}, u32[]{:S(2)}) collective-permute-start(bf16[400,128]{1,0:T(8,128)(2,1)S(1)} %get-tuple-element.30), channel_id=1, source_target_pairs={{0,2},{1,3},{2,0},{3,1},{4,6},{5,7},{6,4},{7,5},{8,10},{9,11},{10,... | collective-permute-start | bytes 307208 | tf_op jit(solution)/shard_map/ppermute | solution.py:521
  9.8 1.6 %collective-permute-start.5 = (bf16[400,128]{1,0:T(8,128)(2,1)S(1)}, bf16[400,128]{1,0:T(8,128)(2,1)S(1)}, u32[]{:S(2)}, u32[]{:S(2)}) collective-permute-start(bf16[400,128]{1,0:T(8,128)(2,1)S(1)} %get-tuple-element.31), channel_id=1, source_target_pairs={{0,10},{1,11},{2,8},{3,9},{4,14},{5,15},{6,12},{7,13},{8,2},{9,3},... | collective-permute-start | bytes 307208 | tf_op jit(solution)/shard_map/ppermute | solution.py:521
  11.4 1.5 %collective-permute-done.refs_1_ = bf16[400,128]{1,0:T(8,128)(2,1)S(1)} collective-permute-done((bf16[400,128]{1,0:T(8,128)(2,1)S(1)}, bf16[400,128]{1,0:T(8,128)(2,1)S(1)}, u32[]{:S(2)}, u32[]{:S(2)}) %collective-permute-start) | collective-permute-done | bytes 102432 | tf_op jit(solution)/shard_map/ppermute | solution.py:521
  12.9 2.0 %collective-permute-start.6 = (bf16[400,128]{1,0:T(8,128)(2,1)S(1)}, bf16[400,128]{1,0:T(8,128)(2,1)S(1)}, u32[]{:S(2)}, u32[]{:S(2)}) collective-permute-start(bf16[400,128]{1,0:T(8,128)(2,1)S(1)} %get-tuple-element.32), channel_id=1, source_target_pairs={{0,6},{1,7},{2,4},{3,5},{4,2},{5,3},{6,0},{7,1},{8,14},{9,15},{10,... | collective-permute-start | bytes 307208 | tf_op jit(solution)/shard_map/ppermute | solution.py:521
  14.9 0.0 collective-permute-done.1.refs_2_
  14.9 4.8 %collective-permute-start.7 = (bf16[400,128]{1,0:T(8,128)(2,1)S(1)}, bf16[400,128]{1,0:T(8,128)(2,1)S(1)}, u32[]{:S(2)}, u32[]{:S(2)}) collective-permute-start(bf16[400,128]{1,0:T(8,128)(2,1)S(1)} %get-tuple-element.33), channel_id=1, source_target_pairs={{0,14},{1,15},{2,12},{3,13},{4,10},{5,11},{6,8},{7,9},{8,6},{9,7},... | collective-permute-start | bytes 307208 | tf_op jit(solution)/shard_map/ppermute | solution.py:521
  19.7 0.0 collective-permute-done.2.refs_3_
  19.7 0.0 collective-permute-done.3.refs_4_
  19.8 0.1 collective-permute-start.4
  19.8 3.8 %load_down.1 = (s32[1,256]{1,0:T(1,128)S(1)}, bf16[1,1024,3584]{2,1,0:T(8,128)(2,1)S(1)}) custom-call(s32[1,64]{1,0:T(1,128)} %bitcast.8, s32[1,64]{1,0:T(1,128)} %bitcast.10, bf16[1,1024,3584]{2,1,0:T(8,128)(2,1)} %down_ref.1), custom_call_target="tpu_custom_call" | custom-call | bytes 7340032 | tf_op jit(solution)/shard_map/load_down/pallas_call | solution.py:339
  23.6 0.8 %collective-permute-done.5.refs_5_ = bf16[400,128]{1,0:T(8,128)(2,1)S(1)} collective-permute-done((bf16[400,128]{1,0:T(8,128)(2,1)S(1)}, bf16[400,128]{1,0:T(8,128)(2,1)S(1)}, u32[]{:S(2)}, u32[]{:S(2)}) %collective-permute-start.5) | collective-permute-done | bytes 102432 | tf_op jit(solution)/shard_map/ppermute | solution.py:521
  24.4 0.0 collective-permute-done.6.refs_6_
  24.4 0.0 collective-permute-done.7.refs_7_
  24.5 0.1 collective-permute-start.8
  24.6 1.1 %expert_kept.1 = (f32[128,1792]{1,0:T(8,128)S(1)}, f32[128,1792]{1,0:T(8,128)S(1)}) custom-call(bf16[1,1024,3584]{2,1,0:T(8,128)(2,1)S(1)} %get-tuple-element.37.down_ref, bf16[400,128]{1,0:T(8,128)(2,1)S(1)} %get-tuple-element.27.refs_0_, bf16[400,128]{1,0:T(8,128)(2,1)S(1)} %collective-permute-done.refs_1_, ...), custom_call_target="tpu_custom_call" | custom-call | flops 939524096 | bytes 7340032 | tf_op jit(solution)/shard_map/expert_kept/pallas_call | solution.py:501
  25.7 0.2 collective-permute-done.8.late_ref.refs_9_
  25.9 0.0 collective-permute-done.4.early_ref.refs_8_
  25.9 0.7 %expert_sent.2 = bf16[128,1792]{1,0:T(8,128)(2,1)S(1)} custom-call(bf16[1,1024,3584]{2,1,0:T(8,128)(2,1)S(1)} %get-tuple-element.37.down_ref, bf16[1040,128]{1,0:T(8,128)(2,1)S(1)} %collective-permute-done.4.early_ref.refs_8_, bf16[624,128]{1,0:T(8,128)(2,1)S(1)} %collective-permute-done.8.late_ref.refs_9_), custom_call_target="tpu_custom_call" | custom-call | flops 469762048 | bytes 3670016 | tf_op jit(solution)/shard_map/expert_sent/pallas_call | solution.py:501
  26.6 0.0 copy-start
  26.6 0.0 copy-start.1
  26.6 0.3 collective-permute-start.9
  27.0 0.7 %expert_sent.3 = bf16[128,1792]{1,0:T(8,128)(2,1)S(1)} custom-call(bf16[1,1024,3584]{2,1,0:T(8,128)(2,1)S(1)} %get-tuple-element.37.down_ref, bf16[1040,128]{1,0:T(8,128)(2,1)S(1)} %collective-permute-done.4.early_ref.refs_8_, bf16[624,128]{1,0:T(8,128)(2,1)S(1)} %collective-permute-done.8.late_ref.refs_9_), custom_call_target="tpu_custom_call" | custom-call | flops 469762048 | bytes 3670016 | tf_op jit(solution)/shard_map/expert_sent/pallas_call | solution.py:501
  27.7 0.3 collective-permute-start.10
  28.0 0.6 %collective-permute-done.9 = bf16[128,1792]{1,0:T(8,128)(2,1)S(1)} collective-permute-done((bf16[128,1792]{1,0:T(8,128)(2,1)S(1)}, bf16[128,1792]{1,0:T(8,128)(2,1)S(1)}, u32[]{:S(2)}, u32[]{:S(2)}) %collective-permute-start.9) | collective-permute-done | bytes 458784 | tf_op jit(solution)/shard_map/ppermute | solution.py:521
  28.5 0.1 convert_add_fusion.1
  28.6 0.4 collective-permute-start.11
  29.1 0.5 collective-permute-done.10
  29.5 0.1 convert_add_fusion
  29.7 1.9 %collective-permute-start.13 = (bf16[64,1792]{1,0:T(8,128)(2,1)S(1)}, bf16[64,1792]{1,0:T(8,128)(2,1)S(1)}, u32[]{:S(2)}, u32[]{:S(2)}) collective-permute-start(bf16[64,1792]{1,0:T(8,128)(2,1)S(1)} %slice.117), channel_id=1, source_target_pairs={{0,4},{1,5},{2,6},{3,7},{4,0},{5,1},{6,2},{7,3},{8,12},{9,13},{10,... | collective-permute-start | bytes 688136 | tf_op jit(solution)/shard_map/ppermute | solution.py:521
  31.6 0.0 copy-done
  31.6 0.0 copy-done.1
  31.6 4.8 %attend.1 = bf16[4,4,64,512]{3,2,1,0:T(8,128)(2,1)} custom-call(bf16[4,4,64,576]{3,2,1,0:T(8,128)(2,1)S(1)} %copy-done, bf16[4,4,576]{2,1,0:T(4,128)(2,1)S(1)} %copy-done.1, s32[1,256]{1,0:T(1,128)S(1)} %get-tuple-element.44.tags_ref, bf16[400,128]{1,0:T(8,128)(2,1)S(1)} %get-tuple-element.27.refs_0_, bf16[400,128]{1,0:T(8,128)(2,1)S(1)} %collective-permute-done.refs_1_, ...), custom_call_target="tpu_custom_call" | custom-call | flops 570425344 | bytes 2228224 | tf_op jit(solution)/shard_map/attend/pallas_call | solution.py:442
  36.3 0.2 collective-permute-done.11
  36.6 1.9 %collective-permute-start.12 = (bf16[32,1792]{1,0:T(8,128)(2,1)S(1)}, bf16[32,1792]{1,0:T(8,128)(2,1)S(1)}, u32[]{:S(2)}, u32[]{:S(2)}) collective-permute-start(bf16[32,1792]{1,0:T(8,128)(2,1)S(1)} %slice.120), channel_id=1, source_target_pairs={{0,4},{1,5},{2,6},{3,7},{4,0},{5,1},{6,2},{7,3},{8,12},{9,13},{10,... | collective-permute-start | bytes 344072 | tf_op jit(solution)/shard_map/ppermute | solution.py:521
  38.4 0.0 collective-permute-done.13
  38.5 0.7 %collective-permute-start.14 = (bf16[32,1792]{1,0:T(8,128)(2,1)S(1)}, bf16[32,1792]{1,0:T(8,128)(2,1)S(1)}, u32[]{:S(2)}, u32[]{:S(2)}) collective-permute-start(bf16[32,1792]{1,0:T(8,128)(2,1)S(1)} %slice.119), channel_id=1, source_target_pairs={{0,2},{1,3},{2,0},{3,1},{4,6},{5,7},{6,4},{7,5},{8,10},{9,11},{10,... | collective-permute-start | bytes 344072 | tf_op jit(solution)/shard_map/ppermute | solution.py:521
  39.3 2.2 %collective-permute-done.12 = bf16[32,1792]{1,0:T(8,128)(2,1)S(1)} collective-permute-done((bf16[32,1792]{1,0:T(8,128)(2,1)S(1)}, bf16[32,1792]{1,0:T(8,128)(2,1)S(1)}, u32[]{:S(2)}, u32[]{:S(2)}) %collective-permute-start.12) | collective-permute-done | bytes 114720 | tf_op jit(solution)/shard_map/ppermute | solution.py:521
  41.5 1.9 %collective-permute-done.14 = bf16[32,1792]{1,0:T(8,128)(2,1)S(1)} collective-permute-done((bf16[32,1792]{1,0:T(8,128)(2,1)S(1)}, bf16[32,1792]{1,0:T(8,128)(2,1)S(1)}, u32[]{:S(2)}, u32[]{:S(2)}) %collective-permute-start.14) | collective-permute-done | bytes 114720 | tf_op jit(solution)/shard_map/ppermute | solution.py:521
  43.4 2.9 %collective-permute-start.15 = (bf16[16,3584]{1,0:T(8,128)(2,1)S(1)}, bf16[16,3584]{1,0:T(8,128)(2,1)S(1)}, u32[]{:S(2)}, u32[]{:S(2)}) collective-permute-start(bf16[16,3584]{1,0:T(8,128)(2,1)S(1)} %pad_maximum_fusion.1), channel_id=1, source_target_pairs={{0,8},{1,9},{2,10},{3,11},{4,12},{5,13},{6,14},{7,15},{8,0},{9,1},... | collective-permute-start | bytes 344072 | tf_op jit(solution)/shard_map/ppermute | solution.py:521
  46.4 4.3 %collective-permute-done.15 = bf16[16,3584]{1,0:T(8,128)(2,1)S(1)} collective-permute-done((bf16[16,3584]{1,0:T(8,128)(2,1)S(1)}, bf16[16,3584]{1,0:T(8,128)(2,1)S(1)}, u32[]{:S(2)}, u32[]{:S(2)}) %collective-permute-start.15) | collective-permute-done | bytes 114720 | tf_op jit(solution)/shard_map/ppermute | solution.py:521
  50.7 0.7 %reshape.24 = bf16[4,4,3584]{2,1,0:T(4,128)(2,1)} reshape(bf16[16,3584]{1,0:T(8,128)(2,1)S(1)} %fusion) | data formatting | bytes 229376 | tf_op jit(solution)/shard_map/reshape | solution.py:599
  (23 shorter events, 0.4 us)
Async XLA Ops:
  2.3 10.6 %collective-permute-start = (bf16[400,128]{1,0:T(8,128)(2,1)S(1)}, bf16[400,128]{1,0:T(8,128)(2,1)S(1)}, u32[]{:S(2)}, u32[]{:S(2)}) collective-permute-start(bf16[400,128]{1,0:T(8,128)(2,1)S(1)} %get-tuple-element.24), channel_id=1, source_target_pairs={{0,8},{1,9},{2,10},{3,11},{4,12},{5,13},{6,14},{7,15},{8,0},{9,1},... | collective-permute-start | bytes 307208 | tf_op jit(solution)/shard_map/ppermute | solution.py:521
  6.4 8.5 %collective-permute-start.1 = (bf16[400,128]{1,0:T(8,128)(2,1)S(1)}, bf16[400,128]{1,0:T(8,128)(2,1)S(1)}, u32[]{:S(2)}, u32[]{:S(2)}) collective-permute-start(bf16[400,128]{1,0:T(8,128)(2,1)S(1)} %get-tuple-element.28), channel_id=1, source_target_pairs={{0,4},{1,5},{2,6},{3,7},{4,0},{5,1},{6,2},{7,3},{8,12},{9,13},{10,... | collective-permute-start | bytes 307208 | tf_op jit(solution)/shard_map/ppermute | solution.py:521
  8.0 11.7 %collective-permute-start.2 = (bf16[400,128]{1,0:T(8,128)(2,1)S(1)}, bf16[400,128]{1,0:T(8,128)(2,1)S(1)}, u32[]{:S(2)}, u32[]{:S(2)}) collective-permute-start(bf16[400,128]{1,0:T(8,128)(2,1)S(1)} %get-tuple-element.29), channel_id=1, source_target_pairs={{0,12},{1,13},{2,14},{3,15},{4,8},{5,9},{6,10},{7,11},{8,4},{9,5},... | collective-permute-start | bytes 307208 | tf_op jit(solution)/shard_map/ppermute | solution.py:521
  8.0 11.7 %collective-permute-start.3 = (bf16[400,128]{1,0:T(8,128)(2,1)S(1)}, bf16[400,128]{1,0:T(8,128)(2,1)S(1)}, u32[]{:S(2)}, u32[]{:S(2)}) collective-permute-start(bf16[400,128]{1,0:T(8,128)(2,1)S(1)} %get-tuple-element.30), channel_id=1, source_target_pairs={{0,2},{1,3},{2,0},{3,1},{4,6},{5,7},{6,4},{7,5},{8,10},{9,11},{10,... | collective-permute-start | bytes 307208 | tf_op jit(solution)/shard_map/ppermute | solution.py:521
  9.8 14.6 %collective-permute-start.5 = (bf16[400,128]{1,0:T(8,128)(2,1)S(1)}, bf16[400,128]{1,0:T(8,128)(2,1)S(1)}, u32[]{:S(2)}, u32[]{:S(2)}) collective-permute-start(bf16[400,128]{1,0:T(8,128)(2,1)S(1)} %get-tuple-element.31), channel_id=1, source_target_pairs={{0,10},{1,11},{2,8},{3,9},{4,14},{5,15},{6,12},{7,13},{8,2},{9,3},... | collective-permute-start | bytes 307208 | tf_op jit(solution)/shard_map/ppermute | solution.py:521
  12.9 11.5 %collective-permute-start.6 = (bf16[400,128]{1,0:T(8,128)(2,1)S(1)}, bf16[400,128]{1,0:T(8,128)(2,1)S(1)}, u32[]{:S(2)}, u32[]{:S(2)}) collective-permute-start(bf16[400,128]{1,0:T(8,128)(2,1)S(1)} %get-tuple-element.32), channel_id=1, source_target_pairs={{0,6},{1,7},{2,4},{3,5},{4,2},{5,3},{6,0},{7,1},{8,14},{9,15},{10,... | collective-permute-start | bytes 307208 | tf_op jit(solution)/shard_map/ppermute | solution.py:521
  14.9 9.5 %collective-permute-start.7 = (bf16[400,128]{1,0:T(8,128)(2,1)S(1)}, bf16[400,128]{1,0:T(8,128)(2,1)S(1)}, u32[]{:S(2)}, u32[]{:S(2)}) collective-permute-start(bf16[400,128]{1,0:T(8,128)(2,1)S(1)} %get-tuple-element.33), channel_id=1, source_target_pairs={{0,14},{1,15},{2,12},{3,13},{4,10},{5,11},{6,8},{7,9},{8,6},{9,7},... | collective-permute-start | bytes 307208 | tf_op jit(solution)/shard_map/ppermute | solution.py:521
  19.8 6.2 %collective-permute-start.4 = (bf16[1040,128]{1,0:T(8,128)(2,1)S(1)}, bf16[1040,128]{1,0:T(8,128)(2,1)S(1)}, u32[]{:S(2)}, u32[]{:S(2)}) collective-permute-start(bf16[1040,128]{1,0:T(8,128)(2,1)S(1)} %slice_dynamic-update-slice_fusion), channel_id=1, source_target_pairs={{0,1},{1,0},{2,3},{3,2},{4,5},{5,4},{6,7},{7,6},{8,9},{9,8},{10,11... | collective-permute-start | bytes 798728 | tf_op jit(solution)/shard_map/ppermute | solution.py:521
  24.5 1.5 %collective-permute-start.8 = (bf16[624,128]{1,0:T(8,128)(2,1)S(1)}, bf16[624,128]{1,0:T(8,128)(2,1)S(1)}, u32[]{:S(2)}, u32[]{:S(2)}) collective-permute-start(bf16[624,128]{1,0:T(8,128)(2,1)S(1)} %pad_maximum_fusion), channel_id=1, source_target_pairs={{0,1},{1,0},{2,3},{3,2},{4,5},{5,4},{6,7},{7,6},{8,9},{9,8},{10,11... | collective-permute-start | bytes 479240 | tf_op jit(solution)/shard_map/ppermute | solution.py:521
  26.6 4.9 %copy-start = (bf16[4,4,64,576]{3,2,1,0:T(8,128)(2,1)S(1)}, bf16[4,4,64,576]{3,2,1,0:T(8,128)(2,1)}, u32[]{:S(2)}) copy-start(bf16[4,4,64,576]{3,2,1,0:T(8,128)(2,1)} %queries_ref.1) | copy-start | bytes 3538948
  26.6 4.9 %copy-start.1 = (bf16[4,4,576]{2,1,0:T(4,128)(2,1)S(1)}, bf16[4,4,576]{2,1,0:T(4,128)(2,1)}, u32[]{:S(2)}) copy-start(bf16[4,4,576]{2,1,0:T(4,128)(2,1)} %fresh_ref.1) | copy-start | bytes 55300
  26.6 1.9 %collective-permute-start.9 = (bf16[128,1792]{1,0:T(8,128)(2,1)S(1)}, bf16[128,1792]{1,0:T(8,128)(2,1)S(1)}, u32[]{:S(2)}, u32[]{:S(2)}) collective-permute-start(bf16[128,1792]{1,0:T(8,128)(2,1)S(1)} %expert_sent.2), channel_id=1, source_target_pairs={{0,1},{1,0},{2,3},{3,2},{4,5},{5,4},{6,7},{7,6},{8,9},{9,8},{10,11... | collective-permute-start | bytes 1376264 | tf_op jit(solution)/shard_map/ppermute | solution.py:521
  27.7 1.9 %collective-permute-start.10 = (bf16[128,1792]{1,0:T(8,128)(2,1)S(1)}, bf16[128,1792]{1,0:T(8,128)(2,1)S(1)}, u32[]{:S(2)}, u32[]{:S(2)}) collective-permute-start(bf16[128,1792]{1,0:T(8,128)(2,1)S(1)} %expert_sent.3), channel_id=1, source_target_pairs={{0,1},{1,0},{2,3},{3,2},{4,5},{5,4},{6,7},{7,6},{8,9},{9,8},{10,11... | collective-permute-start | bytes 1376264 | tf_op jit(solution)/shard_map/ppermute | solution.py:521
  28.6 7.9 %collective-permute-start.11 = (bf16[64,1792]{1,0:T(8,128)(2,1)S(1)}, bf16[64,1792]{1,0:T(8,128)(2,1)S(1)}, u32[]{:S(2)}, u32[]{:S(2)}) collective-permute-start(bf16[64,1792]{1,0:T(8,128)(2,1)S(1)} %slice.118), channel_id=1, source_target_pairs={{0,2},{1,3},{2,0},{3,1},{4,6},{5,7},{6,4},{7,5},{8,10},{9,11},{10,... | collective-permute-start | bytes 688136 | tf_op jit(solution)/shard_map/ppermute | solution.py:521
  29.7 8.8 %collective-permute-start.13 = (bf16[64,1792]{1,0:T(8,128)(2,1)S(1)}, bf16[64,1792]{1,0:T(8,128)(2,1)S(1)}, u32[]{:S(2)}, u32[]{:S(2)}) collective-permute-start(bf16[64,1792]{1,0:T(8,128)(2,1)S(1)} %slice.117), channel_id=1, source_target_pairs={{0,4},{1,5},{2,6},{3,7},{4,0},{5,1},{6,2},{7,3},{8,12},{9,13},{10,... | collective-permute-start | bytes 688136 | tf_op jit(solution)/shard_map/ppermute | solution.py:521
  36.6 4.9 %collective-permute-start.12 = (bf16[32,1792]{1,0:T(8,128)(2,1)S(1)}, bf16[32,1792]{1,0:T(8,128)(2,1)S(1)}, u32[]{:S(2)}, u32[]{:S(2)}) collective-permute-start(bf16[32,1792]{1,0:T(8,128)(2,1)S(1)} %slice.120), channel_id=1, source_target_pairs={{0,4},{1,5},{2,6},{3,7},{4,0},{5,1},{6,2},{7,3},{8,12},{9,13},{10,... | collective-permute-start | bytes 344072 | tf_op jit(solution)/shard_map/ppermute | solution.py:521
  38.5 4.9 %collective-permute-start.14 = (bf16[32,1792]{1,0:T(8,128)(2,1)S(1)}, bf16[32,1792]{1,0:T(8,128)(2,1)S(1)}, u32[]{:S(2)}, u32[]{:S(2)}) collective-permute-start(bf16[32,1792]{1,0:T(8,128)(2,1)S(1)} %slice.119), channel_id=1, source_target_pairs={{0,2},{1,3},{2,0},{3,1},{4,6},{5,7},{6,4},{7,5},{8,10},{9,11},{10,... | collective-permute-start | bytes 344072 | tf_op jit(solution)/shard_map/ppermute | solution.py:521
  43.4 7.3 %collective-permute-start.15 = (bf16[16,3584]{1,0:T(8,128)(2,1)S(1)}, bf16[16,3584]{1,0:T(8,128)(2,1)S(1)}, u32[]{:S(2)}, u32[]{:S(2)}) collective-permute-start(bf16[16,3584]{1,0:T(8,128)(2,1)S(1)} %pad_maximum_fusion.1), channel_id=1, source_target_pairs={{0,8},{1,9},{2,10},{3,11},{4,12},{5,13},{6,14},{7,15},{8,0},{9,1},... | collective-permute-start | bytes 344072 | tf_op jit(solution)/shard_map/ppermute | solution.py:521

commit v6 on v5

--- a/solution.py
+++ b/solution.py
@@ -153,8 +153,9 @@
 
 BLOCK = 16
 LANES = 128
-CHIP_ORDER = (0, 4, 2, 6, 1, 5, 3, 7)
+CHIP_ORDER = (0, 6, 1, 4, 2, 5, 3, 7)
 EARLY = 5
+SOONER = (6, 4)
 SCOPED_BYTES = 16 * 2**20
 
 
@@ -166,12 +167,12 @@
     return jnp.sum(jnp.where(eye, row, 0), axis=1, keepdims=True)
 
 
-def flat_row(table, tokens, top):
+def flat_row(table, tokens, top, precision):
     lanes = tokens * top
     place = lax.broadcasted_iota(jnp.int32, (top, lanes), 1) % top
     spread = (place == lax.broadcasted_iota(jnp.int32, (top, lanes), 0)).astype(jnp.float32)
     wide = jnp.dot(
-        table, spread, precision=lax.Precision.HIGHEST, preferred_element_type=jnp.float32
+        table, spread, precision=precision, preferred_element_type=jnp.float32
     )
     owner = lax.broadcasted_iota(jnp.int32, (tokens, lanes), 1) // top
     mine = owner == lax.broadcasted_iota(jnp.int32, (tokens, lanes), 0)
@@ -200,8 +201,16 @@
     return apart
 
 
+def distance_of(block, chips):
+    distance = block * 0
+    for i, chip in enumerate(chips):
+        distance = jnp.where(block // 2 == i, 2 * chip + block % 2, distance)
+    return distance
+
+
 def outbox_kernel(
-    chips,
+    chosen_chips,
+    devices,
     per_owner,
     routes_ref,
     weights_ref,
@@ -212,21 +221,19 @@
     *out_refs,
 ):
     me = lax.axis_index("seq")
-    devices = 2 * chips
     room = BLOCK
-    slots = room * devices
+    slots = 2 * room * len(chosen_chips)
     rows, steps, top = routes_ref.shape
     tokens = rows * steps
     lanes = tokens * top
     hidden_width = hidden_ref.shape[1]
     routes = jnp.concatenate([routes_ref[i] for i in range(rows)], axis=0).astype(jnp.float32)
     weights = jnp.concatenate([weights_ref[i] for i in range(rows)], axis=0)
-    route_row = flat_row(routes, tokens, top).astype(jnp.int32)
-    weight_row = flat_row(weights, tokens, top)
+    route_row = flat_row(routes, tokens, top, lax.Precision.DEFAULT).astype(jnp.int32)
+    weight_row = flat_row(weights, tokens, top, lax.Precision.HIGHEST)
     slot = lax.broadcasted_iota(jnp.int32, (slots, lanes), 0)
     lane = lax.broadcasted_iota(jnp.int32, (slots, lanes), 1)
-    block = slot // room
-    target = me ^ block
+    target = me ^ distance_of(slot // room, chosen_chips)
     pick = (lane // top == slot % room) & (route_row == target)
     scale = jnp.sum(jnp.where(pick, weight_row, 0.0), axis=1, keepdims=True)
     chosen = jnp.where(pick, 1.0, 0.0).astype(jnp.bfloat16)
@@ -252,8 +259,7 @@
     offset = jnp.sum(jnp.where(same, as_column(count), 0), axis=0, keepdims=True)
     slot = lax.broadcasted_iota(jnp.int32, (slots, requests), 0)
     decode = lax.broadcasted_iota(jnp.int32, (slots, requests), 1)
-    block = slot // room
-    target = me ^ block
+    target = me ^ distance_of(slot // room, chosen_chips)
     rank = slot % room - offset
     held = (target == decode // per_owner) & (rank >= 0) & (rank < count)
     source = jnp.sum(jnp.where(held, low + rank + 1, 0), axis=1, keepdims=True) - 1
@@ -279,12 +285,12 @@
 
 
 def pack_outboxes(
-    routes, route_weights, expert_hidden, lengths, assignment, prefill_kv, devices
+    routes, route_weights, expert_hidden, lengths, assignment, prefill_kv, devices, chips
 ):
     rows, steps, top, hidden_width = expert_hidden.shape
     here, kv_width = prefill_kv.shape
     tokens = rows * steps
-    slots = tokens * devices
+    slots = 2 * tokens * len(chips)
     tiles = (hidden_width + kv_width) // LANES
     operands = (
         routes,
@@ -295,9 +301,9 @@
         prefill_kv.T,
     )
     return pl.pallas_call(
-        functools.partial(outbox_kernel, devices // 2, rows),
+        functools.partial(outbox_kernel, chips, devices, rows),
         out_shape=(jax.ShapeDtypeStruct(((2 * tiles + 1) * tokens, LANES), jnp.bfloat16),)
-        * (devices // 2),
+        * len(chips),
         compiler_params=pltpu.CompilerParams(vmem_limit_bytes=SCOPED_BYTES),
         cost_estimate=pl.CostEstimate(
             flops=2 * slots * (tokens * top * hidden_width + here * kv_width),
@@ -527,6 +533,34 @@
     return total[:half], total[half:].astype(jnp.bfloat16)
 
 
+def last_kernel(*refs):
+    kept_refs, received_ref, out_ref = refs[:-2], refs[-2], refs[-1]
+    rows, steps, _ = out_ref.shape
+    first = 0
+    for kept_ref in kept_refs:
+        width = kept_ref.shape[1]
+        columns = slice(first, first + width)
+        total = kept_ref[...] + received_ref[:, columns].astype(jnp.float32)
+        out_ref[:, :, columns] = total.reshape(rows, steps, width).astype(jnp.bfloat16)
+        first += width
+
+
+def last_sum(kept, received, rows, steps):
+    width = received.shape[1]
+    vmem = pl.BlockSpec(memory_space=pltpu.VMEM)
+    return pl.pallas_call(
+        last_kernel,
+        in_specs=[vmem] * (len(kept) + 1),
+        out_specs=vmem,
+        out_shape=jax.ShapeDtypeStruct((rows, steps, width), jnp.bfloat16),
+        compiler_params=pltpu.CompilerParams(vmem_limit_bytes=SCOPED_BYTES),
+        cost_estimate=pl.CostEstimate(
+            flops=rows * steps * width, bytes_accessed=8 * rows * steps * width, transcendentals=0
+        ),
+        name="last_sum",
+    )(*kept, received)
+
+
 def per_device_dense(
     prefill_kv,
     lengths,
@@ -542,9 +576,12 @@
     steps, per_owner = queries.shape[:2]
     rows, _, top, hidden_width = expert_hidden.shape
     model_width = expert_down.shape[2]
-    outboxes = pack_outboxes(
-        routes, route_weights, expert_hidden, lengths, assignment, prefill_kv, devices
-    )
+    outboxes = {}
+    for group in (SOONER, tuple(chip for chip in sorted(CHIP_ORDER) if chip not in SOONER)):
+        packed = pack_outboxes(
+            routes, route_weights, expert_hidden, lengths, assignment, prefill_kv, devices, group
+        )
+        outboxes.update(zip(group, packed))
     chips = devices // 2
     tiles = (hidden_width + prefill_kv.shape[1]) // LANES
     arrived = [
@@ -592,11 +629,10 @@
     flows = [fold(kept, got) for (kept, _), got in zip(flows, received)]
     received = [swap(sent, 2 * bits[1], devices) for (_, sent), bits in zip(flows, orders)]
     flows = [fold(kept, got) for (kept, _), got in zip(flows, received)]
-    kept = jnp.concatenate([kept for kept, _ in flows], axis=1)
     sent = jnp.concatenate([sent for _, sent in flows], axis=1)
     received = swap(sent, 2 * orders[0][-1], devices)
-    moe_out = (kept + received.astype(jnp.float32)).astype(jnp.bfloat16)
-    return context, moe_out.reshape(rows, steps, model_width)
+    moe_out = last_sum([kept for kept, _ in flows], received, rows, steps)
+    return context, moe_out
 
 
 def per_device(*arrays):

time: 51.6 us -> 51.4 us (level)
  Pallas kernels: 12.7 us -> 15 us
  starting transfers between devices: 24.5 us -> 22.9 us
  local copies, waits for them, and re-layouts: 0.87 us -> 0.19 us
    pallas_call x1 -> x3, Pallas kernels: 1.71 us -> 3.96 us  [the longest x2 3.26 us: pack_outboxes(): pl.pallas_call(functools.partial(outbox_kernel, chips, devices, rows), ou...]
    ppermute x16, starting transfers between devices: 24.5 us -> 22.9 us  [swap(): return lax.ppermute(values, 'seq', [(i, i ^ bit) for i in range(devices)])]
    reshape x1 -> x0, local copies, waits for them, and re-layouts: 0.68 us -> none  [per_device_dense(): return (context, moe_out.reshape(rows, steps, model_width))]
  transfers between devices with their start and end apart: 16 -> 16, of which waited for: 9 -> 8; matrix products, arithmetic and copies ran while one was open for 1% -> 1% of each run, Pallas kernels for 20% -> 24%
where the time goes in v6:
time: 51.4 us; the launch traced here: 51.1 us
  starting transfers between devices  22.9 us (45%)
  Pallas kernels  15 us (29%)
  waiting for transfers between devices  11.9 us (23%)
  between operations  0.86 us (2%)
    ppermute x16, starting transfers between devices, swap(): return lax.ppermute(values, 'seq', [(i, i ^ bit) for i in range(devices)])  22.9 us
    ppermute x16, waiting for transfers between devices, swap(): return lax.ppermute(values, 'seq', [(i, i ^ bit) for i in range(devices)])  11.9 us
    pallas_call x1, Pallas kernels, attend(): pl.pallas_call(functools.partial(attend_kernel, first, len(arrived)), gri...  4.77 us
    pallas_call x1, Pallas kernels, load_down(): pl.pallas_call(functools.partial(load_kernel, devices, per_owner), in_spe...  3.77 us
    pallas_call x2, Pallas kernels, pack_outboxes(): pl.pallas_call(functools.partial(outbox_kernel, chips, devices, rows), ou...  3.26 us
    pallas_call x3, Pallas kernels, expert_call(): pl.pallas_call(kernel, in_specs=[vmem] * (1 + len(arrays)), out_specs=[vm...  2.47 us
  transfers between devices with their start and end apart: 16, of which 8 were waited for; matrix products, arithmetic and copies ran while one was open for 1% of the time, Pallas kernels for 24%

profile of v6, /device:TPU:0, one launch (start us, length us, event | category | flops | bytes accessed | tf_op | source)
XLA Modules:
  0.0 51.1 jit_solution(6615387827211476336)
XLA Ops:
  0.6 1.6 %pack_outboxes.2 = (bf16[400,128]{1,0:T(8,128)(2,1)S(1)}, bf16[400,128]{1,0:T(8,128)(2,1)S(1)}) custom-call(s32[4,4,8]{2,1,0:T(4,128)} %routes_ref.3, f32[4,4,8]{2,1,0:T(4,128)} %weights_ref.3, bf16[128,1024]{1,0:T(8,128)(2,1)} %bitcast.5, s32[1,64]{1,0:T(1,128)} %bitcast.9, s32[1,64]{1,0:T(1,128)} %bitcast.12, bf16[576,128]{1,0:T(8,128)(2,1)} %bitcast.7), custom_call_target="tpu_custom_call" | custom-call | flops 26214400 | bytes 409600 | tf_op jit(solution)/shard_map/pack_outboxes/pallas_call | solution.py:303
  2.2 5.1 %collective-permute-start = (bf16[400,128]{1,0:T(8,128)(2,1)S(1)}, bf16[400,128]{1,0:T(8,128)(2,1)S(1)}, u32[]{:S(2)}, u32[]{:S(2)}) collective-permute-start(bf16[400,128]{1,0:T(8,128)(2,1)S(1)} %get-tuple-element.24), channel_id=1, source_target_pairs={{0,12},{1,13},{2,14},{3,15},{4,8},{5,9},{6,10},{7,11},{8,4},{9,5},... | collective-permute-start | bytes 307208 | tf_op jit(solution)/shard_map/ppermute | solution.py:527
  7.3 0.0 collective-permute-start.2
  7.3 1.7 %pack_outboxes.3 = (bf16[400,128]{1,0:T(8,128)(2,1)S(1)}, bf16[400,128]{1,0:T(8,128)(2,1)S(1)}, bf16[400,128]{1,0:T(8,128)(2,1)S(1)}, bf16[400,128]{1,0:T(8,128)...) custom-call(s32[4,4,8]{2,1,0:T(4,128)} %routes_ref.3, f32[4,4,8]{2,1,0:T(4,128)} %weights_ref.3, ...), custom_call_target="tpu_custom_call" | custom-call | flops 78643200 | bytes 1228800 | tf_op jit(solution)/shard_map/pack_outboxes/pallas_call | solution.py:303
  9.0 1.6 %collective-permute-start.1 = (bf16[400,128]{1,0:T(8,128)(2,1)S(1)}, bf16[400,128]{1,0:T(8,128)(2,1)S(1)}, u32[]{:S(2)}, u32[]{:S(2)}) collective-permute-start(bf16[400,128]{1,0:T(8,128)(2,1)S(1)} %get-tuple-element.28), channel_id=1, source_target_pairs={{0,2},{1,3},{2,0},{3,1},{4,6},{5,7},{6,4},{7,5},{8,10},{9,11},{10,... | collective-permute-start | bytes 307208 | tf_op jit(solution)/shard_map/ppermute | solution.py:527
  10.5 0.8 %collective-permute-start.3 = (bf16[400,128]{1,0:T(8,128)(2,1)S(1)}, bf16[400,128]{1,0:T(8,128)(2,1)S(1)}, u32[]{:S(2)}, u32[]{:S(2)}) collective-permute-start(bf16[400,128]{1,0:T(8,128)(2,1)S(1)} %get-tuple-element.30), channel_id=1, source_target_pairs={{0,4},{1,5},{2,6},{3,7},{4,0},{5,1},{6,2},{7,3},{8,12},{9,13},{10,... | collective-permute-start | bytes 307208 | tf_op jit(solution)/shard_map/ppermute | solution.py:527
  11.3 2.1 %collective-permute-start.5 = (bf16[400,128]{1,0:T(8,128)(2,1)S(1)}, bf16[400,128]{1,0:T(8,128)(2,1)S(1)}, u32[]{:S(2)}, u32[]{:S(2)}) collective-permute-start(bf16[400,128]{1,0:T(8,128)(2,1)S(1)} %get-tuple-element.31), channel_id=1, source_target_pairs={{0,10},{1,11},{2,8},{3,9},{4,14},{5,15},{6,12},{7,13},{8,2},{9,3},... | collective-permute-start | bytes 307208 | tf_op jit(solution)/shard_map/ppermute | solution.py:527
  13.4 0.0 collective-permute-done.refs_1_
  13.4 3.1 %collective-permute-start.6 = (bf16[400,128]{1,0:T(8,128)(2,1)S(1)}, bf16[400,128]{1,0:T(8,128)(2,1)S(1)}, u32[]{:S(2)}, u32[]{:S(2)}) collective-permute-start(bf16[400,128]{1,0:T(8,128)(2,1)S(1)} %get-tuple-element.32), channel_id=1, source_target_pairs={{0,6},{1,7},{2,4},{3,5},{4,2},{5,3},{6,0},{7,1},{8,14},{9,15},{10,... | collective-permute-start | bytes 307208 | tf_op jit(solution)/shard_map/ppermute | solution.py:527
  16.5 0.0 collective-permute-done.1.refs_2_
  16.5 2.6 %collective-permute-start.7 = (bf16[400,128]{1,0:T(8,128)(2,1)S(1)}, bf16[400,128]{1,0:T(8,128)(2,1)S(1)}, u32[]{:S(2)}, u32[]{:S(2)}) collective-permute-start(bf16[400,128]{1,0:T(8,128)(2,1)S(1)} %get-tuple-element.33), channel_id=1, source_target_pairs={{0,14},{1,15},{2,12},{3,13},{4,10},{5,11},{6,8},{7,9},{8,6},{9,7},... | collective-permute-start | bytes 307208 | tf_op jit(solution)/shard_map/ppermute | solution.py:527
  19.1 0.0 collective-permute-done.2.refs_3_
  19.1 0.1 collective-permute-done.3.refs_4_
  19.2 0.1 collective-permute-start.4
  19.3 3.8 %load_down.1 = (s32[1,256]{1,0:T(1,128)S(1)}, bf16[1,1024,3584]{2,1,0:T(8,128)(2,1)S(1)}) custom-call(s32[1,64]{1,0:T(1,128)} %bitcast.11, s32[1,64]{1,0:T(1,128)} %bitcast.14, bf16[1,1024,3584]{2,1,0:T(8,128)(2,1)} %down_ref.1), custom_call_target="tpu_custom_call" | custom-call | bytes 7340032 | tf_op jit(solution)/shard_map/load_down/pallas_call | solution.py:345
  23.1 1.4 %collective-permute-done.5.refs_5_ = bf16[400,128]{1,0:T(8,128)(2,1)S(1)} collective-permute-done((bf16[400,128]{1,0:T(8,128)(2,1)S(1)}, bf16[400,128]{1,0:T(8,128)(2,1)S(1)}, u32[]{:S(2)}, u32[]{:S(2)}) %collective-permute-start.5) | collective-permute-done | bytes 102432 | tf_op jit(solution)/shard_map/ppermute | solution.py:527
  24.5 0.0 collective-permute-done.6.refs_6_
  24.5 0.0 collective-permute-done.7.refs_7_
  24.5 0.1 collective-permute-start.8
  24.6 1.1 %expert_kept.1 = (f32[128,1792]{1,0:T(8,128)S(1)}, f32[128,1792]{1,0:T(8,128)S(1)}) custom-call(bf16[1,1024,3584]{2,1,0:T(8,128)(2,1)S(1)} %get-tuple-element.37.down_ref, bf16[400,128]{1,0:T(8,128)(2,1)S(1)} %get-tuple-element.27.refs_0_, bf16[400,128]{1,0:T(8,128)(2,1)S(1)} %collective-permute-done.refs_1_, ...), custom_call_target="tpu_custom_call" | custom-call | flops 939524096 | bytes 7340032 | tf_op jit(solution)/shard_map/expert_kept/pallas_call | solution.py:507
  25.8 0.2 collective-permute-done.8.late_ref.refs_9_
  26.0 0.0 collective-permute-done.4.early_ref.refs_8_
  26.0 0.7 %expert_sent.2 = bf16[128,1792]{1,0:T(8,128)(2,1)S(1)} custom-call(bf16[1,1024,3584]{2,1,0:T(8,128)(2,1)S(1)} %get-tuple-element.37.down_ref, bf16[1040,128]{1,0:T(8,128)(2,1)S(1)} %collective-permute-done.4.early_ref.refs_8_, bf16[624,128]{1,0:T(8,128)(2,1)S(1)} %collective-permute-done.8.late_ref.refs_9_), custom_call_target="tpu_custom_call" | custom-call | flops 469762048 | bytes 3670016 | tf_op jit(solution)/shard_map/expert_sent/pallas_call | solution.py:507
  26.7 0.0 copy-start
  26.7 0.0 copy-start.1
  26.7 0.3 collective-permute-start.9
  27.1 0.7 %expert_sent.3 = bf16[128,1792]{1,0:T(8,128)(2,1)S(1)} custom-call(bf16[1,1024,3584]{2,1,0:T(8,128)(2,1)S(1)} %get-tuple-element.37.down_ref, bf16[1040,128]{1,0:T(8,128)(2,1)S(1)} %collective-permute-done.4.early_ref.refs_8_, bf16[624,128]{1,0:T(8,128)(2,1)S(1)} %collective-permute-done.8.late_ref.refs_9_), custom_call_target="tpu_custom_call" | custom-call | flops 469762048 | bytes 3670016 | tf_op jit(solution)/shard_map/expert_sent/pallas_call | solution.py:507
  27.7 0.3 collective-permute-start.10
  28.0 0.6 %collective-permute-done.9 = bf16[128,1792]{1,0:T(8,128)(2,1)S(1)} collective-permute-done((bf16[128,1792]{1,0:T(8,128)(2,1)S(1)}, bf16[128,1792]{1,0:T(8,128)(2,1)S(1)}, u32[]{:S(2)}, u32[]{:S(2)}) %collective-permute-start.9) | collective-permute-done | bytes 458784 | tf_op jit(solution)/shard_map/ppermute | solution.py:527
  28.6 0.1 convert_add_fusion.1
  28.7 1.0 %collective-permute-start.11 = (bf16[64,1792]{1,0:T(8,128)(2,1)S(1)}, bf16[64,1792]{1,0:T(8,128)(2,1)S(1)}, u32[]{:S(2)}, u32[]{:S(2)}) collective-permute-start(bf16[64,1792]{1,0:T(8,128)(2,1)S(1)} %slice.118), channel_id=1, source_target_pairs={{0,2},{1,3},{2,0},{3,1},{4,6},{5,7},{6,4},{7,5},{8,10},{9,11},{10,... | collective-permute-start | bytes 688136 | tf_op jit(solution)/shard_map/ppermute | solution.py:527
  29.7 0.0 collective-permute-done.10
  29.7 0.1 convert_add_fusion
  29.8 1.7 %collective-permute-start.13 = (bf16[64,1792]{1,0:T(8,128)(2,1)S(1)}, bf16[64,1792]{1,0:T(8,128)(2,1)S(1)}, u32[]{:S(2)}, u32[]{:S(2)}) collective-permute-start(bf16[64,1792]{1,0:T(8,128)(2,1)S(1)} %slice.117), channel_id=1, source_target_pairs={{0,4},{1,5},{2,6},{3,7},{4,0},{5,1},{6,2},{7,3},{8,12},{9,13},{10,... | collective-permute-start | bytes 688136 | tf_op jit(solution)/shard_map/ppermute | solution.py:527
  31.6 0.0 copy-done
  31.6 0.0 copy-done.1
  31.6 4.8 %attend.1 = bf16[4,4,64,512]{3,2,1,0:T(8,128)(2,1)} custom-call(bf16[4,4,64,576]{3,2,1,0:T(8,128)(2,1)S(1)} %copy-done, bf16[4,4,576]{2,1,0:T(4,128)(2,1)S(1)} %copy-done.1, s32[1,256]{1,0:T(1,128)S(1)} %get-tuple-element.44.tags_ref, bf16[400,128]{1,0:T(8,128)(2,1)S(1)} %get-tuple-element.27.refs_0_, bf16[400,128]{1,0:T(8,128)(2,1)S(1)} %collective-permute-done.refs_1_, ...), custom_call_target="tpu_custom_call" | custom-call | flops 570425344 | bytes 2228224 | tf_op jit(solution)/shard_map/attend/pallas_call | solution.py:448
  36.4 0.2 collective-permute-done.11
  36.6 1.8 %collective-permute-start.12 = (bf16[32,1792]{1,0:T(8,128)(2,1)S(1)}, bf16[32,1792]{1,0:T(8,128)(2,1)S(1)}, u32[]{:S(2)}, u32[]{:S(2)}) collective-permute-start(bf16[32,1792]{1,0:T(8,128)(2,1)S(1)} %slice.120), channel_id=1, source_target_pairs={{0,4},{1,5},{2,6},{3,7},{4,0},{5,1},{6,2},{7,3},{8,12},{9,13},{10,... | collective-permute-start | bytes 344072 | tf_op jit(solution)/shard_map/ppermute | solution.py:527
  38.5 0.0 collective-permute-done.13
  38.5 0.5 %collective-permute-start.14 = (bf16[32,1792]{1,0:T(8,128)(2,1)S(1)}, bf16[32,1792]{1,0:T(8,128)(2,1)S(1)}, u32[]{:S(2)}, u32[]{:S(2)}) collective-permute-start(bf16[32,1792]{1,0:T(8,128)(2,1)S(1)} %slice.119), channel_id=1, source_target_pairs={{0,2},{1,3},{2,0},{3,1},{4,6},{5,7},{6,4},{7,5},{8,10},{9,11},{10,... | collective-permute-start | bytes 344072 | tf_op jit(solution)/shard_map/ppermute | solution.py:527
  39.1 2.4 %collective-permute-done.12 = bf16[32,1792]{1,0:T(8,128)(2,1)S(1)} collective-permute-done((bf16[32,1792]{1,0:T(8,128)(2,1)S(1)}, bf16[32,1792]{1,0:T(8,128)(2,1)S(1)}, u32[]{:S(2)}, u32[]{:S(2)}) %collective-permute-start.12) | collective-permute-done | bytes 114720 | tf_op jit(solution)/shard_map/ppermute | solution.py:527
  41.5 1.9 %collective-permute-done.14 = bf16[32,1792]{1,0:T(8,128)(2,1)S(1)} collective-permute-done((bf16[32,1792]{1,0:T(8,128)(2,1)S(1)}, bf16[32,1792]{1,0:T(8,128)(2,1)S(1)}, u32[]{:S(2)}, u32[]{:S(2)}) %collective-permute-start.14) | collective-permute-done | bytes 114720 | tf_op jit(solution)/shard_map/ppermute | solution.py:527
  43.5 1.8 %collective-permute-start.15 = (bf16[16,3584]{1,0:T(8,128)(2,1)S(1)}, bf16[16,3584]{1,0:T(8,128)(2,1)S(1)}, u32[]{:S(2)}, u32[]{:S(2)}) collective-permute-start(bf16[16,3584]{1,0:T(8,128)(2,1)S(1)} %pad_maximum_fusion.1), channel_id=1, source_target_pairs={{0,8},{1,9},{2,10},{3,11},{4,12},{5,13},{6,14},{7,15},{8,0},{9,1},... | collective-permute-start | bytes 344072 | tf_op jit(solution)/shard_map/ppermute | solution.py:527
  45.3 5.1 %collective-permute-done.15.refs_2_ = bf16[16,3584]{1,0:T(8,128)(2,1)S(1)} collective-permute-done((bf16[16,3584]{1,0:T(8,128)(2,1)S(1)}, bf16[16,3584]{1,0:T(8,128)(2,1)S(1)}, u32[]{:S(2)}, u32[]{:S(2)}) %collective-permute-start.15) | collective-permute-done | bytes 114720 | tf_op jit(solution)/shard_map/ppermute | solution.py:527
  50.4 0.7 %last_sum.1 = bf16[4,4,3584]{2,1,0:T(4,128)(2,1)} custom-call(f32[16,1792]{1,0:T(8,128)S(1)} %slice.95.refs_0_, f32[16,1792]{1,0:T(8,128)S(1)} %slice.99.refs_1_, bf16[16,3584]{1,0:T(8,128)(2,1)S(1)} %collective-permute-done.15.refs_2_), custom_call_target="tpu_custom_call" | custom-call | flops 57344 | bytes 458752 | tf_op jit(solution)/shard_map/last_sum/pallas_call | solution.py:551
  (22 shorter events, 0.3 us)
Async XLA Ops:
  2.2 11.2 %collective-permute-start = (bf16[400,128]{1,0:T(8,128)(2,1)S(1)}, bf16[400,128]{1,0:T(8,128)(2,1)S(1)}, u32[]{:S(2)}, u32[]{:S(2)}) collective-permute-start(bf16[400,128]{1,0:T(8,128)(2,1)S(1)} %get-tuple-element.24), channel_id=1, source_target_pairs={{0,12},{1,13},{2,14},{3,15},{4,8},{5,9},{6,10},{7,11},{8,4},{9,5},... | collective-permute-start | bytes 307208 | tf_op jit(solution)/shard_map/ppermute | solution.py:527
  7.3 11.8 %collective-permute-start.2 = (bf16[400,128]{1,0:T(8,128)(2,1)S(1)}, bf16[400,128]{1,0:T(8,128)(2,1)S(1)}, u32[]{:S(2)}, u32[]{:S(2)}) collective-permute-start(bf16[400,128]{1,0:T(8,128)(2,1)S(1)} %get-tuple-element.29), channel_id=1, source_target_pairs={{0,8},{1,9},{2,10},{3,11},{4,12},{5,13},{6,14},{7,15},{8,0},{9,1},... | collective-permute-start | bytes 307208 | tf_op jit(solution)/shard_map/ppermute | solution.py:527
  9.0 7.5 %collective-permute-start.1 = (bf16[400,128]{1,0:T(8,128)(2,1)S(1)}, bf16[400,128]{1,0:T(8,128)(2,1)S(1)}, u32[]{:S(2)}, u32[]{:S(2)}) collective-permute-start(bf16[400,128]{1,0:T(8,128)(2,1)S(1)} %get-tuple-element.28), channel_id=1, source_target_pairs={{0,2},{1,3},{2,0},{3,1},{4,6},{5,7},{6,4},{7,5},{8,10},{9,11},{10,... | collective-permute-start | bytes 307208 | tf_op jit(solution)/shard_map/ppermute | solution.py:527
  10.5 8.6 %collective-permute-start.3 = (bf16[400,128]{1,0:T(8,128)(2,1)S(1)}, bf16[400,128]{1,0:T(8,128)(2,1)S(1)}, u32[]{:S(2)}, u32[]{:S(2)}) collective-permute-start(bf16[400,128]{1,0:T(8,128)(2,1)S(1)} %get-tuple-element.30), channel_id=1, source_target_pairs={{0,4},{1,5},{2,6},{3,7},{4,0},{5,1},{6,2},{7,3},{8,12},{9,13},{10,... | collective-permute-start | bytes 307208 | tf_op jit(solution)/shard_map/ppermute | solution.py:527
  11.3 13.2 %collective-permute-start.5 = (bf16[400,128]{1,0:T(8,128)(2,1)S(1)}, bf16[400,128]{1,0:T(8,128)(2,1)S(1)}, u32[]{:S(2)}, u32[]{:S(2)}) collective-permute-start(bf16[400,128]{1,0:T(8,128)(2,1)S(1)} %get-tuple-element.31), channel_id=1, source_target_pairs={{0,10},{1,11},{2,8},{3,9},{4,14},{5,15},{6,12},{7,13},{8,2},{9,3},... | collective-permute-start | bytes 307208 | tf_op jit(solution)/shard_map/ppermute | solution.py:527
  13.4 11.1 %collective-permute-start.6 = (bf16[400,128]{1,0:T(8,128)(2,1)S(1)}, bf16[400,128]{1,0:T(8,128)(2,1)S(1)}, u32[]{:S(2)}, u32[]{:S(2)}) collective-permute-start(bf16[400,128]{1,0:T(8,128)(2,1)S(1)} %get-tuple-element.32), channel_id=1, source_target_pairs={{0,6},{1,7},{2,4},{3,5},{4,2},{5,3},{6,0},{7,1},{8,14},{9,15},{10,... | collective-permute-start | bytes 307208 | tf_op jit(solution)/shard_map/ppermute | solution.py:527
  16.5 8.0 %collective-permute-start.7 = (bf16[400,128]{1,0:T(8,128)(2,1)S(1)}, bf16[400,128]{1,0:T(8,128)(2,1)S(1)}, u32[]{:S(2)}, u32[]{:S(2)}) collective-permute-start(bf16[400,128]{1,0:T(8,128)(2,1)S(1)} %get-tuple-element.33), channel_id=1, source_target_pairs={{0,14},{1,15},{2,12},{3,13},{4,10},{5,11},{6,8},{7,9},{8,6},{9,7},... | collective-permute-start | bytes 307208 | tf_op jit(solution)/shard_map/ppermute | solution.py:527
  19.2 6.8 %collective-permute-start.4 = (bf16[1040,128]{1,0:T(8,128)(2,1)S(1)}, bf16[1040,128]{1,0:T(8,128)(2,1)S(1)}, u32[]{:S(2)}, u32[]{:S(2)}) collective-permute-start(bf16[1040,128]{1,0:T(8,128)(2,1)S(1)} %slice_dynamic-update-slice_fusion), channel_id=1, source_target_pairs={{0,1},{1,0},{2,3},{3,2},{4,5},{5,4},{6,7},{7,6},{8,9},{9,8},{10,11... | collective-permute-start | bytes 798728 | tf_op jit(solution)/shard_map/ppermute | solution.py:527
  24.5 1.5 %collective-permute-start.8 = (bf16[624,128]{1,0:T(8,128)(2,1)S(1)}, bf16[624,128]{1,0:T(8,128)(2,1)S(1)}, u32[]{:S(2)}, u32[]{:S(2)}) collective-permute-start(bf16[624,128]{1,0:T(8,128)(2,1)S(1)} %pad_maximum_fusion), channel_id=1, source_target_pairs={{0,1},{1,0},{2,3},{3,2},{4,5},{5,4},{6,7},{7,6},{8,9},{9,8},{10,11... | collective-permute-start | bytes 479240 | tf_op jit(solution)/shard_map/ppermute | solution.py:527
  26.7 4.9 %copy-start = (bf16[4,4,64,576]{3,2,1,0:T(8,128)(2,1)S(1)}, bf16[4,4,64,576]{3,2,1,0:T(8,128)(2,1)}, u32[]{:S(2)}) copy-start(bf16[4,4,64,576]{3,2,1,0:T(8,128)(2,1)} %queries_ref.1) | copy-start | bytes 3538948
  26.7 4.9 %copy-start.1 = (bf16[4,4,576]{2,1,0:T(4,128)(2,1)S(1)}, bf16[4,4,576]{2,1,0:T(4,128)(2,1)}, u32[]{:S(2)}) copy-start(bf16[4,4,576]{2,1,0:T(4,128)(2,1)} %fresh_ref.1) | copy-start | bytes 55300
  26.7 1.9 %collective-permute-start.9 = (bf16[128,1792]{1,0:T(8,128)(2,1)S(1)}, bf16[128,1792]{1,0:T(8,128)(2,1)S(1)}, u32[]{:S(2)}, u32[]{:S(2)}) collective-permute-start(bf16[128,1792]{1,0:T(8,128)(2,1)S(1)} %expert_sent.2), channel_id=1, source_target_pairs={{0,1},{1,0},{2,3},{3,2},{4,5},{5,4},{6,7},{7,6},{8,9},{9,8},{10,11... | collective-permute-start | bytes 1376264 | tf_op jit(solution)/shard_map/ppermute | solution.py:527
  27.7 2.0 %collective-permute-start.10 = (bf16[128,1792]{1,0:T(8,128)(2,1)S(1)}, bf16[128,1792]{1,0:T(8,128)(2,1)S(1)}, u32[]{:S(2)}, u32[]{:S(2)}) collective-permute-start(bf16[128,1792]{1,0:T(8,128)(2,1)S(1)} %expert_sent.3), channel_id=1, source_target_pairs={{0,1},{1,0},{2,3},{3,2},{4,5},{5,4},{6,7},{7,6},{8,9},{9,8},{10,11... | collective-permute-start | bytes 1376264 | tf_op jit(solution)/shard_map/ppermute | solution.py:527
  28.7 7.9 %collective-permute-start.11 = (bf16[64,1792]{1,0:T(8,128)(2,1)S(1)}, bf16[64,1792]{1,0:T(8,128)(2,1)S(1)}, u32[]{:S(2)}, u32[]{:S(2)}) collective-permute-start(bf16[64,1792]{1,0:T(8,128)(2,1)S(1)} %slice.118), channel_id=1, source_target_pairs={{0,2},{1,3},{2,0},{3,1},{4,6},{5,7},{6,4},{7,5},{8,10},{9,11},{10,... | collective-permute-start | bytes 688136 | tf_op jit(solution)/shard_map/ppermute | solution.py:527
  29.8 8.6 %collective-permute-start.13 = (bf16[64,1792]{1,0:T(8,128)(2,1)S(1)}, bf16[64,1792]{1,0:T(8,128)(2,1)S(1)}, u32[]{:S(2)}, u32[]{:S(2)}) collective-permute-start(bf16[64,1792]{1,0:T(8,128)(2,1)S(1)} %slice.117), channel_id=1, source_target_pairs={{0,4},{1,5},{2,6},{3,7},{4,0},{5,1},{6,2},{7,3},{8,12},{9,13},{10,... | collective-permute-start | bytes 688136 | tf_op jit(solution)/shard_map/ppermute | solution.py:527
  36.6 4.9 %collective-permute-start.12 = (bf16[32,1792]{1,0:T(8,128)(2,1)S(1)}, bf16[32,1792]{1,0:T(8,128)(2,1)S(1)}, u32[]{:S(2)}, u32[]{:S(2)}) collective-permute-start(bf16[32,1792]{1,0:T(8,128)(2,1)S(1)} %slice.120), channel_id=1, source_target_pairs={{0,4},{1,5},{2,6},{3,7},{4,0},{5,1},{6,2},{7,3},{8,12},{9,13},{10,... | collective-permute-start | bytes 344072 | tf_op jit(solution)/shard_map/ppermute | solution.py:527
  38.5 4.9 %collective-permute-start.14 = (bf16[32,1792]{1,0:T(8,128)(2,1)S(1)}, bf16[32,1792]{1,0:T(8,128)(2,1)S(1)}, u32[]{:S(2)}, u32[]{:S(2)}) collective-permute-start(bf16[32,1792]{1,0:T(8,128)(2,1)S(1)} %slice.119), channel_id=1, source_target_pairs={{0,2},{1,3},{2,0},{3,1},{4,6},{5,7},{6,4},{7,5},{8,10},{9,11},{10,... | collective-permute-start | bytes 344072 | tf_op jit(solution)/shard_map/ppermute | solution.py:527
  43.5 7.0 %collective-permute-start.15 = (bf16[16,3584]{1,0:T(8,128)(2,1)S(1)}, bf16[16,3584]{1,0:T(8,128)(2,1)S(1)}, u32[]{:S(2)}, u32[]{:S(2)}) collective-permute-start(bf16[16,3584]{1,0:T(8,128)(2,1)S(1)} %pad_maximum_fusion.1), channel_id=1, source_target_pairs={{0,8},{1,9},{2,10},{3,11},{4,12},{5,13},{6,14},{7,15},{8,0},{9,1},... | collective-permute-start | bytes 344072 | tf_op jit(solution)/shard_map/ppermute | solution.py:527

commit v7 on v6

--- a/solution.py
+++ b/solution.py
@@ -598,7 +598,7 @@
         for group in (arrived[:EARLY], late)
     ]
 
-    orders = ((1, 2, 4), (2, 1, 4))
+    orders = ((2, 1, 4), (1, 2, 4))
     width = model_width // len(orders)
     half = devices * BLOCK // 2
     kept = expert_call(

time: 51.4 us -> 51.1 us (level)
  transfers between devices with their start and end apart: 16 -> 16, of which waited for: 8 -> 9; matrix products, arithmetic and copies ran while one was open for 1% -> 1% of each run, Pallas kernels for 24% -> 24%
where the time goes in v7:
time: 51.1 us; the launch traced here: 50.9 us
  starting transfers between devices  22.5 us (44%)
  Pallas kernels  15 us (29%)
  waiting for transfers between devices  12.1 us (24%)
  between operations  0.86 us (2%)
    ppermute x16, starting transfers between devices, swap(): return lax.ppermute(values, 'seq', [(i, i ^ bit) for i in range(devices)])  22.5 us
    ppermute x16, waiting for transfers between devices, swap(): return lax.ppermute(values, 'seq', [(i, i ^ bit) for i in range(devices)])  12.1 us
    pallas_call x1, Pallas kernels, attend(): pl.pallas_call(functools.partial(attend_kernel, first, len(arrived)), gri...  4.77 us
    pallas_call x1, Pallas kernels, load_down(): pl.pallas_call(functools.partial(load_kernel, devices, per_owner), in_spe...  3.77 us
    pallas_call x2, Pallas kernels, pack_outboxes(): pl.pallas_call(functools.partial(outbox_kernel, chips, devices, rows), ou...  3.26 us
    pallas_call x3, Pallas kernels, expert_call(): pl.pallas_call(kernel, in_specs=[vmem] * (1 + len(arrays)), out_specs=[vm...  2.48 us
  transfers between devices with their start and end apart: 16, of which 9 were waited for; matrix products, arithmetic and copies ran while one was open for 1% of the time, Pallas kernels for 24%

profile of v7, /device:TPU:0, one launch (start us, length us, event | category | flops | bytes accessed | tf_op | source)
XLA Modules:
  0.0 50.9 jit_solution(17239799883075351425)
XLA Ops:
  0.6 1.6 %pack_outboxes.2 = (bf16[400,128]{1,0:T(8,128)(2,1)S(1)}, bf16[400,128]{1,0:T(8,128)(2,1)S(1)}) custom-call(s32[4,4,8]{2,1,0:T(4,128)} %routes_ref.3, f32[4,4,8]{2,1,0:T(4,128)} %weights_ref.3, bf16[128,1024]{1,0:T(8,128)(2,1)} %bitcast.5, s32[1,64]{1,0:T(1,128)} %bitcast.9, s32[1,64]{1,0:T(1,128)} %bitcast.12, bf16[576,128]{1,0:T(8,128)(2,1)} %bitcast.7), custom_call_target="tpu_custom_call" | custom-call | flops 26214400 | bytes 409600 | tf_op jit(solution)/shard_map/pack_outboxes/pallas_call | solution.py:303
  2.2 5.1 %collective-permute-start = (bf16[400,128]{1,0:T(8,128)(2,1)S(1)}, bf16[400,128]{1,0:T(8,128)(2,1)S(1)}, u32[]{:S(2)}, u32[]{:S(2)}) collective-permute-start(bf16[400,128]{1,0:T(8,128)(2,1)S(1)} %get-tuple-element.24), channel_id=1, source_target_pairs={{0,12},{1,13},{2,14},{3,15},{4,8},{5,9},{6,10},{7,11},{8,4},{9,5},... | collective-permute-start | bytes 307208 | tf_op jit(solution)/shard_map/ppermute | solution.py:527
  7.3 0.0 collective-permute-start.2
  7.3 1.7 %pack_outboxes.3 = (bf16[400,128]{1,0:T(8,128)(2,1)S(1)}, bf16[400,128]{1,0:T(8,128)(2,1)S(1)}, bf16[400,128]{1,0:T(8,128)(2,1)S(1)}, bf16[400,128]{1,0:T(8,128)...) custom-call(s32[4,4,8]{2,1,0:T(4,128)} %routes_ref.3, f32[4,4,8]{2,1,0:T(4,128)} %weights_ref.3, ...), custom_call_target="tpu_custom_call" | custom-call | flops 78643200 | bytes 1228800 | tf_op jit(solution)/shard_map/pack_outboxes/pallas_call | solution.py:303
  9.0 1.6 %collective-permute-start.1 = (bf16[400,128]{1,0:T(8,128)(2,1)S(1)}, bf16[400,128]{1,0:T(8,128)(2,1)S(1)}, u32[]{:S(2)}, u32[]{:S(2)}) collective-permute-start(bf16[400,128]{1,0:T(8,128)(2,1)S(1)} %get-tuple-element.28), channel_id=1, source_target_pairs={{0,2},{1,3},{2,0},{3,1},{4,6},{5,7},{6,4},{7,5},{8,10},{9,11},{10,... | collective-permute-start | bytes 307208 | tf_op jit(solution)/shard_map/ppermute | solution.py:527
  10.5 0.8 %collective-permute-start.3 = (bf16[400,128]{1,0:T(8,128)(2,1)S(1)}, bf16[400,128]{1,0:T(8,128)(2,1)S(1)}, u32[]{:S(2)}, u32[]{:S(2)}) collective-permute-start(bf16[400,128]{1,0:T(8,128)(2,1)S(1)} %get-tuple-element.30), channel_id=1, source_target_pairs={{0,4},{1,5},{2,6},{3,7},{4,0},{5,1},{6,2},{7,3},{8,12},{9,13},{10,... | collective-permute-start | bytes 307208 | tf_op jit(solution)/shard_map/ppermute | solution.py:527
  11.3 2.1 %collective-permute-start.5 = (bf16[400,128]{1,0:T(8,128)(2,1)S(1)}, bf16[400,128]{1,0:T(8,128)(2,1)S(1)}, u32[]{:S(2)}, u32[]{:S(2)}) collective-permute-start(bf16[400,128]{1,0:T(8,128)(2,1)S(1)} %get-tuple-element.31), channel_id=1, source_target_pairs={{0,10},{1,11},{2,8},{3,9},{4,14},{5,15},{6,12},{7,13},{8,2},{9,3},... | collective-permute-start | bytes 307208 | tf_op jit(solution)/shard_map/ppermute | solution.py:527
  13.4 0.0 collective-permute-done.refs_1_
  13.4 3.1 %collective-permute-start.6 = (bf16[400,128]{1,0:T(8,128)(2,1)S(1)}, bf16[400,128]{1,0:T(8,128)(2,1)S(1)}, u32[]{:S(2)}, u32[]{:S(2)}) collective-permute-start(bf16[400,128]{1,0:T(8,128)(2,1)S(1)} %get-tuple-element.32), channel_id=1, source_target_pairs={{0,6},{1,7},{2,4},{3,5},{4,2},{5,3},{6,0},{7,1},{8,14},{9,15},{10,... | collective-permute-start | bytes 307208 | tf_op jit(solution)/shard_map/ppermute | solution.py:527
  16.5 0.0 collective-permute-done.1.refs_2_
  16.5 2.6 %collective-permute-start.7 = (bf16[400,128]{1,0:T(8,128)(2,1)S(1)}, bf16[400,128]{1,0:T(8,128)(2,1)S(1)}, u32[]{:S(2)}, u32[]{:S(2)}) collective-permute-start(bf16[400,128]{1,0:T(8,128)(2,1)S(1)} %get-tuple-element.33), channel_id=1, source_target_pairs={{0,14},{1,15},{2,12},{3,13},{4,10},{5,11},{6,8},{7,9},{8,6},{9,7},... | collective-permute-start | bytes 307208 | tf_op jit(solution)/shard_map/ppermute | solution.py:527
  19.1 0.0 collective-permute-done.2.refs_3_
  19.1 0.1 collective-permute-done.3.refs_4_
  19.2 0.1 collective-permute-start.4
  19.3 3.8 %load_down.1 = (s32[1,256]{1,0:T(1,128)S(1)}, bf16[1,1024,3584]{2,1,0:T(8,128)(2,1)S(1)}) custom-call(s32[1,64]{1,0:T(1,128)} %bitcast.11, s32[1,64]{1,0:T(1,128)} %bitcast.14, bf16[1,1024,3584]{2,1,0:T(8,128)(2,1)} %down_ref.1), custom_call_target="tpu_custom_call" | custom-call | bytes 7340032 | tf_op jit(solution)/shard_map/load_down/pallas_call | solution.py:345
  23.1 1.4 %collective-permute-done.5.refs_5_ = bf16[400,128]{1,0:T(8,128)(2,1)S(1)} collective-permute-done((bf16[400,128]{1,0:T(8,128)(2,1)S(1)}, bf16[400,128]{1,0:T(8,128)(2,1)S(1)}, u32[]{:S(2)}, u32[]{:S(2)}) %collective-permute-start.5) | collective-permute-done | bytes 102432 | tf_op jit(solution)/shard_map/ppermute | solution.py:527
  24.5 0.0 collective-permute-done.6.refs_6_
  24.5 0.0 collective-permute-done.7.refs_7_
  24.5 0.1 collective-permute-start.8
  24.6 1.1 %expert_kept.1 = (f32[128,1792]{1,0:T(8,128)S(1)}, f32[128,1792]{1,0:T(8,128)S(1)}) custom-call(bf16[1,1024,3584]{2,1,0:T(8,128)(2,1)S(1)} %get-tuple-element.37.down_ref, bf16[400,128]{1,0:T(8,128)(2,1)S(1)} %get-tuple-element.27.refs_0_, bf16[400,128]{1,0:T(8,128)(2,1)S(1)} %collective-permute-done.refs_1_, ...), custom_call_target="tpu_custom_call" | custom-call | flops 939524096 | bytes 7340032 | tf_op jit(solution)/shard_map/expert_kept/pallas_call | solution.py:507
  25.8 0.2 collective-permute-done.8.late_ref.refs_9_
  26.0 0.0 collective-permute-done.4.early_ref.refs_8_
  26.0 0.7 %expert_sent.2 = bf16[128,1792]{1,0:T(8,128)(2,1)S(1)} custom-call(bf16[1,1024,3584]{2,1,0:T(8,128)(2,1)S(1)} %get-tuple-element.37.down_ref, bf16[1040,128]{1,0:T(8,128)(2,1)S(1)} %collective-permute-done.4.early_ref.refs_8_, bf16[624,128]{1,0:T(8,128)(2,1)S(1)} %collective-permute-done.8.late_ref.refs_9_), custom_call_target="tpu_custom_call" | custom-call | flops 469762048 | bytes 3670016 | tf_op jit(solution)/shard_map/expert_sent/pallas_call | solution.py:507
  26.7 0.0 copy-start
  26.7 0.0 copy-start.1
  26.7 0.3 collective-permute-start.9
  27.1 0.7 %expert_sent.3 = bf16[128,1792]{1,0:T(8,128)(2,1)S(1)} custom-call(bf16[1,1024,3584]{2,1,0:T(8,128)(2,1)S(1)} %get-tuple-element.37.down_ref, bf16[1040,128]{1,0:T(8,128)(2,1)S(1)} %collective-permute-done.4.early_ref.refs_8_, bf16[624,128]{1,0:T(8,128)(2,1)S(1)} %collective-permute-done.8.late_ref.refs_9_), custom_call_target="tpu_custom_call" | custom-call | flops 469762048 | bytes 3670016 | tf_op jit(solution)/shard_map/expert_sent/pallas_call | solution.py:507
  27.7 0.3 collective-permute-start.10
  28.0 0.6 %collective-permute-done.9 = bf16[128,1792]{1,0:T(8,128)(2,1)S(1)} collective-permute-done((bf16[128,1792]{1,0:T(8,128)(2,1)S(1)}, bf16[128,1792]{1,0:T(8,128)(2,1)S(1)}, u32[]{:S(2)}, u32[]{:S(2)}) %collective-permute-start.9) | collective-permute-done | bytes 458784 | tf_op jit(solution)/shard_map/ppermute | solution.py:527
  28.6 0.1 convert_add_fusion.1
  28.7 1.8 %collective-permute-start.11 = (bf16[64,1792]{1,0:T(8,128)(2,1)S(1)}, bf16[64,1792]{1,0:T(8,128)(2,1)S(1)}, u32[]{:S(2)}, u32[]{:S(2)}) collective-permute-start(bf16[64,1792]{1,0:T(8,128)(2,1)S(1)} %slice.118), channel_id=1, source_target_pairs={{0,4},{1,5},{2,6},{3,7},{4,0},{5,1},{6,2},{7,3},{8,12},{9,13},{10,... | collective-permute-start | bytes 688136 | tf_op jit(solution)/shard_map/ppermute | solution.py:527
  30.6 0.0 collective-permute-done.10
  30.6 0.1 convert_add_fusion
  30.7 0.5 %collective-permute-start.13 = (bf16[64,1792]{1,0:T(8,128)(2,1)S(1)}, bf16[64,1792]{1,0:T(8,128)(2,1)S(1)}, u32[]{:S(2)}, u32[]{:S(2)}) collective-permute-start(bf16[64,1792]{1,0:T(8,128)(2,1)S(1)} %slice.117), channel_id=1, source_target_pairs={{0,2},{1,3},{2,0},{3,1},{4,6},{5,7},{6,4},{7,5},{8,10},{9,11},{10,... | collective-permute-start | bytes 688136 | tf_op jit(solution)/shard_map/ppermute | solution.py:527
  31.2 0.0 copy-done
  31.2 0.0 copy-done.1
  31.2 4.8 %attend.1 = bf16[4,4,64,512]{3,2,1,0:T(8,128)(2,1)} custom-call(bf16[4,4,64,576]{3,2,1,0:T(8,128)(2,1)S(1)} %copy-done, bf16[4,4,576]{2,1,0:T(4,128)(2,1)S(1)} %copy-done.1, s32[1,256]{1,0:T(1,128)S(1)} %get-tuple-element.44.tags_ref, bf16[400,128]{1,0:T(8,128)(2,1)S(1)} %get-tuple-element.27.refs_0_, bf16[400,128]{1,0:T(8,128)(2,1)S(1)} %collective-permute-done.refs_1_, ...), custom_call_target="tpu_custom_call" | custom-call | flops 570425344 | bytes 2228224 | tf_op jit(solution)/shard_map/attend/pallas_call | solution.py:448
  36.0 0.6 %collective-permute-done.11 = bf16[64,1792]{1,0:T(8,128)(2,1)S(1)} collective-permute-done((bf16[64,1792]{1,0:T(8,128)(2,1)S(1)}, bf16[64,1792]{1,0:T(8,128)(2,1)S(1)}, u32[]{:S(2)}, u32[]{:S(2)}) %collective-permute-start.11) | collective-permute-done | bytes 229408 | tf_op jit(solution)/shard_map/ppermute | solution.py:527
  36.7 1.0 %collective-permute-start.12 = (bf16[32,1792]{1,0:T(8,128)(2,1)S(1)}, bf16[32,1792]{1,0:T(8,128)(2,1)S(1)}, u32[]{:S(2)}, u32[]{:S(2)}) collective-permute-start(bf16[32,1792]{1,0:T(8,128)(2,1)S(1)} %slice.120), channel_id=1, source_target_pairs={{0,2},{1,3},{2,0},{3,1},{4,6},{5,7},{6,4},{7,5},{8,10},{9,11},{10,... | collective-permute-start | bytes 344072 | tf_op jit(solution)/shard_map/ppermute | solution.py:527
  37.7 0.6 %collective-permute-done.13 = bf16[64,1792]{1,0:T(8,128)(2,1)S(1)} collective-permute-done((bf16[64,1792]{1,0:T(8,128)(2,1)S(1)}, bf16[64,1792]{1,0:T(8,128)(2,1)S(1)}, u32[]{:S(2)}, u32[]{:S(2)}) %collective-permute-start.13) | collective-permute-done | bytes 229408 | tf_op jit(solution)/shard_map/ppermute | solution.py:527
  38.3 1.1 %collective-permute-start.14 = (bf16[32,1792]{1,0:T(8,128)(2,1)S(1)}, bf16[32,1792]{1,0:T(8,128)(2,1)S(1)}, u32[]{:S(2)}, u32[]{:S(2)}) collective-permute-start(bf16[32,1792]{1,0:T(8,128)(2,1)S(1)} %slice.119), channel_id=1, source_target_pairs={{0,4},{1,5},{2,6},{3,7},{4,0},{5,1},{6,2},{7,3},{8,12},{9,13},{10,... | collective-permute-start | bytes 344072 | tf_op jit(solution)/shard_map/ppermute | solution.py:527
  39.4 2.1 %collective-permute-done.12 = bf16[32,1792]{1,0:T(8,128)(2,1)S(1)} collective-permute-done((bf16[32,1792]{1,0:T(8,128)(2,1)S(1)}, bf16[32,1792]{1,0:T(8,128)(2,1)S(1)}, u32[]{:S(2)}, u32[]{:S(2)}) %collective-permute-start.12) | collective-permute-done | bytes 114720 | tf_op jit(solution)/shard_map/ppermute | solution.py:527
  41.6 1.6 %collective-permute-done.14 = bf16[32,1792]{1,0:T(8,128)(2,1)S(1)} collective-permute-done((bf16[32,1792]{1,0:T(8,128)(2,1)S(1)}, bf16[32,1792]{1,0:T(8,128)(2,1)S(1)}, u32[]{:S(2)}, u32[]{:S(2)}) %collective-permute-start.14) | collective-permute-done | bytes 114720 | tf_op jit(solution)/shard_map/ppermute | solution.py:527
  43.2 2.1 %collective-permute-start.15 = (bf16[16,3584]{1,0:T(8,128)(2,1)S(1)}, bf16[16,3584]{1,0:T(8,128)(2,1)S(1)}, u32[]{:S(2)}, u32[]{:S(2)}) collective-permute-start(bf16[16,3584]{1,0:T(8,128)(2,1)S(1)} %pad_maximum_fusion.1), channel_id=1, source_target_pairs={{0,8},{1,9},{2,10},{3,11},{4,12},{5,13},{6,14},{7,15},{8,0},{9,1},... | collective-permute-start | bytes 344072 | tf_op jit(solution)/shard_map/ppermute | solution.py:527
  45.3 4.9 %collective-permute-done.15.refs_2_ = bf16[16,3584]{1,0:T(8,128)(2,1)S(1)} collective-permute-done((bf16[16,3584]{1,0:T(8,128)(2,1)S(1)}, bf16[16,3584]{1,0:T(8,128)(2,1)S(1)}, u32[]{:S(2)}, u32[]{:S(2)}) %collective-permute-start.15) | collective-permute-done | bytes 114720 | tf_op jit(solution)/shard_map/ppermute | solution.py:527
  50.2 0.7 %last_sum.1 = bf16[4,4,3584]{2,1,0:T(4,128)(2,1)} custom-call(f32[16,1792]{1,0:T(8,128)S(1)} %slice.95.refs_0_, f32[16,1792]{1,0:T(8,128)S(1)} %slice.99.refs_1_, bf16[16,3584]{1,0:T(8,128)(2,1)S(1)} %collective-permute-done.15.refs_2_), custom_call_target="tpu_custom_call" | custom-call | flops 57344 | bytes 458752 | tf_op jit(solution)/shard_map/last_sum/pallas_call | solution.py:551
  (22 shorter events, 0.3 us)
Async XLA Ops:
  2.2 11.2 %collective-permute-start = (bf16[400,128]{1,0:T(8,128)(2,1)S(1)}, bf16[400,128]{1,0:T(8,128)(2,1)S(1)}, u32[]{:S(2)}, u32[]{:S(2)}) collective-permute-start(bf16[400,128]{1,0:T(8,128)(2,1)S(1)} %get-tuple-element.24), channel_id=1, source_target_pairs={{0,12},{1,13},{2,14},{3,15},{4,8},{5,9},{6,10},{7,11},{8,4},{9,5},... | collective-permute-start | bytes 307208 | tf_op jit(solution)/shard_map/ppermute | solution.py:527
  7.3 11.8 %collective-permute-start.2 = (bf16[400,128]{1,0:T(8,128)(2,1)S(1)}, bf16[400,128]{1,0:T(8,128)(2,1)S(1)}, u32[]{:S(2)}, u32[]{:S(2)}) collective-permute-start(bf16[400,128]{1,0:T(8,128)(2,1)S(1)} %get-tuple-element.29), channel_id=1, source_target_pairs={{0,8},{1,9},{2,10},{3,11},{4,12},{5,13},{6,14},{7,15},{8,0},{9,1},... | collective-permute-start | bytes 307208 | tf_op jit(solution)/shard_map/ppermute | solution.py:527
  9.0 7.5 %collective-permute-start.1 = (bf16[400,128]{1,0:T(8,128)(2,1)S(1)}, bf16[400,128]{1,0:T(8,128)(2,1)S(1)}, u32[]{:S(2)}, u32[]{:S(2)}) collective-permute-start(bf16[400,128]{1,0:T(8,128)(2,1)S(1)} %get-tuple-element.28), channel_id=1, source_target_pairs={{0,2},{1,3},{2,0},{3,1},{4,6},{5,7},{6,4},{7,5},{8,10},{9,11},{10,... | collective-permute-start | bytes 307208 | tf_op jit(solution)/shard_map/ppermute | solution.py:527
  10.5 8.6 %collective-permute-start.3 = (bf16[400,128]{1,0:T(8,128)(2,1)S(1)}, bf16[400,128]{1,0:T(8,128)(2,1)S(1)}, u32[]{:S(2)}, u32[]{:S(2)}) collective-permute-start(bf16[400,128]{1,0:T(8,128)(2,1)S(1)} %get-tuple-element.30), channel_id=1, source_target_pairs={{0,4},{1,5},{2,6},{3,7},{4,0},{5,1},{6,2},{7,3},{8,12},{9,13},{10,... | collective-permute-start | bytes 307208 | tf_op jit(solution)/shard_map/ppermute | solution.py:527
  11.3 13.2 %collective-permute-start.5 = (bf16[400,128]{1,0:T(8,128)(2,1)S(1)}, bf16[400,128]{1,0:T(8,128)(2,1)S(1)}, u32[]{:S(2)}, u32[]{:S(2)}) collective-permute-start(bf16[400,128]{1,0:T(8,128)(2,1)S(1)} %get-tuple-element.31), channel_id=1, source_target_pairs={{0,10},{1,11},{2,8},{3,9},{4,14},{5,15},{6,12},{7,13},{8,2},{9,3},... | collective-permute-start | bytes 307208 | tf_op jit(solution)/shard_map/ppermute | solution.py:527
  13.4 11.1 %collective-permute-start.6 = (bf16[400,128]{1,0:T(8,128)(2,1)S(1)}, bf16[400,128]{1,0:T(8,128)(2,1)S(1)}, u32[]{:S(2)}, u32[]{:S(2)}) collective-permute-start(bf16[400,128]{1,0:T(8,128)(2,1)S(1)} %get-tuple-element.32), channel_id=1, source_target_pairs={{0,6},{1,7},{2,4},{3,5},{4,2},{5,3},{6,0},{7,1},{8,14},{9,15},{10,... | collective-permute-start | bytes 307208 | tf_op jit(solution)/shard_map/ppermute | solution.py:527
  16.5 8.0 %collective-permute-start.7 = (bf16[400,128]{1,0:T(8,128)(2,1)S(1)}, bf16[400,128]{1,0:T(8,128)(2,1)S(1)}, u32[]{:S(2)}, u32[]{:S(2)}) collective-permute-start(bf16[400,128]{1,0:T(8,128)(2,1)S(1)} %get-tuple-element.33), channel_id=1, source_target_pairs={{0,14},{1,15},{2,12},{3,13},{4,10},{5,11},{6,8},{7,9},{8,6},{9,7},... | collective-permute-start | bytes 307208 | tf_op jit(solution)/shard_map/ppermute | solution.py:527
  19.2 6.8 %collective-permute-start.4 = (bf16[1040,128]{1,0:T(8,128)(2,1)S(1)}, bf16[1040,128]{1,0:T(8,128)(2,1)S(1)}, u32[]{:S(2)}, u32[]{:S(2)}) collective-permute-start(bf16[1040,128]{1,0:T(8,128)(2,1)S(1)} %slice_dynamic-update-slice_fusion), channel_id=1, source_target_pairs={{0,1},{1,0},{2,3},{3,2},{4,5},{5,4},{6,7},{7,6},{8,9},{9,8},{10,11... | collective-permute-start | bytes 798728 | tf_op jit(solution)/shard_map/ppermute | solution.py:527
  24.5 1.5 %collective-permute-start.8 = (bf16[624,128]{1,0:T(8,128)(2,1)S(1)}, bf16[624,128]{1,0:T(8,128)(2,1)S(1)}, u32[]{:S(2)}, u32[]{:S(2)}) collective-permute-start(bf16[624,128]{1,0:T(8,128)(2,1)S(1)} %pad_maximum_fusion), channel_id=1, source_target_pairs={{0,1},{1,0},{2,3},{3,2},{4,5},{5,4},{6,7},{7,6},{8,9},{9,8},{10,11... | collective-permute-start | bytes 479240 | tf_op jit(solution)/shard_map/ppermute | solution.py:527
  26.7 4.5 %copy-start = (bf16[4,4,64,576]{3,2,1,0:T(8,128)(2,1)S(1)}, bf16[4,4,64,576]{3,2,1,0:T(8,128)(2,1)}, u32[]{:S(2)}) copy-start(bf16[4,4,64,576]{3,2,1,0:T(8,128)(2,1)} %queries_ref.1) | copy-start | bytes 3538948
  26.7 4.5 %copy-start.1 = (bf16[4,4,576]{2,1,0:T(4,128)(2,1)S(1)}, bf16[4,4,576]{2,1,0:T(4,128)(2,1)}, u32[]{:S(2)}) copy-start(bf16[4,4,576]{2,1,0:T(4,128)(2,1)} %fresh_ref.1) | copy-start | bytes 55300
  26.7 1.9 %collective-permute-start.9 = (bf16[128,1792]{1,0:T(8,128)(2,1)S(1)}, bf16[128,1792]{1,0:T(8,128)(2,1)S(1)}, u32[]{:S(2)}, u32[]{:S(2)}) collective-permute-start(bf16[128,1792]{1,0:T(8,128)(2,1)S(1)} %expert_sent.2), channel_id=1, source_target_pairs={{0,1},{1,0},{2,3},{3,2},{4,5},{5,4},{6,7},{7,6},{8,9},{9,8},{10,11... | collective-permute-start | bytes 1376264 | tf_op jit(solution)/shard_map/ppermute | solution.py:527
  27.7 2.8 %collective-permute-start.10 = (bf16[128,1792]{1,0:T(8,128)(2,1)S(1)}, bf16[128,1792]{1,0:T(8,128)(2,1)S(1)}, u32[]{:S(2)}, u32[]{:S(2)}) collective-permute-start(bf16[128,1792]{1,0:T(8,128)(2,1)S(1)} %expert_sent.3), channel_id=1, source_target_pairs={{0,1},{1,0},{2,3},{3,2},{4,5},{5,4},{6,7},{7,6},{8,9},{9,8},{10,11... | collective-permute-start | bytes 1376264 | tf_op jit(solution)/shard_map/ppermute | solution.py:527
  28.7 7.9 %collective-permute-start.11 = (bf16[64,1792]{1,0:T(8,128)(2,1)S(1)}, bf16[64,1792]{1,0:T(8,128)(2,1)S(1)}, u32[]{:S(2)}, u32[]{:S(2)}) collective-permute-start(bf16[64,1792]{1,0:T(8,128)(2,1)S(1)} %slice.118), channel_id=1, source_target_pairs={{0,4},{1,5},{2,6},{3,7},{4,0},{5,1},{6,2},{7,3},{8,12},{9,13},{10,... | collective-permute-start | bytes 688136 | tf_op jit(solution)/shard_map/ppermute | solution.py:527
  30.7 7.6 %collective-permute-start.13 = (bf16[64,1792]{1,0:T(8,128)(2,1)S(1)}, bf16[64,1792]{1,0:T(8,128)(2,1)S(1)}, u32[]{:S(2)}, u32[]{:S(2)}) collective-permute-start(bf16[64,1792]{1,0:T(8,128)(2,1)S(1)} %slice.117), channel_id=1, source_target_pairs={{0,2},{1,3},{2,0},{3,1},{4,6},{5,7},{6,4},{7,5},{8,10},{9,11},{10,... | collective-permute-start | bytes 688136 | tf_op jit(solution)/shard_map/ppermute | solution.py:527
  36.7 4.9 %collective-permute-start.12 = (bf16[32,1792]{1,0:T(8,128)(2,1)S(1)}, bf16[32,1792]{1,0:T(8,128)(2,1)S(1)}, u32[]{:S(2)}, u32[]{:S(2)}) collective-permute-start(bf16[32,1792]{1,0:T(8,128)(2,1)S(1)} %slice.120), channel_id=1, source_target_pairs={{0,2},{1,3},{2,0},{3,1},{4,6},{5,7},{6,4},{7,5},{8,10},{9,11},{10,... | collective-permute-start | bytes 344072 | tf_op jit(solution)/shard_map/ppermute | solution.py:527
  38.3 4.9 %collective-permute-start.14 = (bf16[32,1792]{1,0:T(8,128)(2,1)S(1)}, bf16[32,1792]{1,0:T(8,128)(2,1)S(1)}, u32[]{:S(2)}, u32[]{:S(2)}) collective-permute-start(bf16[32,1792]{1,0:T(8,128)(2,1)S(1)} %slice.119), channel_id=1, source_target_pairs={{0,4},{1,5},{2,6},{3,7},{4,0},{5,1},{6,2},{7,3},{8,12},{9,13},{10,... | collective-permute-start | bytes 344072 | tf_op jit(solution)/shard_map/ppermute | solution.py:527
  43.2 7.0 %collective-permute-start.15 = (bf16[16,3584]{1,0:T(8,128)(2,1)S(1)}, bf16[16,3584]{1,0:T(8,128)(2,1)S(1)}, u32[]{:S(2)}, u32[]{:S(2)}) collective-permute-start(bf16[16,3584]{1,0:T(8,128)(2,1)S(1)} %pad_maximum_fusion.1), channel_id=1, source_target_pairs={{0,8},{1,9},{2,10},{3,11},{4,12},{5,13},{6,14},{7,15},{8,0},{9,1},... | collective-permute-start | bytes 344072 | tf_op jit(solution)/shard_map/ppermute | solution.py:527

commit v8 on v7

--- a/solution.py
+++ b/solution.py
@@ -625,7 +625,7 @@
     received = [swap(sent, 2 * bits[0], devices) for (_, sent), bits in zip(flows, orders)]
     late_tags, _ = after((tags, [sent for _, sent in flows]))
     context = attend(queries, new_kv, arrived, crossed, hidden_width, late_tags)
-    received[1], _ = after((received[1], context))
+    received[0], _ = after((received[0], context))
     flows = [fold(kept, got) for (kept, _), got in zip(flows, received)]
     received = [swap(sent, 2 * bits[1], devices) for (_, sent), bits in zip(flows, orders)]
     flows = [fold(kept, got) for (kept, _), got in zip(flows, received)]

time: 51.1 us -> 51.1 us (level)
  no operation moved by 1% of the time
where the time goes in v8:
time: 51.1 us; the launch traced here: 50.9 us
  starting transfers between devices  22.5 us (44%)
  Pallas kernels  15 us (29%)
  waiting for transfers between devices  12.1 us (24%)
  between operations  0.86 us (2%)
    ppermute x16, starting transfers between devices, swap(): return lax.ppermute(values, 'seq', [(i, i ^ bit) for i in range(devices)])  22.5 us
    ppermute x16, waiting for transfers between devices, swap(): return lax.ppermute(values, 'seq', [(i, i ^ bit) for i in range(devices)])  12.1 us
    pallas_call x1, Pallas kernels, attend(): pl.pallas_call(functools.partial(attend_kernel, first, len(arrived)), gri...  4.77 us
    pallas_call x1, Pallas kernels, load_down(): pl.pallas_call(functools.partial(load_kernel, devices, per_owner), in_spe...  3.77 us
    pallas_call x2, Pallas kernels, pack_outboxes(): pl.pallas_call(functools.partial(outbox_kernel, chips, devices, rows), ou...  3.26 us
    pallas_call x3, Pallas kernels, expert_call(): pl.pallas_call(kernel, in_specs=[vmem] * (1 + len(arrays)), out_specs=[vm...  2.48 us
  transfers between devices with their start and end apart: 16, of which 9 were waited for; matrix products, arithmetic and copies ran while one was open for 1% of the time, Pallas kernels for 24%

profile of v8, /device:TPU:0, one launch (start us, length us, event | category | flops | bytes accessed | tf_op | source)
XLA Modules:
  0.0 50.9 jit_solution(17239799883075351425)
XLA Ops:
  0.6 1.6 %pack_outboxes.2 = (bf16[400,128]{1,0:T(8,128)(2,1)S(1)}, bf16[400,128]{1,0:T(8,128)(2,1)S(1)}) custom-call(s32[4,4,8]{2,1,0:T(4,128)} %routes_ref.3, f32[4,4,8]{2,1,0:T(4,128)} %weights_ref.3, bf16[128,1024]{1,0:T(8,128)(2,1)} %bitcast.5, s32[1,64]{1,0:T(1,128)} %bitcast.9, s32[1,64]{1,0:T(1,128)} %bitcast.12, bf16[576,128]{1,0:T(8,128)(2,1)} %bitcast.7), custom_call_target="tpu_custom_call" | custom-call | flops 26214400 | bytes 409600 | tf_op jit(solution)/shard_map/pack_outboxes/pallas_call | solution.py:303
  2.2 5.1 %collective-permute-start = (bf16[400,128]{1,0:T(8,128)(2,1)S(1)}, bf16[400,128]{1,0:T(8,128)(2,1)S(1)}, u32[]{:S(2)}, u32[]{:S(2)}) collective-permute-start(bf16[400,128]{1,0:T(8,128)(2,1)S(1)} %get-tuple-element.24), channel_id=1, source_target_pairs={{0,12},{1,13},{2,14},{3,15},{4,8},{5,9},{6,10},{7,11},{8,4},{9,5},... | collective-permute-start | bytes 307208 | tf_op jit(solution)/shard_map/ppermute | solution.py:527
  7.3 0.0 collective-permute-start.2
  7.3 1.7 %pack_outboxes.3 = (bf16[400,128]{1,0:T(8,128)(2,1)S(1)}, bf16[400,128]{1,0:T(8,128)(2,1)S(1)}, bf16[400,128]{1,0:T(8,128)(2,1)S(1)}, bf16[400,128]{1,0:T(8,128)...) custom-call(s32[4,4,8]{2,1,0:T(4,128)} %routes_ref.3, f32[4,4,8]{2,1,0:T(4,128)} %weights_ref.3, ...), custom_call_target="tpu_custom_call" | custom-call | flops 78643200 | bytes 1228800 | tf_op jit(solution)/shard_map/pack_outboxes/pallas_call | solution.py:303
  9.0 1.6 %collective-permute-start.1 = (bf16[400,128]{1,0:T(8,128)(2,1)S(1)}, bf16[400,128]{1,0:T(8,128)(2,1)S(1)}, u32[]{:S(2)}, u32[]{:S(2)}) collective-permute-start(bf16[400,128]{1,0:T(8,128)(2,1)S(1)} %get-tuple-element.28), channel_id=1, source_target_pairs={{0,2},{1,3},{2,0},{3,1},{4,6},{5,7},{6,4},{7,5},{8,10},{9,11},{10,... | collective-permute-start | bytes 307208 | tf_op jit(solution)/shard_map/ppermute | solution.py:527
  10.5 0.8 %collective-permute-start.3 = (bf16[400,128]{1,0:T(8,128)(2,1)S(1)}, bf16[400,128]{1,0:T(8,128)(2,1)S(1)}, u32[]{:S(2)}, u32[]{:S(2)}) collective-permute-start(bf16[400,128]{1,0:T(8,128)(2,1)S(1)} %get-tuple-element.30), channel_id=1, source_target_pairs={{0,4},{1,5},{2,6},{3,7},{4,0},{5,1},{6,2},{7,3},{8,12},{9,13},{10,... | collective-permute-start | bytes 307208 | tf_op jit(solution)/shard_map/ppermute | solution.py:527
  11.3 2.1 %collective-permute-start.5 = (bf16[400,128]{1,0:T(8,128)(2,1)S(1)}, bf16[400,128]{1,0:T(8,128)(2,1)S(1)}, u32[]{:S(2)}, u32[]{:S(2)}) collective-permute-start(bf16[400,128]{1,0:T(8,128)(2,1)S(1)} %get-tuple-element.31), channel_id=1, source_target_pairs={{0,10},{1,11},{2,8},{3,9},{4,14},{5,15},{6,12},{7,13},{8,2},{9,3},... | collective-permute-start | bytes 307208 | tf_op jit(solution)/shard_map/ppermute | solution.py:527
  13.4 0.0 collective-permute-done.refs_1_
  13.4 3.1 %collective-permute-start.6 = (bf16[400,128]{1,0:T(8,128)(2,1)S(1)}, bf16[400,128]{1,0:T(8,128)(2,1)S(1)}, u32[]{:S(2)}, u32[]{:S(2)}) collective-permute-start(bf16[400,128]{1,0:T(8,128)(2,1)S(1)} %get-tuple-element.32), channel_id=1, source_target_pairs={{0,6},{1,7},{2,4},{3,5},{4,2},{5,3},{6,0},{7,1},{8,14},{9,15},{10,... | collective-permute-start | bytes 307208 | tf_op jit(solution)/shard_map/ppermute | solution.py:527
  16.5 0.0 collective-permute-done.1.refs_2_
  16.5 2.6 %collective-permute-start.7 = (bf16[400,128]{1,0:T(8,128)(2,1)S(1)}, bf16[400,128]{1,0:T(8,128)(2,1)S(1)}, u32[]{:S(2)}, u32[]{:S(2)}) collective-permute-start(bf16[400,128]{1,0:T(8,128)(2,1)S(1)} %get-tuple-element.33), channel_id=1, source_target_pairs={{0,14},{1,15},{2,12},{3,13},{4,10},{5,11},{6,8},{7,9},{8,6},{9,7},... | collective-permute-start | bytes 307208 | tf_op jit(solution)/shard_map/ppermute | solution.py:527
  19.1 0.0 collective-permute-done.2.refs_3_
  19.1 0.1 collective-permute-done.3.refs_4_
  19.2 0.1 collective-permute-start.4
  19.3 3.8 %load_down.1 = (s32[1,256]{1,0:T(1,128)S(1)}, bf16[1,1024,3584]{2,1,0:T(8,128)(2,1)S(1)}) custom-call(s32[1,64]{1,0:T(1,128)} %bitcast.11, s32[1,64]{1,0:T(1,128)} %bitcast.14, bf16[1,1024,3584]{2,1,0:T(8,128)(2,1)} %down_ref.1), custom_call_target="tpu_custom_call" | custom-call | bytes 7340032 | tf_op jit(solution)/shard_map/load_down/pallas_call | solution.py:345
  23.1 1.4 %collective-permute-done.5.refs_5_ = bf16[400,128]{1,0:T(8,128)(2,1)S(1)} collective-permute-done((bf16[400,128]{1,0:T(8,128)(2,1)S(1)}, bf16[400,128]{1,0:T(8,128)(2,1)S(1)}, u32[]{:S(2)}, u32[]{:S(2)}) %collective-permute-start.5) | collective-permute-done | bytes 102432 | tf_op jit(solution)/shard_map/ppermute | solution.py:527
  24.5 0.0 collective-permute-done.6.refs_6_
  24.5 0.0 collective-permute-done.7.refs_7_
  24.5 0.1 collective-permute-start.8
  24.6 1.1 %expert_kept.1 = (f32[128,1792]{1,0:T(8,128)S(1)}, f32[128,1792]{1,0:T(8,128)S(1)}) custom-call(bf16[1,1024,3584]{2,1,0:T(8,128)(2,1)S(1)} %get-tuple-element.37.down_ref, bf16[400,128]{1,0:T(8,128)(2,1)S(1)} %get-tuple-element.27.refs_0_, bf16[400,128]{1,0:T(8,128)(2,1)S(1)} %collective-permute-done.refs_1_, ...), custom_call_target="tpu_custom_call" | custom-call | flops 939524096 | bytes 7340032 | tf_op jit(solution)/shard_map/expert_kept/pallas_call | solution.py:507
  25.8 0.2 collective-permute-done.8.late_ref.refs_9_
  26.0 0.0 collective-permute-done.4.early_ref.refs_8_
  26.0 0.7 %expert_sent.2 = bf16[128,1792]{1,0:T(8,128)(2,1)S(1)} custom-call(bf16[1,1024,3584]{2,1,0:T(8,128)(2,1)S(1)} %get-tuple-element.37.down_ref, bf16[1040,128]{1,0:T(8,128)(2,1)S(1)} %collective-permute-done.4.early_ref.refs_8_, bf16[624,128]{1,0:T(8,128)(2,1)S(1)} %collective-permute-done.8.late_ref.refs_9_), custom_call_target="tpu_custom_call" | custom-call | flops 469762048 | bytes 3670016 | tf_op jit(solution)/shard_map/expert_sent/pallas_call | solution.py:507
  26.7 0.0 copy-start
  26.7 0.0 copy-start.1
  26.7 0.3 collective-permute-start.9
  27.1 0.7 %expert_sent.3 = bf16[128,1792]{1,0:T(8,128)(2,1)S(1)} custom-call(bf16[1,1024,3584]{2,1,0:T(8,128)(2,1)S(1)} %get-tuple-element.37.down_ref, bf16[1040,128]{1,0:T(8,128)(2,1)S(1)} %collective-permute-done.4.early_ref.refs_8_, bf16[624,128]{1,0:T(8,128)(2,1)S(1)} %collective-permute-done.8.late_ref.refs_9_), custom_call_target="tpu_custom_call" | custom-call | flops 469762048 | bytes 3670016 | tf_op jit(solution)/shard_map/expert_sent/pallas_call | solution.py:507
  27.7 0.3 collective-permute-start.10
  28.0 0.6 %collective-permute-done.9 = bf16[128,1792]{1,0:T(8,128)(2,1)S(1)} collective-permute-done((bf16[128,1792]{1,0:T(8,128)(2,1)S(1)}, bf16[128,1792]{1,0:T(8,128)(2,1)S(1)}, u32[]{:S(2)}, u32[]{:S(2)}) %collective-permute-start.9) | collective-permute-done | bytes 458784 | tf_op jit(solution)/shard_map/ppermute | solution.py:527
  28.6 0.1 convert_add_fusion.1
  28.7 1.8 %collective-permute-start.11 = (bf16[64,1792]{1,0:T(8,128)(2,1)S(1)}, bf16[64,1792]{1,0:T(8,128)(2,1)S(1)}, u32[]{:S(2)}, u32[]{:S(2)}) collective-permute-start(bf16[64,1792]{1,0:T(8,128)(2,1)S(1)} %slice.118), channel_id=1, source_target_pairs={{0,4},{1,5},{2,6},{3,7},{4,0},{5,1},{6,2},{7,3},{8,12},{9,13},{10,... | collective-permute-start | bytes 688136 | tf_op jit(solution)/shard_map/ppermute | solution.py:527
  30.6 0.0 collective-permute-done.10
  30.6 0.1 convert_add_fusion
  30.7 0.5 %collective-permute-start.13 = (bf16[64,1792]{1,0:T(8,128)(2,1)S(1)}, bf16[64,1792]{1,0:T(8,128)(2,1)S(1)}, u32[]{:S(2)}, u32[]{:S(2)}) collective-permute-start(bf16[64,1792]{1,0:T(8,128)(2,1)S(1)} %slice.117), channel_id=1, source_target_pairs={{0,2},{1,3},{2,0},{3,1},{4,6},{5,7},{6,4},{7,5},{8,10},{9,11},{10,... | collective-permute-start | bytes 688136 | tf_op jit(solution)/shard_map/ppermute | solution.py:527
  31.2 0.0 copy-done
  31.2 0.0 copy-done.1
  31.2 4.8 %attend.1 = bf16[4,4,64,512]{3,2,1,0:T(8,128)(2,1)} custom-call(bf16[4,4,64,576]{3,2,1,0:T(8,128)(2,1)S(1)} %copy-done, bf16[4,4,576]{2,1,0:T(4,128)(2,1)S(1)} %copy-done.1, s32[1,256]{1,0:T(1,128)S(1)} %get-tuple-element.44.tags_ref, bf16[400,128]{1,0:T(8,128)(2,1)S(1)} %get-tuple-element.27.refs_0_, bf16[400,128]{1,0:T(8,128)(2,1)S(1)} %collective-permute-done.refs_1_, ...), custom_call_target="tpu_custom_call" | custom-call | flops 570425344 | bytes 2228224 | tf_op jit(solution)/shard_map/attend/pallas_call | solution.py:448
  36.0 0.6 %collective-permute-done.11 = bf16[64,1792]{1,0:T(8,128)(2,1)S(1)} collective-permute-done((bf16[64,1792]{1,0:T(8,128)(2,1)S(1)}, bf16[64,1792]{1,0:T(8,128)(2,1)S(1)}, u32[]{:S(2)}, u32[]{:S(2)}) %collective-permute-start.11) | collective-permute-done | bytes 229408 | tf_op jit(solution)/shard_map/ppermute | solution.py:527
  36.7 1.0 %collective-permute-start.12 = (bf16[32,1792]{1,0:T(8,128)(2,1)S(1)}, bf16[32,1792]{1,0:T(8,128)(2,1)S(1)}, u32[]{:S(2)}, u32[]{:S(2)}) collective-permute-start(bf16[32,1792]{1,0:T(8,128)(2,1)S(1)} %slice.120), channel_id=1, source_target_pairs={{0,2},{1,3},{2,0},{3,1},{4,6},{5,7},{6,4},{7,5},{8,10},{9,11},{10,... | collective-permute-start | bytes 344072 | tf_op jit(solution)/shard_map/ppermute | solution.py:527
  37.7 0.6 %collective-permute-done.13 = bf16[64,1792]{1,0:T(8,128)(2,1)S(1)} collective-permute-done((bf16[64,1792]{1,0:T(8,128)(2,1)S(1)}, bf16[64,1792]{1,0:T(8,128)(2,1)S(1)}, u32[]{:S(2)}, u32[]{:S(2)}) %collective-permute-start.13) | collective-permute-done | bytes 229408 | tf_op jit(solution)/shard_map/ppermute | solution.py:527
  38.3 1.1 %collective-permute-start.14 = (bf16[32,1792]{1,0:T(8,128)(2,1)S(1)}, bf16[32,1792]{1,0:T(8,128)(2,1)S(1)}, u32[]{:S(2)}, u32[]{:S(2)}) collective-permute-start(bf16[32,1792]{1,0:T(8,128)(2,1)S(1)} %slice.119), channel_id=1, source_target_pairs={{0,4},{1,5},{2,6},{3,7},{4,0},{5,1},{6,2},{7,3},{8,12},{9,13},{10,... | collective-permute-start | bytes 344072 | tf_op jit(solution)/shard_map/ppermute | solution.py:527
  39.4 2.1 %collective-permute-done.12 = bf16[32,1792]{1,0:T(8,128)(2,1)S(1)} collective-permute-done((bf16[32,1792]{1,0:T(8,128)(2,1)S(1)}, bf16[32,1792]{1,0:T(8,128)(2,1)S(1)}, u32[]{:S(2)}, u32[]{:S(2)}) %collective-permute-start.12) | collective-permute-done | bytes 114720 | tf_op jit(solution)/shard_map/ppermute | solution.py:527
  41.6 1.6 %collective-permute-done.14 = bf16[32,1792]{1,0:T(8,128)(2,1)S(1)} collective-permute-done((bf16[32,1792]{1,0:T(8,128)(2,1)S(1)}, bf16[32,1792]{1,0:T(8,128)(2,1)S(1)}, u32[]{:S(2)}, u32[]{:S(2)}) %collective-permute-start.14) | collective-permute-done | bytes 114720 | tf_op jit(solution)/shard_map/ppermute | solution.py:527
  43.2 2.1 %collective-permute-start.15 = (bf16[16,3584]{1,0:T(8,128)(2,1)S(1)}, bf16[16,3584]{1,0:T(8,128)(2,1)S(1)}, u32[]{:S(2)}, u32[]{:S(2)}) collective-permute-start(bf16[16,3584]{1,0:T(8,128)(2,1)S(1)} %pad_maximum_fusion.1), channel_id=1, source_target_pairs={{0,8},{1,9},{2,10},{3,11},{4,12},{5,13},{6,14},{7,15},{8,0},{9,1},... | collective-permute-start | bytes 344072 | tf_op jit(solution)/shard_map/ppermute | solution.py:527
  45.3 4.9 %collective-permute-done.15.refs_2_ = bf16[16,3584]{1,0:T(8,128)(2,1)S(1)} collective-permute-done((bf16[16,3584]{1,0:T(8,128)(2,1)S(1)}, bf16[16,3584]{1,0:T(8,128)(2,1)S(1)}, u32[]{:S(2)}, u32[]{:S(2)}) %collective-permute-start.15) | collective-permute-done | bytes 114720 | tf_op jit(solution)/shard_map/ppermute | solution.py:527
  50.2 0.7 %last_sum.1 = bf16[4,4,3584]{2,1,0:T(4,128)(2,1)} custom-call(f32[16,1792]{1,0:T(8,128)S(1)} %slice.95.refs_0_, f32[16,1792]{1,0:T(8,128)S(1)} %slice.99.refs_1_, bf16[16,3584]{1,0:T(8,128)(2,1)S(1)} %collective-permute-done.15.refs_2_), custom_call_target="tpu_custom_call" | custom-call | flops 57344 | bytes 458752 | tf_op jit(solution)/shard_map/last_sum/pallas_call | solution.py:551
  (22 shorter events, 0.3 us)
Async XLA Ops:
  2.2 11.2 %collective-permute-start = (bf16[400,128]{1,0:T(8,128)(2,1)S(1)}, bf16[400,128]{1,0:T(8,128)(2,1)S(1)}, u32[]{:S(2)}, u32[]{:S(2)}) collective-permute-start(bf16[400,128]{1,0:T(8,128)(2,1)S(1)} %get-tuple-element.24), channel_id=1, source_target_pairs={{0,12},{1,13},{2,14},{3,15},{4,8},{5,9},{6,10},{7,11},{8,4},{9,5},... | collective-permute-start | bytes 307208 | tf_op jit(solution)/shard_map/ppermute | solution.py:527
  7.3 11.8 %collective-permute-start.2 = (bf16[400,128]{1,0:T(8,128)(2,1)S(1)}, bf16[400,128]{1,0:T(8,128)(2,1)S(1)}, u32[]{:S(2)}, u32[]{:S(2)}) collective-permute-start(bf16[400,128]{1,0:T(8,128)(2,1)S(1)} %get-tuple-element.29), channel_id=1, source_target_pairs={{0,8},{1,9},{2,10},{3,11},{4,12},{5,13},{6,14},{7,15},{8,0},{9,1},... | collective-permute-start | bytes 307208 | tf_op jit(solution)/shard_map/ppermute | solution.py:527
  9.0 7.5 %collective-permute-start.1 = (bf16[400,128]{1,0:T(8,128)(2,1)S(1)}, bf16[400,128]{1,0:T(8,128)(2,1)S(1)}, u32[]{:S(2)}, u32[]{:S(2)}) collective-permute-start(bf16[400,128]{1,0:T(8,128)(2,1)S(1)} %get-tuple-element.28), channel_id=1, source_target_pairs={{0,2},{1,3},{2,0},{3,1},{4,6},{5,7},{6,4},{7,5},{8,10},{9,11},{10,... | collective-permute-start | bytes 307208 | tf_op jit(solution)/shard_map/ppermute | solution.py:527
  10.5 8.6 %collective-permute-start.3 = (bf16[400,128]{1,0:T(8,128)(2,1)S(1)}, bf16[400,128]{1,0:T(8,128)(2,1)S(1)}, u32[]{:S(2)}, u32[]{:S(2)}) collective-permute-start(bf16[400,128]{1,0:T(8,128)(2,1)S(1)} %get-tuple-element.30), channel_id=1, source_target_pairs={{0,4},{1,5},{2,6},{3,7},{4,0},{5,1},{6,2},{7,3},{8,12},{9,13},{10,... | collective-permute-start | bytes 307208 | tf_op jit(solution)/shard_map/ppermute | solution.py:527
  11.3 13.2 %collective-permute-start.5 = (bf16[400,128]{1,0:T(8,128)(2,1)S(1)}, bf16[400,128]{1,0:T(8,128)(2,1)S(1)}, u32[]{:S(2)}, u32[]{:S(2)}) collective-permute-start(bf16[400,128]{1,0:T(8,128)(2,1)S(1)} %get-tuple-element.31), channel_id=1, source_target_pairs={{0,10},{1,11},{2,8},{3,9},{4,14},{5,15},{6,12},{7,13},{8,2},{9,3},... | collective-permute-start | bytes 307208 | tf_op jit(solution)/shard_map/ppermute | solution.py:527
  13.4 11.1 %collective-permute-start.6 = (bf16[400,128]{1,0:T(8,128)(2,1)S(1)}, bf16[400,128]{1,0:T(8,128)(2,1)S(1)}, u32[]{:S(2)}, u32[]{:S(2)}) collective-permute-start(bf16[400,128]{1,0:T(8,128)(2,1)S(1)} %get-tuple-element.32), channel_id=1, source_target_pairs={{0,6},{1,7},{2,4},{3,5},{4,2},{5,3},{6,0},{7,1},{8,14},{9,15},{10,... | collective-permute-start | bytes 307208 | tf_op jit(solution)/shard_map/ppermute | solution.py:527
  16.5 8.0 %collective-permute-start.7 = (bf16[400,128]{1,0:T(8,128)(2,1)S(1)}, bf16[400,128]{1,0:T(8,128)(2,1)S(1)}, u32[]{:S(2)}, u32[]{:S(2)}) collective-permute-start(bf16[400,128]{1,0:T(8,128)(2,1)S(1)} %get-tuple-element.33), channel_id=1, source_target_pairs={{0,14},{1,15},{2,12},{3,13},{4,10},{5,11},{6,8},{7,9},{8,6},{9,7},... | collective-permute-start | bytes 307208 | tf_op jit(solution)/shard_map/ppermute | solution.py:527
  19.2 6.8 %collective-permute-start.4 = (bf16[1040,128]{1,0:T(8,128)(2,1)S(1)}, bf16[1040,128]{1,0:T(8,128)(2,1)S(1)}, u32[]{:S(2)}, u32[]{:S(2)}) collective-permute-start(bf16[1040,128]{1,0:T(8,128)(2,1)S(1)} %slice_dynamic-update-slice_fusion), channel_id=1, source_target_pairs={{0,1},{1,0},{2,3},{3,2},{4,5},{5,4},{6,7},{7,6},{8,9},{9,8},{10,11... | collective-permute-start | bytes 798728 | tf_op jit(solution)/shard_map/ppermute | solution.py:527
  24.5 1.5 %collective-permute-start.8 = (bf16[624,128]{1,0:T(8,128)(2,1)S(1)}, bf16[624,128]{1,0:T(8,128)(2,1)S(1)}, u32[]{:S(2)}, u32[]{:S(2)}) collective-permute-start(bf16[624,128]{1,0:T(8,128)(2,1)S(1)} %pad_maximum_fusion), channel_id=1, source_target_pairs={{0,1},{1,0},{2,3},{3,2},{4,5},{5,4},{6,7},{7,6},{8,9},{9,8},{10,11... | collective-permute-start | bytes 479240 | tf_op jit(solution)/shard_map/ppermute | solution.py:527
  26.7 4.5 %copy-start = (bf16[4,4,64,576]{3,2,1,0:T(8,128)(2,1)S(1)}, bf16[4,4,64,576]{3,2,1,0:T(8,128)(2,1)}, u32[]{:S(2)}) copy-start(bf16[4,4,64,576]{3,2,1,0:T(8,128)(2,1)} %queries_ref.1) | copy-start | bytes 3538948
  26.7 4.5 %copy-start.1 = (bf16[4,4,576]{2,1,0:T(4,128)(2,1)S(1)}, bf16[4,4,576]{2,1,0:T(4,128)(2,1)}, u32[]{:S(2)}) copy-start(bf16[4,4,576]{2,1,0:T(4,128)(2,1)} %fresh_ref.1) | copy-start | bytes 55300
  26.7 1.9 %collective-permute-start.9 = (bf16[128,1792]{1,0:T(8,128)(2,1)S(1)}, bf16[128,1792]{1,0:T(8,128)(2,1)S(1)}, u32[]{:S(2)}, u32[]{:S(2)}) collective-permute-start(bf16[128,1792]{1,0:T(8,128)(2,1)S(1)} %expert_sent.2), channel_id=1, source_target_pairs={{0,1},{1,0},{2,3},{3,2},{4,5},{5,4},{6,7},{7,6},{8,9},{9,8},{10,11... | collective-permute-start | bytes 1376264 | tf_op jit(solution)/shard_map/ppermute | solution.py:527
  27.7 2.8 %collective-permute-start.10 = (bf16[128,1792]{1,0:T(8,128)(2,1)S(1)}, bf16[128,1792]{1,0:T(8,128)(2,1)S(1)}, u32[]{:S(2)}, u32[]{:S(2)}) collective-permute-start(bf16[128,1792]{1,0:T(8,128)(2,1)S(1)} %expert_sent.3), channel_id=1, source_target_pairs={{0,1},{1,0},{2,3},{3,2},{4,5},{5,4},{6,7},{7,6},{8,9},{9,8},{10,11... | collective-permute-start | bytes 1376264 | tf_op jit(solution)/shard_map/ppermute | solution.py:527
  28.7 7.9 %collective-permute-start.11 = (bf16[64,1792]{1,0:T(8,128)(2,1)S(1)}, bf16[64,1792]{1,0:T(8,128)(2,1)S(1)}, u32[]{:S(2)}, u32[]{:S(2)}) collective-permute-start(bf16[64,1792]{1,0:T(8,128)(2,1)S(1)} %slice.118), channel_id=1, source_target_pairs={{0,4},{1,5},{2,6},{3,7},{4,0},{5,1},{6,2},{7,3},{8,12},{9,13},{10,... | collective-permute-start | bytes 688136 | tf_op jit(solution)/shard_map/ppermute | solution.py:527
  30.7 7.6 %collective-permute-start.13 = (bf16[64,1792]{1,0:T(8,128)(2,1)S(1)}, bf16[64,1792]{1,0:T(8,128)(2,1)S(1)}, u32[]{:S(2)}, u32[]{:S(2)}) collective-permute-start(bf16[64,1792]{1,0:T(8,128)(2,1)S(1)} %slice.117), channel_id=1, source_target_pairs={{0,2},{1,3},{2,0},{3,1},{4,6},{5,7},{6,4},{7,5},{8,10},{9,11},{10,... | collective-permute-start | bytes 688136 | tf_op jit(solution)/shard_map/ppermute | solution.py:527
  36.7 4.9 %collective-permute-start.12 = (bf16[32,1792]{1,0:T(8,128)(2,1)S(1)}, bf16[32,1792]{1,0:T(8,128)(2,1)S(1)}, u32[]{:S(2)}, u32[]{:S(2)}) collective-permute-start(bf16[32,1792]{1,0:T(8,128)(2,1)S(1)} %slice.120), channel_id=1, source_target_pairs={{0,2},{1,3},{2,0},{3,1},{4,6},{5,7},{6,4},{7,5},{8,10},{9,11},{10,... | collective-permute-start | bytes 344072 | tf_op jit(solution)/shard_map/ppermute | solution.py:527
  38.3 4.9 %collective-permute-start.14 = (bf16[32,1792]{1,0:T(8,128)(2,1)S(1)}, bf16[32,1792]{1,0:T(8,128)(2,1)S(1)}, u32[]{:S(2)}, u32[]{:S(2)}) collective-permute-start(bf16[32,1792]{1,0:T(8,128)(2,1)S(1)} %slice.119), channel_id=1, source_target_pairs={{0,4},{1,5},{2,6},{3,7},{4,0},{5,1},{6,2},{7,3},{8,12},{9,13},{10,... | collective-permute-start | bytes 344072 | tf_op jit(solution)/shard_map/ppermute | solution.py:527
  43.2 7.0 %collective-permute-start.15 = (bf16[16,3584]{1,0:T(8,128)(2,1)S(1)}, bf16[16,3584]{1,0:T(8,128)(2,1)S(1)}, u32[]{:S(2)}, u32[]{:S(2)}) collective-permute-start(bf16[16,3584]{1,0:T(8,128)(2,1)S(1)} %pad_maximum_fusion.1), channel_id=1, source_target_pairs={{0,8},{1,9},{2,10},{3,11},{4,12},{5,13},{6,14},{7,15},{8,0},{9,1},... | collective-permute-start | bytes 344072 | tf_op jit(solution)/shard_map/ppermute | solution.py:527
